TPU v7x, 256 devices: a whole 4x4x8 slice. The times are simulated.
256 devices in a mesh: gx: 16 (over y, x), gy: 16 (over z, core).
Axes of the slice: x: 4, y: 4, z: 8, core: 2. Of those that a mesh axis runs over, the one named last changes fastest.
Arguments:
- field_in: bfloat16 [256, 128, 20, 128], P('gx', 'gy'), may hold values from -6 to 6
- point_weight: bfloat16 [20, 20], replicated, may hold values from -1.25 to 1.25
- point_bias: float32 [20], replicated, may hold values from -3 to 3
- spec_weight: bfloat16 [24, 20, 20, 2, 2304], P(None, None, None, None, ('gx', 'gy')), may hold values from -1 to 1
- out_cotangent: bfloat16 [256, 128, 20, 128], P('gx', 'gy'), may hold values from -6 to 6
Outputs:
- output_field: bfloat16 [256, 128, 20, 128], P('gx', 'gy')
- grad_in: bfloat16 [256, 128, 20, 128], P('gx', 'gy')
- grad_spec: float32 [24, 20, 20, 2, 2304], P(None, None, None, None, ('gx', 'gy'))
- grad_point: float32 [20, 20], replicated
- grad_bias: float32 [20], replicated
All inputs are finite; a program needn't handle non-finite values.
Results may differ from a plain program's by a relative error of at most 0.029.
Values may be sent and summed in bfloat16 or wider, within the bound.
No kernel may reach another device: no remote copies, remote signals or barrier semaphores. Data moves between devices by JAX's collectives and lax.ppermute only.
A program may use at most 64 MiB of HBM per device.

v0:
```python
import math

import jax
import jax.numpy as jnp
import ml_dtypes
import numpy as np
from jax import lax
from jax.experimental import pallas as pl
from jax.experimental.pallas import tpu as pltpu
from jax.sharding import PartitionSpec as P

C = 20
Z = 32
T_SIZE = 4
KX = 24
KY = 24
KZ = 24
KT = 4
NX = 256
NY = 128
ZT = 128
M = 96
N = 16
CX = NX // N
CY = NY // N
ROWS = 12 * C
GROUPS = C // 4
PAIRS = 9
LINE = PAIRS * KY

BF = jnp.bfloat16
F32 = jnp.float32


def centered(count):
    return (np.arange(count) + count // 2) % count - count // 2


def rounded(table):
    return np.asarray(table, np.float32).astype(ml_dtypes.bfloat16)


def line_table(modes, length, scale):
    turns = centered(modes)[:, None] * np.arange(length)[None, :] % length
    angle = turns.astype(np.float32) * np.float32(2.0 * math.pi / length)
    scale = np.float32(scale)
    return rounded(np.cos(angle) * scale), rounded(np.sin(angle) * scale)


def depth_table(scale):
    cells = np.arange(ZT)
    turn_z = centered(KZ)[:, None] * (cells // T_SIZE)[None, :] % Z
    turn_t = centered(KT)[:, None] * (cells % T_SIZE)[None, :] % T_SIZE
    angle = turn_z.astype(np.float32)[:, None, :] * np.float32(2.0 * math.pi / Z)
    angle = angle + turn_t.astype(np.float32)[None, :, :] * np.float32(2.0 * math.pi / T_SIZE)
    angle = angle.reshape(M, ZT)
    return rounded(np.stack([np.cos(angle), -np.sin(angle)]) * np.float32(scale))


def depth_matrix(scale):
    table = depth_table(scale).astype(np.float32).reshape(2, N, 2, 3, ZT)
    eye = np.eye(4, dtype=np.float32)
    full = np.einsum("sghmn,ce->ghcsmen", table, eye)
    return rounded(full.reshape(N * 2 * 4 * 2 * 3, 4 * ZT))


def x_matrix(scale):
    cosine, sine = line_table(KX, NX, scale)
    eye = np.eye(CY, dtype=np.float32)
    return rounded(
        np.concatenate([np.kron(t.astype(np.float32), eye) for t in (cosine, sine)], axis=0)
    )


def y_matrix(scale):
    return np.concatenate(line_table(KY, NY, scale), axis=0)


def lane_maps():
    plain = np.zeros((ROWS, 256), np.float32)
    turned = np.zeros((ROWS, 256), np.float32)
    for row in range(ROWS):
        group, rest = divmod(row, 48)
        half, rest = divmod(rest, 24)
        channel, rest = divmod(rest, 6)
        part, mode = divmod(rest, 3)
        base = half * 128 + (group * 4 + channel) * 6 + mode
        plain[row, base + 3 * part] = 1.0
        turned[row, base + 3 * (1 - part)] = 1.0 if part == 1 else -1.0
    return rounded(plain), rounded(turned)


def lane_picks():
    lanes = np.arange(128)
    inside = lanes < 6 * C
    channel = np.stack([(lanes // 6 == c) & inside for c in range(24)])
    kind = np.stack([(lanes % 6 == k) & inside for k in range(6)] + [inside * 0] * 2)
    return rounded(channel), kind.astype(np.float32)


def channel_spread():
    return rounded(np.kron(np.eye(C, dtype=np.float32), np.ones((1, CY), np.float32)))


DEPTH_IN = depth_matrix(ZT**-0.5)
DEPTH_MID = depth_matrix(M**-0.5)
X_IN = x_matrix(NX**-0.5)
X_MID = x_matrix(KX**-0.5)
Y_IN = y_matrix(NY**-0.5)
Y_MID = y_matrix(KY**-0.5)
PLAIN, TURNED = lane_maps()
CHANNEL, KIND = lane_picks()
SPREAD = channel_spread()


def dot(left, right, left_dim=1, right_dim=0, precision=None):
    return lax.dot_general(
        left,
        right,
        (((left_dim,), (right_dim,)), ((), ())),
        precision=precision,
        preferred_element_type=F32,
    )


def call(kernel, out_shape, flops=10**8, megabytes=4, name=None):
    return pl.pallas_call(
        kernel,
        out_shape=out_shape,
        compiler_params=pltpu.CompilerParams(vmem_limit_bytes=24 * 2**20),
        cost_estimate=pl.CostEstimate(
            flops=flops, bytes_accessed=megabytes * 10**6, transcendentals=0
        ),
        name=name,
    )


def shaped(shape, dtype):
    return jax.ShapeDtypeStruct(shape, dtype)


def to_columns(values):
    wide = values.astype(F32).reshape(CX, 4, CY, ZT)
    return jnp.concatenate([wide[:, k].reshape(CX * CY, ZT) for k in range(4)], axis=1)


def to_cells(columns):
    parts = [columns[:, k * ZT : (k + 1) * ZT].reshape(CX, CY, ZT) for k in range(4)]
    return jnp.stack(parts, axis=1).reshape(CX, 4 * CY, ZT)


def spectrum_kernel(field, depth, out):
    for group in range(GROUPS):
        columns = to_columns(field[:, group * 32 : group * 32 + 32, :]).astype(BF)
        spectrum = dot(depth[...], columns, 1, 1)
        out[:, group * 48 : group * 48 + 48, :] = spectrum.astype(BF).reshape(N, 48, 128)


def split_dot(left, right):
    high = left.astype(BF)
    low = (left - high.astype(F32)).astype(BF)
    return dot(high, right) + dot(low, right)


def x_analysis_kernel(lines, table, plain, turned, out):
    rows = jnp.concatenate([lines[a] for a in range(N)], axis=1)
    both = dot(table[...], rows, 1, 1)
    half = KX * CY
    coef = split_dot(both[:half], plain[...]) + split_dot(both[half:], turned[...])
    units = [coef[:, k * 128 : k * 128 + 128].reshape(KX, CY, 128) for k in range(2)]
    out[...] = jnp.stack(units, axis=1).reshape(N, 24, 128).astype(BF)


def x_synthesis(modes, table, plain, turned):
    units = modes.reshape(KX, 2, CY, 128)
    flat = jnp.concatenate([units[:, k].reshape(KX * CY, 128) for k in range(2)], axis=1)
    flat = flat.astype(BF)
    half = KX * CY
    first = dot(plain, flat, 1, 1).astype(BF)
    second = dot(turned, flat, 1, 1).astype(BF)
    return dot(first, table[:half]) + dot(second, table[half:])


def x_synthesis_kernel(modes, table, plain, turned, out):
    lines = x_synthesis(modes[...].astype(F32), table[...], plain[...], turned[...])
    lines = lines.astype(BF)
    for a in range(N):
        out[a] = lines[:, a * 128 : a * 128 + 128]


def x_synthesis_sums_kernel(modes, table, plain, turned, out):
    wide = modes[...].astype(F32)
    lines = x_synthesis(wide[:, :24], table[...], plain[...], turned[...]).astype(BF)
    sums = jnp.sum(wide[:, 24:], axis=0)
    block = pack_sums(sums[:4] + sums[4:])
    tail = jnp.concatenate([block, jnp.zeros_like(block)], axis=0).astype(BF)
    for a in range(N):
        out[a, :ROWS] = lines[:, a * 128 : a * 128 + 128]
        out[a, ROWS:] = tail


def pack_sums(values):
    high = values.astype(BF).astype(F32)
    return jnp.concatenate([high, values - high], axis=0)


def turn_lanes(values, sign):
    part = lax.broadcasted_iota(jnp.int32, values.shape, 1) % 6
    ahead = pltpu.roll(values, 125, 1)
    behind = pltpu.roll(values, 3, 1)
    return jnp.where(part < 3, sign * ahead, -sign * behind)


def y_analysis(lines, table, channel, kind):
    wide = lines.astype(F32).reshape(N, 3, CY, 128)
    wide = jnp.concatenate([wide[:, u].reshape(NY, 128) for u in range(3)], axis=1)
    both = dot(table, wide.astype(BF))
    coefs = []
    for u in range(3):
        piece = both[:, u * 128 : u * 128 + 128]
        coef = piece[:KY] + turn_lanes(piece[KY:], 1.0)
        coefs.append(coef.astype(BF).astype(F32))
    result = []
    for part in range(2):
        rows = [
            coefs[u] * kind[part * 3 + mode : part * 3 + mode + 1]
            for u in range(3)
            for mode in range(3)
        ]
        rows = jnp.concatenate(rows, axis=0).astype(BF)
        result.append(dot(channel, rows, 1, 1))
    return result


def y_synthesis(parts, table, channel, kind):
    picked = [dot(part.astype(BF), channel[:C], 0, 0) for part in parts]
    columns = []
    for u in range(3):
        total = jnp.zeros((KY, 128), F32)
        for part in range(2):
            for mode in range(3):
                start = (u * 3 + mode) * KY
                mask = kind[part * 3 + mode : part * 3 + mode + 1]
                total = total + picked[part][start : start + KY] * mask
        columns.append(jnp.concatenate([total, turn_lanes(total, -1.0)], axis=0))
    columns = jnp.concatenate(columns, axis=1).astype(BF)
    lines = dot(table, columns, 0, 0)
    units = [lines[:, u * 128 : u * 128 + 128].reshape(N, CY, 128) for u in range(3)]
    return jnp.stack(units, axis=1).reshape(N, 24, 128)


def product_kernel(lines, weights, analysis, synthesis, channel, kind, out, coef):
    kinds = kind[...]
    real, imag = y_analysis(lines[...], analysis[...], channel[...], kinds)
    coef[0] = real
    coef[1] = imag
    product_re = jnp.zeros((C, LINE), F32)
    product_im = jnp.zeros((C, LINE), F32)
    for i in range(C):
        weight_re, weight_im = weights[0, i], weights[1, i]
        re, im = real[i : i + 1], imag[i : i + 1]
        product_re = product_re + (weight_re * re - weight_im * im)
        product_im = product_im + (weight_re * im + weight_im * re)
    out[...] = y_synthesis([product_re, product_im], synthesis[...], channel[...], kinds).astype(BF)


def back_kernel(lines, weights, sums, analysis, synthesis, channel, kind, out, dual):
    kinds = kind[...]
    real, imag = y_analysis(lines[...], analysis[...], channel[...], kinds)
    dual[0] = real
    dual[1] = imag
    re, im = real[:C], imag[:C]
    back_re, back_im = [], []
    for i in range(C):
        weight_re, weight_im = weights[0, i], weights[1, i]
        back_re.append(jnp.sum(weight_re * re + weight_im * im, axis=0, keepdims=True))
        back_im.append(jnp.sum(weight_re * im - weight_im * re, axis=0, keepdims=True))
    parts = [jnp.concatenate(back_re, axis=0), jnp.concatenate(back_im, axis=0)]
    modes = y_synthesis(parts, synthesis[...], channel[...], kinds)
    tail = jnp.broadcast_to(sums[...].reshape(1, 8, 128), (N, 8, 128))
    out[...] = jnp.concatenate([modes, tail], axis=1).astype(BF)


def weight_grad_kernel(coef, dual, out):
    dual_re, dual_im = dual[0, :C], dual[1, :C]
    for i in range(C):
        re, im = coef[0, i : i + 1], coef[1, i : i + 1]
        out[0, i] = re * dual_re + im * dual_im
        out[1, i] = re * dual_im - im * dual_re


def same_cell(size):
    row = lax.broadcasted_iota(jnp.int32, (size, size), 0) % CY
    column = lax.broadcasted_iota(jnp.int32, (size, size), 1) % CY
    return jnp.where(row == column, 1.0, 0.0)


def spread_map(weight, spread, weight_dim):
    tall = dot(spread, weight, 0, weight_dim).astype(BF)
    return (dot(tall, spread) * same_cell(C * CY)).astype(BF)


def pointwise_kernel(field, weight, bias, spread, out):
    mixing = spread_map(weight[...], spread[...], 1)
    for x in range(CX):
        out[x] = dot(mixing, field[x]) + bias[...]


def point_back_kernel(field, slope, weight, spread, out, sums):
    mixing = spread_map(weight[...], spread[...], 0)
    for x in range(CX):
        out[x] = dot(mixing, slope[x])
    fields = jnp.concatenate([field[x] for x in range(CX)], axis=1)
    slopes = jnp.concatenate([slope[x] for x in range(CX)], axis=1)
    cross = dot(fields, slopes, 1, 1) * same_cell(C * CY)
    ones = jnp.ones((8, CX * ZT), BF)
    bias = dot(ones, slopes, 1, 1)
    picks = spread[...].astype(F32)
    exact = lax.Precision.HIGHEST
    point = dot(dot(picks, cross, 1, 0, exact), picks, 1, 1, exact)
    total = dot(bias, picks, 1, 1, exact)[:1]
    rows = jnp.concatenate([point, total], axis=0)
    rows = jnp.concatenate([rows, jnp.zeros((C + 1, 128 - C), F32)], axis=1)
    packed = []
    for r in range(4):
        line = jnp.zeros((1, 128), F32)
        for q in range(6):
            if r * 6 + q <= C:
                row = rows[r * 6 + q : r * 6 + q + 1]
                line = line + (pltpu.roll(row, q * C, 1) if q > 0 else row)
        packed.append(line)
    sums[...] = pack_sums(jnp.concatenate(packed, axis=0))


def cells_kernel(lines, depth, pointwise, cotangent, field_out, slope_out, out):
    for group in range(GROUPS):
        rows = lines[:, group * 48 : group * 48 + 48, :].reshape(N * 48, 128)
        span = slice(group * 32, group * 32 + 32)
        pre = dot(rows, depth[...], 0, 0) + to_columns(pointwise[:, span, :])
        phi = 0.5 * (1.0 + lax.erf(pre * 0.7071067811865476))
        field_out[:, span, :] = to_cells(pre * phi).astype(BF)
        slope = phi + pre * jnp.exp(-0.5 * pre * pre) * 0.3989422804014327
        slope = slope * to_columns(cotangent[:, span, :])
        slope_out[:, span, :] = to_cells(slope).astype(BF)
        spectrum = dot(depth[...], slope.astype(BF), 1, 1)
        out[:, group * 48 : group * 48 + 48, :] = spectrum.astype(BF).reshape(N, 48, 128)


def last_kernel(lines, depth, pointwise, field_out, point_out, bias_out):
    for group in range(GROUPS):
        rows = lines[:, group * 48 : group * 48 + 48, :].reshape(N * 48, 128)
        span = slice(group * 32, group * 32 + 32)
        total = to_cells(dot(rows, depth[...], 0, 0)) + pointwise[:, span, :]
        field_out[:, span, :] = total.astype(BF)
    tails = jnp.sum(lines[:, ROWS:, :].astype(F32), axis=0)
    sums = (tails[:4] + tails[4:8]) * (NX * NY * ZT) ** -0.5
    for r in range(4):
        for q in range(6):
            index = r * 6 + q
            if index <= C:
                row = sums[r : r + 1]
                row = pltpu.roll(row, 128 - q * C, 1) if q > 0 else row
                if index < C:
                    point_out[index : index + 1, :] = row[:, :C]
                else:
                    bias_out[...] = row[:, :C]


def exchange(values, axis):
    return lax.all_to_all(values, axis, split_axis=0, concat_axis=0, tiled=True)


def body(field_in, point_weight, point_bias, spec_weight, out_cotangent):
    cells = (CX, C * CY, ZT)
    line_message = shaped((N, ROWS, 128), BF)
    mode_message = shaped((N, 24, 128), BF)
    field = field_in.transpose(0, 2, 1, 3).reshape(cells)
    cotangent = out_cotangent.transpose(0, 2, 1, 3).reshape(cells)
    weights = spec_weight.transpose(3, 1, 2, 4, 0).reshape(2, C, C, LINE).astype(F32)
    bias = jnp.broadcast_to(point_bias[:, None, None], (C, CY, 1)).reshape(C * CY, 1)

    message = call(spectrum_kernel, line_message, name="spectrum")(field, DEPTH_IN)
    message = exchange(message, "gx")
    pointwise = call(pointwise_kernel, shaped(cells, F32), name="pointwise")(
        field, point_weight, bias, SPREAD
    )
    message = call(x_analysis_kernel, mode_message, name="x_analysis")(message, X_IN, PLAIN, TURNED)
    message = exchange(message, "gy")
    message, coef = call(
        product_kernel, (mode_message, shaped((2, 24, LINE), F32)), name="product"
    )(message, weights, Y_IN, Y_MID, CHANNEL, KIND)
    message = exchange(message, "gy")
    message = call(x_synthesis_kernel, line_message, name="x_synthesis")(
        message, X_MID, PLAIN, TURNED
    )
    message = exchange(message, "gx")
    output_field, slope, message = call(
        cells_kernel, (shaped(cells, BF), shaped(cells, BF), line_message), name="cells"
    )(message, DEPTH_MID, pointwise, cotangent)
    message = exchange(message, "gx")
    point_back, sums = call(
        point_back_kernel, (shaped(cells, F32), shaped((8, 128), F32)), name="point_back"
    )(field, slope, point_weight, SPREAD)
    message = call(x_analysis_kernel, mode_message, name="x_analysis_back")(
        message, X_MID, PLAIN, TURNED
    )
    message = exchange(message, "gy")
    message, dual = call(
        back_kernel,
        (shaped((N, 32, 128), BF), shaped((2, 24, LINE), F32)),
        name="back",
    )(message, weights, sums, Y_MID, Y_IN, CHANNEL, KIND)
    message = exchange(message, "gy")
    weight_grad = call(weight_grad_kernel, shaped((2, C, C, LINE), F32), name="weight_grad")(
        coef, dual
    )
    message = call(x_synthesis_sums_kernel, shaped((N, 256, 128), BF), name="x_synthesis_back")(
        message, X_IN, PLAIN, TURNED
    )
    message = exchange(message, "gx")
    grad_in, grad_point, grad_bias = call(
        last_kernel,
        (shaped(cells, BF), shaped((C, C), F32), shaped((1, C), F32)),
        name="last",
    )(message, DEPTH_IN, point_back)
    grad_spec = weight_grad.reshape(2, C, C, PAIRS, KY).transpose(4, 1, 2, 0, 3)

    def natural(values):
        return values.reshape(CX, C, CY, ZT).transpose(0, 2, 1, 3)

    return natural(output_field), natural(grad_in), grad_spec, grad_point, grad_bias.reshape(C)


def solution(mesh):
    return jax.shard_map(
        body,
        mesh=mesh,
        in_specs=(
            P("gx", "gy", None, None),
            P(),
            P(),
            P(None, None, None, None, ("gx", "gy")),
            P("gx", "gy", None, None),
        ),
        out_specs=(
            P("gx", "gy", None, None),
            P("gx", "gy", None, None),
            P(None, None, None, None, ("gx", "gy")),
            P(),
            P(),
        ),
        check_vma=False,
    )
```

profile of v0, /device:TPU:1, one launch (start us, length us, event | category | flops | bytes accessed | tf_op | source)
XLA Modules:
  0.0 180.6 jit_solution(7967816402618821219)
XLA Ops:
  0.6 1.1 copy-done.3
  1.7 1.1 copy-done.8
  2.9 1.2 spectrum.1
  4.0 23.0 %all_to_all.40.lines = bf16[16,240,128]{2,1,0:T(8,128)(2,1)S(1)} all-to-all(bf16[16,240,128]{2,1,0:T(8,128)(2,1)S(1)} %spectrum.1), channel_id=1, replica_groups=mesh['gx'=16,'gy'=16] {'gx'}, dimensions={0} | all-to-all | bytes 1966080 | tf_op jit(solution)/shard_map/all_to_all | solution.py:370
  27.0 1.6 x_analysis.1
  28.6 10.3 %all-to-all-start.1 = ((bf16[16,24,128]{2,1,0:T(8,128)(2,1)}), bf16[16,24,128]{2,1,0:T(8,128)(2,1)S(1)}, u32[]{:S(2)}, u32[]{:S(2)}) async-start(bf16[16,24,128]{2,1,0:T(8,128)(2,1)} %x_analysis.1), calls=%async_computation.1 | async-start | bytes 196608 | tf_op jit(solution)/shard_map/all_to_all | solution.py:370
  38.9 2.8 %convert_bitcast_fusion = f32[2,20,20,9,24]{4,0,3,2,1:T(2,128)S(1)} fusion(bf16[24,20,20,2,9]{0,3,4,2,1:T(2,128)(2,1)} %param.19), kind=kLoop, calls=%fused_computation | loop fusion | flops 172800 | bytes 1036800 | tf_op jit(solution)/shard_map/convert_element_type | solution.py:379
  41.7 3.6 %copy.29 = f32[2,20,20,9,24]{4,3,2,1,0:T(8,128)} copy(f32[2,20,20,9,24]{4,0,3,2,1:T(2,128)S(1)} %convert_bitcast_fusion) | data formatting | bytes 1382400 | tf_op jit(solution)/shard_map/convert_element_type | solution.py:379
  45.3 4.5 %reshape.45.weights = f32[2,20,20,216]{3,2,1,0:T(8,128)S(1)} reshape(f32[2,20,20,9,24]{4,3,2,1,0:T(8,128)} %copy.29) | data formatting | bytes 1382400 | tf_op jit(solution)/shard_map/convert_element_type | solution.py:379
  51.4 15.5 %all_to_all.41.modes = bf16[16,24,128]{2,1,0:T(8,128)(2,1)S(1)} all-to-all(bf16[16,24,128]{2,1,0:T(8,128)(2,1)S(1)} %get-tuple-element.17), channel_id=1, replica_groups=mesh['gx'=16,'gy'=16] {'gy'}, dimensions={0} | all-to-all | bytes 196608 | tf_op jit(solution)/shard_map/all_to_all | solution.py:370
  66.9 1.4 copy-done.1
  70.1 4.3 %all-to-all-start.3 = ((bf16[16,240,128]{2,1,0:T(8,128)(2,1)}), bf16[16,240,128]{2,1,0:T(8,128)(2,1)}, u32[]{:S(2)}, u32[]{:S(2)}) async-start(bf16[16,240,128]{2,1,0:T(8,128)(2,1)} %copy-done.7), calls=%async_computation.3 | async-start | bytes 1966080 | tf_op jit(solution)/shard_map/all_to_all | solution.py:370
  78.5 14.7 %all-to-all-done.3.lines = bf16[16,240,128]{2,1,0:T(8,128)(2,1)} async-done(((bf16[16,240,128]{2,1,0:T(8,128)(2,1)}), bf16[16,240,128]{2,1,0:T(8,128)(2,1)}, u32[]{:S(2)}, u32[]{:S(2)}) %all-to-all-start.3) | async-done | bytes 983072 | tf_op jit(solution)/shard_map/all_to_all | solution.py:370
  93.2 1.3 copy-done.6
  94.5 1.1 copy-done.14
  95.6 1.1 copy-done.15
  96.7 4.0 %cells.1 = (bf16[16,160,128]{2,1,0:T(8,128)(2,1)}, bf16[16,160,128]{2,1,0:T(8,128)(2,1)S(1)}, bf16[16,240,128]{2,1,0:T(8,128)(2,1)S(1)}) custom-call(bf16[16,240,128]{2,1,0:T(8,128)(2,1)} %all-to-all-done.3.lines, bf16[768,512]{1,0:T(8,128)(2,1)S(1)} %copy-done.14, f32[16,160,128]{2,1,0:T(8,128)S(1)} %copy-done.6, bf16[16,160,128]{2,1,0:T(8,128)(2,1)S(1)} %bitcast.21), custom_call_target="tpu_custom_call" | custom-call | flops 100000000 | bytes 4000000 | tf_op jit(solution)/shard_map/cells/pallas_call | solution.py:397
  100.7 18.3 %all_to_all.42.lines = bf16[16,240,128]{2,1,0:T(8,128)(2,1)S(1)} all-to-all(bf16[16,240,128]{2,1,0:T(8,128)(2,1)S(1)} %get-tuple-element.19), channel_id=1, replica_groups=mesh['gx'=16,'gy'=16] {'gx'}, dimensions={0} | all-to-all | bytes 1966080 | tf_op jit(solution)/shard_map/all_to_all | solution.py:370
  119.0 1.6 x_analysis_back.1
  120.6 5.1 %all-to-all-start.5 = ((bf16[16,24,128]{2,1,0:T(8,128)(2,1)}), bf16[16,24,128]{2,1,0:T(8,128)(2,1)S(1)}, u32[]{:S(2)}, u32[]{:S(2)}) async-start(bf16[16,24,128]{2,1,0:T(8,128)(2,1)} %x_analysis_back.1), calls=%async_computation.5 | async-start | bytes 196608 | tf_op jit(solution)/shard_map/all_to_all | solution.py:370
  125.7 1.1 copy-done.17
  128.2 1.6 point_back.1
  129.8 1.1 copy-done.12
  131.5 2.7 %all-to-all-done.5.lines = bf16[16,24,128]{2,1,0:T(8,128)(2,1)S(1)} async-done(((bf16[16,24,128]{2,1,0:T(8,128)(2,1)}), bf16[16,24,128]{2,1,0:T(8,128)(2,1)S(1)}, u32[]{:S(2)}, u32[]{:S(2)}) %all-to-all-start.5) | async-done | bytes 98336 | tf_op jit(solution)/shard_map/all_to_all | solution.py:370
  138.7 13.5 %all_to_all.43.modes = bf16[16,32,128]{2,1,0:T(8,128)(2,1)S(1)} all-to-all(bf16[16,32,128]{2,1,0:T(8,128)(2,1)S(1)} %get-tuple-element.22), channel_id=1, replica_groups=mesh['gx'=16,'gy'=16] {'gy'}, dimensions={0} | all-to-all | bytes 262144 | tf_op jit(solution)/shard_map/all_to_all | solution.py:370
  152.2 1.9 %x_synthesis_back.1 = bf16[16,256,128]{2,1,0:T(8,128)(2,1)} custom-call(bf16[16,32,128]{2,1,0:T(8,128)(2,1)S(1)} %all_to_all.43.modes, bf16[384,2048]{1,0:T(8,128)(2,1)S(1)} %copy-done, bf16[240,256]{1,0:T(8,128)(2,1)S(1)} %copy-done.10, bf16[240,256]{1,0:T(8,128)(2,1)S(1)} %copy-done.11), custom_call_target="tpu_custom_call" | custom-call | flops 100000000 | bytes 4000000 | tf_op jit(solution)/shard_map/x_synthesis_back/pallas_call | solution.py:417
  154.1 3.7 %all-to-all-start.7 = ((bf16[16,256,128]{2,1,0:T(8,128)(2,1)}), bf16[16,256,128]{2,1,0:T(8,128)(2,1)S(1)}, u32[]{:S(2)}, u32[]{:S(2)}) async-start(bf16[16,256,128]{2,1,0:T(8,128)(2,1)} %x_synthesis_back.1), calls=%async_computation.7 | async-start | bytes 2097152 | tf_op jit(solution)/shard_map/all_to_all | solution.py:370
  158.5 4.5 %reshape.42 = f32[2,20,20,9,24]{4,3,0,2,1:T(8,128)} reshape(f32[2,20,20,216]{3,0,2,1:T(2,128)S(1)} %copy.27) | data formatting | bytes 1382400 | tf_op jit(solution)/shard_map/reshape | solution.py:426
  163.0 6.7 %copy.28 = f32[24,20,20,2,9]{0,3,4,2,1:T(2,128)} copy(f32[24,20,20,2,9]{0,4,3,2,1:T(8,128)} %bitcast.22) | data formatting | bytes 1382400
  169.7 8.0 %all-to-all-done.7.lines = bf16[16,256,128]{2,1,0:T(8,128)(2,1)S(1)} async-done(((bf16[16,256,128]{2,1,0:T(8,128)(2,1)}), bf16[16,256,128]{2,1,0:T(8,128)(2,1)S(1)}, u32[]{:S(2)}, u32[]{:S(2)}) %all-to-all-start.7) | async-done | bytes 1048608 | tf_op jit(solution)/shard_map/all_to_all | solution.py:370
  177.7 1.3 copy-done.13
  179.0 1.5 last.1
  (70 shorter events, 14.6 us)
Async XLA Ops:
  0.6 1.1 copy-start.3
  1.7 1.1 copy-start.8
  2.9 24.1 %copy-start = (bf16[384,2048]{1,0:T(8,128)(2,1)S(1)}, bf16[384,2048]{1,0:T(8,128)(2,1)}, u32[]{:S(2)}) copy-start(bf16[384,2048]{1,0:T(8,128)(2,1)} %constant.24.clone.table) | copy-start | bytes 4718596
  2.9 24.1 %copy-start.10 = (bf16[240,256]{1,0:T(8,128)(2,1)S(1)}, bf16[240,256]{1,0:T(8,128)(2,1)}, u32[]{:S(2)}) copy-start(bf16[240,256]{1,0:T(8,128)(2,1)} %constant.25.clone.plain) | copy-start | bytes 368644
  2.9 24.2 %copy-start.11 = (bf16[240,256]{1,0:T(8,128)(2,1)S(1)}, bf16[240,256]{1,0:T(8,128)(2,1)}, u32[]{:S(2)}) copy-start(bf16[240,256]{1,0:T(8,128)(2,1)} %constant.26.clone.turned) | copy-start | bytes 368644
  28.6 21.2 %all-to-all-start.1 = ((bf16[16,24,128]{2,1,0:T(8,128)(2,1)}), bf16[16,24,128]{2,1,0:T(8,128)(2,1)S(1)}, u32[]{:S(2)}, u32[]{:S(2)}) async-start(bf16[16,24,128]{2,1,0:T(8,128)(2,1)} %x_analysis.1), calls=%async_computation.1 | async-start | bytes 196608 | tf_op jit(solution)/shard_map/all_to_all | solution.py:370
  45.3 4.5 %copy-start.18 = (bf16[48,128]{1,0:T(8,128)(2,1)S(1)}, bf16[48,128]{1,0:T(8,128)(2,1)}, u32[]{:S(2)}) copy-start(bf16[48,128]{1,0:T(8,128)(2,1)} %constant.27.clone.analysis.synthesis) | copy-start | bytes 36868
  45.3 4.5 %copy-start.20 = (bf16[48,128]{1,0:T(8,128)(2,1)S(1)}, bf16[48,128]{1,0:T(8,128)(2,1)}, u32[]{:S(2)}) copy-start(bf16[48,128]{1,0:T(8,128)(2,1)} %constant.28.clone.synthesis.analysis) | copy-start | bytes 36868
  45.3 4.5 %copy-start.26 = (bf16[24,128]{1,0:T(8,128)(2,1)S(1)}, bf16[24,128]{1,0:T(8,128)(2,1)}, u32[]{:S(2)}) copy-start(bf16[24,128]{1,0:T(8,128)(2,1)} %constant.29.clone.channel) | copy-start | bytes 18436
  45.3 4.6 %copy-start.30 = (f32[8,128]{1,0:T(8,128)S(1)}, f32[8,128]{1,0:T(8,128)}, u32[]{:S(2)}) copy-start(f32[8,128]{1,0:T(8,128)} %constant.30.clone.kind) | copy-start | bytes 12292
  66.9 1.4 copy-start.1
  68.3 6.1 %copy-start.34 = (f32[20]{0:T(128)S(1)}, f32[20]{0:T(128)}, u32[]{:S(2)}) copy-start(f32[20]{0:T(128)} %param.18) | copy-start | bytes 244
  68.3 7.6 %copy-start.4 = (bf16[16,8,20,128]{3,1,2,0:T(8,128)(2,1)S(1)}, bf16[16,8,20,128]{3,1,2,0:T(8,128)(2,1)}, u32[]{:S(2)}) copy-start(bf16[16,8,20,128]{3,1,2,0:T(8,128)(2,1)} %param.16) | copy-start | bytes 1966084
  68.3 7.6 %copy-start.24 = (bf16[20,160]{1,0:T(8,128)(2,1)S(1)}, bf16[20,160]{1,0:T(8,128)(2,1)}, u32[]{:S(2)}) copy-start(bf16[20,160]{1,0:T(8,128)(2,1)} %constant.23.clone.spread) | copy-start | bytes 19204
  69.2 1.0 copy-start.7
  70.1 23.1 %all-to-all-start.3 = ((bf16[16,240,128]{2,1,0:T(8,128)(2,1)}), bf16[16,240,128]{2,1,0:T(8,128)(2,1)}, u32[]{:S(2)}, u32[]{:S(2)}) async-start(bf16[16,240,128]{2,1,0:T(8,128)(2,1)} %copy-done.7), calls=%async_computation.3 | async-start | bytes 1966080 | tf_op jit(solution)/shard_map/all_to_all | solution.py:370
  77.4 1.1 copy-start.5
  93.2 1.3 copy-start.6
  94.5 1.1 copy-start.14
  95.6 1.1 copy-start.15
  100.7 18.3 %copy-start.16 = (bf16[16,160,128]{2,1,0:T(8,128)(2,1)}, bf16[16,160,128]{2,1,0:T(8,128)(2,1)S(1)}, u32[]{:S(2)}) copy-start(bf16[16,160,128]{2,1,0:T(8,128)(2,1)S(1)} %get-tuple-element.20.slope) | copy-start | bytes 1966084
  100.7 18.3 %copy-start.2 = (bf16[384,2048]{1,0:T(8,128)(2,1)S(1)}, bf16[384,2048]{1,0:T(8,128)(2,1)}, u32[]{:S(2)}) copy-start(bf16[384,2048]{1,0:T(8,128)(2,1)} %constant.31.clone.table) | copy-start | bytes 4718596
  120.6 13.6 %all-to-all-start.5 = ((bf16[16,24,128]{2,1,0:T(8,128)(2,1)}), bf16[16,24,128]{2,1,0:T(8,128)(2,1)S(1)}, u32[]{:S(2)}, u32[]{:S(2)}) async-start(bf16[16,24,128]{2,1,0:T(8,128)(2,1)} %x_analysis_back.1), calls=%async_computation.5 | async-start | bytes 196608 | tf_op jit(solution)/shard_map/all_to_all | solution.py:370
  125.7 1.1 copy-start.17
  126.8 0.7 copy-start.25
  129.8 1.1 copy-start.12
  134.2 0.7 copy-start.19
  134.9 0.7 copy-start.21
  152.2 5.6 %copy-start.23 = (f32[2,24,216]{2,1,0:T(8,128)S(1)}, f32[2,24,216]{2,1,0:T(8,128)}, u32[]{:S(2)}) copy-start(f32[2,24,216]{2,1,0:T(8,128)} %copy-done.22) | copy-start | bytes 124420
  154.1 23.6 %all-to-all-start.7 = ((bf16[16,256,128]{2,1,0:T(8,128)(2,1)}), bf16[16,256,128]{2,1,0:T(8,128)(2,1)S(1)}, u32[]{:S(2)}, u32[]{:S(2)}) async-start(bf16[16,256,128]{2,1,0:T(8,128)(2,1)} %x_synthesis_back.1), calls=%async_computation.7 | async-start | bytes 2097152 | tf_op jit(solution)/shard_map/all_to_all | solution.py:370
  163.0 14.7 %copy-start.9 = (bf16[768,512]{1,0:T(8,128)(2,1)S(1)}, bf16[768,512]{1,0:T(8,128)(2,1)}, u32[]{:S(2)}) copy-start(bf16[768,512]{1,0:T(8,128)(2,1)} %constant.22.clone.depth) | copy-start | bytes 2359300
  177.7 1.3 copy-start.13
  (7 other events, 4.7 us)
where the time goes:
time: 182 us; the launch traced here: 181 us
  blocking collectives  70.3 us (39%)
  local copies, waits for them, and re-layouts  40.8 us (22%)
  waiting for transfers between devices  25.5 us (14%)
  starting transfers between devices  23.4 us (13%)
  Pallas kernels  17 us (9%)
  other arithmetic  2.77 us (2%)
    all_to_all x4, blocking collectives, exchange(): return lax.all_to_all(values, axis, split_axis=0, concat_axis=0, tiled=True)  70.3 us
    unnamed x71, local copies, waits for them, and re-layouts  26.1 us
    all_to_all x4, waiting for transfers between devices, exchange(): return lax.all_to_all(values, axis, split_axis=0, concat_axis=0, tiled=True)  25.5 us
    all_to_all x4, starting transfers between devices, exchange(): return lax.all_to_all(values, axis, split_axis=0, concat_axis=0, tiled=True)  23.4 us
    convert_element_type x2, local copies, waits for them, and re-layouts, body(): spec_weight.transpose(3, 1, 2, 4, 0).reshape(2, C, C, LINE).astype(F32)  8.08 us
    reshape x1, local copies, waits for them, and re-layouts, body(): grad_spec = weight_grad.reshape(2, C, C, PAIRS, KY).transpose(4, 1, 2, 0, 3)  4.46 us
    pallas_call x1, Pallas kernels, body(): call(cells_kernel, (shaped(cells, BF), shaped(cells, BF), line_message),...  3.96 us
  transfers between devices with their start and end apart: 4, of which 3 were waited for; matrix products, arithmetic and copies ran while one was open for 13% of the time, Pallas kernels for 1%

commit v1 on v0

v1 whole, which is shorter than its diff:
```python
import math

import jax
import jax.numpy as jnp
import ml_dtypes
import numpy as np
from jax import lax
from jax.experimental import pallas as pl
from jax.experimental.pallas import tpu as pltpu
from jax.sharding import PartitionSpec as P

C = 20
Z = 32
T_SIZE = 4
KX = 24
KY = 24
KZ = 24
KT = 4
NX = 256
NY = 128
ZT = 128
M = 96
N = 16
CX = NX // N
CY = NY // N
ROWS = 12 * C
GROUPS = C // 4
PAIRS = 9
WEIGHTS = C * C * PAIRS * 2

BF = jnp.bfloat16
F32 = jnp.float32


def centered(count):
    return (np.arange(count) + count // 2) % count - count // 2


def rounded(table):
    return np.asarray(table, np.float32).astype(ml_dtypes.bfloat16)


def line_table(modes, length, scale):
    turns = centered(modes)[:, None] * np.arange(length)[None, :] % length
    angle = turns.astype(np.float32) * np.float32(2.0 * math.pi / length)
    scale = np.float32(scale)
    return rounded(np.cos(angle) * scale), rounded(np.sin(angle) * scale)


def depth_table(scale):
    cells = np.arange(ZT)
    turn_z = centered(KZ)[:, None] * (cells // T_SIZE)[None, :] % Z
    turn_t = centered(KT)[:, None] * (cells % T_SIZE)[None, :] % T_SIZE
    angle = turn_z.astype(np.float32)[:, None, :] * np.float32(2.0 * math.pi / Z)
    angle = angle + turn_t.astype(np.float32)[None, :, :] * np.float32(2.0 * math.pi / T_SIZE)
    angle = angle.reshape(M, ZT)
    return rounded(np.stack([np.cos(angle), -np.sin(angle)]) * np.float32(scale))


def depth_rows(scale):
    table = depth_table(scale).reshape(2, N, 2, 3, ZT).transpose(1, 2, 0, 3, 4)
    table = np.broadcast_to(table[:, :, None], (N, 2, 4, 2, 3, ZT))
    return np.ascontiguousarray(table).reshape(2 * N, 24, ZT)


def x_rows(scale):
    table = np.concatenate(line_table(KX, NX, scale), axis=0)
    return np.ascontiguousarray(np.repeat(table, CY, axis=1))


def y_rows(scale):
    return np.concatenate(line_table(KY, NY, scale), axis=0)


def lane_picks():
    rows, lanes = np.arange(6 * 24)[:, None], np.arange(128)[None, :]
    return rounded((lanes == rows % 24 * 6 + rows // 24) & (rows % 24 < C))


DEPTH_IN = depth_rows(ZT**-0.5)
DEPTH_MID = depth_rows(M**-0.5)
X_IN = x_rows(NX**-0.5)
X_MID = x_rows(KX**-0.5)
Y_ALL = np.concatenate([y_rows(NY**-0.5), y_rows(KY**-0.5), lane_picks()], axis=0)
Y_IN = slice(0, 48)
Y_MID = slice(48, 96)
PICKS = slice(96, 96 + 144)


def dot(left, right, left_dim=1, right_dim=0, precision=None):
    return lax.dot_general(
        left,
        right,
        (((left_dim,), (right_dim,)), ((), ())),
        precision=precision,
        preferred_element_type=F32,
    )


def call(kernel, out_shape, spaces=None, out_spaces=None, scratch=(), name=None, limit=24 * 2**20):
    def spec(space):
        return pl.BlockSpec(memory_space=space)

    options = {}
    if spaces is not None:
        options["in_specs"] = [spec(space) for space in spaces]
    if out_spaces is not None:
        specs = [spec(space) for space in out_spaces]
        options["out_specs"] = specs if isinstance(out_shape, (tuple, list)) else specs[0]
    return pl.pallas_call(
        kernel,
        out_shape=out_shape,
        scratch_shapes=scratch,
        compiler_params=pltpu.CompilerParams(vmem_limit_bytes=limit),
        cost_estimate=pl.CostEstimate(flops=10**8, bytes_accessed=4 * 10**6, transcendentals=0),
        name=name,
        **options,
    )


VMEM = pltpu.VMEM
HBM = pltpu.HBM
DMA = pltpu.SemaphoreType.DMA


def shaped(shape, dtype):
    return jax.ShapeDtypeStruct(shape, dtype)


def start_copies(pairs, semaphores, base=0):
    copies = [
        pltpu.make_async_copy(source, target, semaphores.at[base + k])
        for k, (source, target) in enumerate(pairs)
    ]
    for copy in copies:
        copy.start()
    return copies


def rows_of(group, count):
    return slice(group * count, group * count + count)


def iota(shape, dim):
    return lax.broadcasted_iota(jnp.int32, shape, dim)


def ones_where(condition):
    return jnp.where(condition, 1.0, 0.0)


def depth_matrix(rows):
    wide = rows.astype(F32)
    channel = iota((1, 24, 1), 1) // 6
    parts = [(wide * ones_where(channel == k)).reshape(N * 48, ZT) for k in range(4)]
    return jnp.concatenate(parts, axis=1).astype(BF)


def x_matrix(rows):
    size = rows.shape[1]
    same = ones_where(iota((1, CY, size), 1) == iota((1, CY, size), 2) % CY)
    wide = rows.astype(F32).reshape(KX, 1, size) * same
    return wide.reshape(KX * CY, size).astype(BF)


def lane_maps():
    row, lane = iota((ROWS, 1), 0), iota((1, 256), 1)
    inner = row % 24
    start = (row // 24) % 2 * 128 + row // 48 * 24
    real = inner % 6 < 3
    plain = ones_where(lane == start + inner)
    other = jnp.where(real, inner + 3, inner - 3)
    turned = ones_where(lane == start + other) * jnp.where(real, -1.0, 1.0)
    return plain.astype(BF), turned.astype(BF)


def spread_matrix():
    return ones_where(iota((C, C * CY), 0) == iota((C, C * CY), 1) // CY)


def to_columns(values):
    wide = values.astype(F32).reshape(CX, 4, CY, ZT)
    return jnp.concatenate([wide[:, k].reshape(CX * CY, ZT) for k in range(4)], axis=1)


def to_cells(columns):
    parts = [columns[:, k * ZT : (k + 1) * ZT].reshape(CX, CY, ZT) for k in range(4)]
    return jnp.stack(parts, axis=1).reshape(CX, 4 * CY, ZT)


def wide_to_columns(wide):
    def channel(k):
        rows = wide[k * CY : k * CY + CY]
        return jnp.concatenate([rows[:, x * ZT : x * ZT + ZT] for x in range(CX)], axis=0)

    return jnp.concatenate([channel(k) for k in range(4)], axis=1)


def wide_to_cells(wide):
    return jnp.stack([wide[:, x * ZT : x * ZT + ZT] for x in range(CX)], axis=0)


def spectrum_kernel(field, depth, out):
    matrix = depth_matrix(depth[...])
    for group in range(GROUPS):
        columns = to_columns(field[:, rows_of(group, 32), :]).astype(BF)
        spectrum = dot(matrix, columns, 1, 1)
        out[:, rows_of(group, 48), :] = spectrum.astype(BF).reshape(N, 48, 128)


def split_dot(left, right):
    high = left.astype(BF)
    low = (left - high.astype(F32)).astype(BF)
    return dot(high, right) + dot(low, right)


def x_analysis_kernel(lines, table, out):
    plain, turned = lane_maps()
    rows = jnp.concatenate([lines[a] for a in range(N)], axis=1)
    coef = split_dot(dot(x_matrix(table[:KX]), rows, 1, 1), plain)
    coef = coef + split_dot(dot(x_matrix(table[KX:]), rows, 1, 1), turned)
    units = [coef[:, k * 128 : k * 128 + 128].reshape(KX, CY, 128) for k in range(2)]
    out[...] = jnp.stack(units, axis=1).reshape(N, 24, 128).astype(BF)


def x_modes(modes):
    plain, turned = lane_maps()
    units = modes.reshape(KX, 2, CY, 128)
    flat = jnp.concatenate([units[:, k].reshape(KX * CY, 128) for k in range(2)], axis=1)
    flat = flat.astype(BF)
    return dot(plain, flat, 1, 1).astype(BF), dot(turned, flat, 1, 1).astype(BF)


def x_lines(first, second, table):
    lines = dot(first, x_matrix(table[:KX])) + dot(second, x_matrix(table[KX:]))
    return lines.astype(BF)


def x_synthesis_kernel(modes, table, out):
    first, second = x_modes(modes[...].astype(F32))
    lines = x_lines(first, second, table[...])
    for a in range(N):
        out[a] = lines[:, a * 128 : a * 128 + 128]


def x_synthesis_sums_kernel(modes, table, out):
    wide = modes[...].astype(F32)
    first, second = x_modes(wide[:, :24])
    lines = x_lines(first, second, table[...])
    sums = jnp.sum(wide[:, 24:], axis=0)
    block = pack_sums(sums[:4] + sums[4:])
    tail = jnp.concatenate([block, jnp.zeros_like(block)], axis=0).astype(BF)
    for a in range(N):
        out[a, :ROWS] = lines[:, a * 128 : a * 128 + 128]
        out[a, ROWS:] = tail


def pack_sums(values):
    high = values.astype(BF).astype(F32)
    return jnp.concatenate([high, values - high], axis=0)


def turn_lanes(values, sign):
    part = iota(values.shape, 1) % 6
    ahead = pltpu.roll(values, 125, 1)
    behind = pltpu.roll(values, 3, 1)
    return jnp.where(part < 3, sign * ahead, -sign * behind)


def y_analysis(lines, table, picks):
    wide = lines.astype(F32).reshape(N, 3, CY, 128)
    wide = jnp.concatenate([wide[:, u].reshape(NY, 128) for u in range(3)], axis=1)
    both = dot(table, wide.astype(BF))
    result = []
    for u in range(3):
        piece = both[:, u * 128 : u * 128 + 128]
        coef = piece[:KY] + turn_lanes(piece[KY:], 1.0)
        result.append(dot(picks, coef.astype(BF), 1, 1))
    return result


def y_synthesis(units, table, picks):
    columns = []
    for unit in units:
        modes = dot(unit.astype(BF), picks, 0, 0)
        columns.append(jnp.concatenate([modes, turn_lanes(modes, -1.0)], axis=0))
    columns = jnp.concatenate(columns, axis=1).astype(BF)
    lines = dot(table, columns, 0, 0)
    lines = [lines[:, u * 128 : u * 128 + 128].reshape(N, CY, 128) for u in range(3)]
    return jnp.stack(lines, axis=1).reshape(N, 24, 128)


def line_of(modes, unit, kind, channel):
    return modes[unit, pl.ds(kind * 24 + channel, 1), :]


def load_weights(weights, wide):
    step = WEIGHTS // 10
    for k in range(10):
        wide[k * step : k * step + step, :] = weights[k * step : k * step + step, :].astype(F32)


def mix_channels(weights, modes, out_step, in_step, sign):
    units = []
    for unit in range(3):
        reals, imags = [], []
        for mode in range(3):
            pair = unit * 3 + mode
            real = jnp.zeros((C, KY), F32)
            imag = jnp.zeros((C, KY), F32)
            for k in range(C):
                start = k * in_step + 2 * pair
                weight_re = weights[pl.ds(start, C, stride=out_step), :]
                weight_im = weights[pl.ds(start + 1, C, stride=out_step), :]
                re = line_of(modes, unit, mode, k)
                im = line_of(modes, unit, 3 + mode, k)
                real = real + (weight_re * re - sign * (weight_im * im))
                imag = imag + (weight_re * im + sign * (weight_im * re))
            reals.append(real)
            imags.append(imag)
        empty = jnp.zeros((4, KY), F32)
        parts = [jnp.concatenate([part, empty], axis=0) for part in reals + imags]
        units.append(jnp.concatenate(parts, axis=0))
    return units


def product_kernel(lines, weights, tables, out, coef, wide):
    load_weights(weights, wide)
    for u, unit in enumerate(y_analysis(lines[...], tables[Y_IN], tables[PICKS])):
        coef[u] = unit
    product = mix_channels(wide, coef, 2 * PAIRS, 2 * PAIRS * C, 1.0)
    out[...] = y_synthesis(product, tables[Y_MID], tables[PICKS]).astype(BF)


def back_kernel(lines, weights, sums, tables, out, dual, wide):
    load_weights(weights, wide)
    for u, unit in enumerate(y_analysis(lines[...], tables[Y_MID], tables[PICKS])):
        dual[u] = unit
    modes = mix_channels(wide, dual, 2 * PAIRS * C, 2 * PAIRS, -1.0)
    modes = y_synthesis(modes, tables[Y_IN], tables[PICKS])
    tail = jnp.broadcast_to(sums[...].reshape(1, 8, 128), (N, 8, 128))
    out[...] = jnp.concatenate([modes, tail], axis=1).astype(BF)


def weight_gradient(coef, dual, channel, out):
    for pair in range(PAIRS):
        unit, mode = divmod(pair, 3)
        dual_re = dual[unit, mode * 24 : mode * 24 + C, :]
        dual_im = dual[unit, (3 + mode) * 24 : (3 + mode) * 24 + C, :]
        re = line_of(coef, unit, mode, channel)
        im = line_of(coef, unit, 3 + mode, channel)
        start = channel * 2 * PAIRS * C + 2 * pair
        out[pl.ds(start, C, stride=2 * PAIRS), :] = re * dual_re + im * dual_im
        out[pl.ds(start + 1, C, stride=2 * PAIRS), :] = re * dual_im - im * dual_re


def same_cell(size):
    return ones_where(iota((size, 1), 0) % CY == iota((1, size), 1) % CY)


def spread_map(weight, weight_dim):
    spread = spread_matrix().astype(BF)
    tall = dot(spread, weight, 0, weight_dim).astype(BF)
    return (dot(tall, spread) * same_cell(C * CY)).astype(BF)


def flat_cells(values):
    return jnp.concatenate([values[x] for x in range(CX)], axis=1)


def pack_lines(cross, bias):
    picks = spread_matrix()
    exact = lax.Precision.HIGHEST
    point = dot(dot(picks, cross * same_cell(C * CY), 1, 0, exact), picks, 1, 1, exact)
    total = dot(bias, picks, 1, 1, exact)[:1]
    rows = jnp.concatenate([point, total], axis=0)
    rows = jnp.concatenate([rows, jnp.zeros((C + 1, 128 - C), F32)], axis=1)
    packed = []
    for r in range(4):
        line = jnp.zeros((1, 128), F32)
        for q in range(6):
            if r * 6 + q <= C:
                row = rows[r * 6 + q : r * 6 + q + 1]
                line = line + (pltpu.roll(row, q * C, 1) if q > 0 else row)
        packed.append(line)
    return jnp.concatenate(packed, axis=0)


def cells_kernel(
    lines,
    depth,
    field,
    cotangent,
    weight,
    bias,
    out,
    sums,
    slope_out,
    field_to,
    field_out,
    semaphores,
):
    matrix = depth_matrix(depth[...])
    mixing = spread_map(weight[...], 1)
    shift = dot(spread_matrix(), bias[...], 0, 1, lax.Precision.HIGHEST)
    fields = flat_cells(field)
    ones = jnp.ones((8, CX * ZT), BF)
    stores, cross, total = [], [], []
    for group in range(GROUPS):
        rows = lines[:, group * 48 : group * 48 + 48, :].reshape(N * 48, 128)
        span = rows_of(group, 32)
        pointwise = dot(mixing[span], fields) + shift[span]
        pre = dot(rows, matrix, 0, 0) + wide_to_columns(pointwise)
        phi = 0.5 * (1.0 + lax.erf(pre * 0.7071067811865476))
        field_out[group] = to_cells(pre * phi).astype(BF)
        slope = phi + pre * jnp.exp(-0.5 * pre * pre) * 0.3989422804014327
        slope = slope * to_columns(cotangent[:, span, :])
        pair = (field_out.at[group], field_to.at[:, span, :])
        stores += start_copies([pair], semaphores, group)
        slopes = to_cells(slope).astype(BF)
        slope_out[:, span, :] = slopes
        spectrum = dot(matrix, slope.astype(BF), 1, 1)
        out[:, group * 48 : group * 48 + 48, :] = spectrum.astype(BF).reshape(N, 48, 128)
        slopes = flat_cells(slopes)
        cross.append(dot(fields, slopes, 1, 1))
        total.append(dot(ones, slopes, 1, 1))
    cross = jnp.concatenate(cross, axis=1)
    total = jnp.concatenate(total, axis=1)
    sums[...] = pack_sums(pack_lines(cross, total))
    for store in stores:
        store.wait()


def last_kernel(
    lines,
    depth,
    slope,
    weight,
    coef,
    dual,
    point_out,
    bias_out,
    field_to,
    weight_to,
    field_out,
    weight_out,
    semaphores,
):
    stores = []
    step = WEIGHTS // GROUPS
    for group in range(GROUPS):
        for k in range(4):
            weight_gradient(coef, dual, group * 4 + k, weight_out)
        pair = (weight_out.at[rows_of(group, step)], weight_to.at[rows_of(group, step)])
        stores += start_copies([pair], semaphores, group)
    tails = jnp.sum(lines[:, ROWS:, :].astype(F32), axis=0)
    sums = (tails[:4] + tails[4:8]) * (NX * NY * ZT) ** -0.5
    for r in range(4):
        for q in range(6):
            index = r * 6 + q
            if index <= C:
                row = sums[r : r + 1]
                row = pltpu.roll(row, 128 - q * C, 1) if q > 0 else row
                if index < C:
                    point_out[index : index + 1, :] = row[:, :C]
                else:
                    bias_out[...] = row[:, :C]
    mixing = spread_map(weight[...], 0)
    slopes = flat_cells(slope)
    matrix = depth_matrix(depth[...])
    for group in range(GROUPS):
        rows = lines[:, group * 48 : group * 48 + 48, :].reshape(N * 48, 128)
        span = rows_of(group, 32)
        pointwise = wide_to_cells(dot(mixing[span], slopes))
        field_out[group] = (to_cells(dot(rows, matrix, 0, 0)) + pointwise).astype(BF)
        pair = (field_out.at[group], field_to.at[:, span, :])
        stores += start_copies([pair], semaphores, GROUPS + group)
    for store in stores:
        store.wait()


def exchange(values, axis):
    return lax.all_to_all(values, axis, split_axis=0, concat_axis=0, tiled=True)


def body(field_in, point_weight, point_bias, spec_weight, out_cotangent):
    cells = (CX, C * CY, ZT)
    line_message = shaped((N, ROWS, 128), BF)
    mode_message = shaped((N, 24, 128), BF)
    mode_lines = shaped((3, 144, KY), F32)
    group_cells = VMEM((GROUPS, CX, 4 * CY, ZT), BF)
    wide_weights = VMEM((WEIGHTS, KY), F32)
    field = field_in.transpose(0, 2, 1, 3).reshape(cells)
    cotangent = out_cotangent.transpose(0, 2, 1, 3).reshape(cells)
    weights = spec_weight.transpose(1, 2, 4, 3, 0).reshape(WEIGHTS, KY)

    message = call(spectrum_kernel, line_message, name="spectrum")(field, DEPTH_IN)
    message = exchange(message, "gx")
    message = call(x_analysis_kernel, mode_message, name="x_analysis")(message, X_IN)
    message = exchange(message, "gy")
    message, coef = call(
        product_kernel, (mode_message, mode_lines), scratch=[wide_weights], name="product"
    )(message, weights, Y_ALL)
    message = exchange(message, "gy")
    message = call(x_synthesis_kernel, line_message, name="x_synthesis")(message, X_MID)
    message = exchange(message, "gx")
    message, sums, slope, output_field = call(
        cells_kernel,
        (line_message, shaped((8, 128), F32), shaped(cells, BF), shaped(cells, BF)),
        [VMEM] * 6,
        [VMEM, VMEM, VMEM, HBM],
        [group_cells, DMA((GROUPS,))],
        "cells",
    )(message, DEPTH_MID, field, cotangent, point_weight, point_bias.reshape(1, C))
    message = exchange(message, "gx")
    message = call(x_analysis_kernel, mode_message, name="x_analysis_back")(message, X_MID)
    message = exchange(message, "gy")
    message, dual = call(
        back_kernel,
        (shaped((N, 32, 128), BF), mode_lines),
        scratch=[wide_weights],
        name="back",
    )(message, weights, sums, Y_ALL)
    message = exchange(message, "gy")
    message = call(
        x_synthesis_sums_kernel, shaped((N, 256, 128), BF), name="x_synthesis_back"
    )(message, X_IN)
    message = exchange(message, "gx")
    grad_point, grad_bias, grad_in, weight_grad = call(
        last_kernel,
        (
            shaped((C, C), F32),
            shaped((1, C), F32),
            shaped(cells, BF),
            shaped((WEIGHTS, KY), F32),
        ),
        [VMEM] * 6,
        [VMEM, VMEM, HBM, HBM],
        [group_cells, wide_weights, DMA((2 * GROUPS,))],
        "last",
    )(message, DEPTH_IN, slope, point_weight, coef, dual)
    grad_spec = weight_grad.reshape(C, C, PAIRS, 2, KY).transpose(4, 0, 1, 3, 2)

    def natural(values):
        return values.reshape(CX, C, CY, ZT).transpose(0, 2, 1, 3)

    return natural(output_field), natural(grad_in), grad_spec, grad_point, grad_bias.reshape(C)


def solution(mesh):
    return jax.shard_map(
        body,
        mesh=mesh,
        in_specs=(
            P("gx", "gy", None, None),
            P(),
            P(),
            P(None, None, None, None, ("gx", "gy")),
            P("gx", "gy", None, None),
        ),
        out_specs=(
            P("gx", "gy", None, None),
            P("gx", "gy", None, None),
            P(None, None, None, None, ("gx", "gy")),
            P(),
            P(),
        ),
        check_vma=False,
    )
```

time: 182 us -> 156 us (0.86)
  blocking collectives: 70.3 us -> 134 us
  local copies, waits for them, and re-layouts: 40.8 us -> 2.18 us
  waiting for transfers between devices: 25.5 us -> 0 us
  starting transfers between devices: 23.4 us -> 0 us
  other arithmetic: 2.77 us -> 0 us
    all_to_all x4 -> x8, blocking collectives: 70.3 us -> 134 us  [exchange(): return lax.all_to_all(values, axis, split_axis=0, concat_axis=0, tiled=True)]
    all_to_all x4 -> x0, waiting for transfers between devices: 25.5 us -> none  [exchange(): return lax.all_to_all(values, axis, split_axis=0, concat_axis=0, tiled=True)]
    unnamed x71 -> x24, local copies, waits for them, and re-layouts: 26.1 us -> 2.18 us
    all_to_all x4 -> x0, starting transfers between devices: 23.4 us -> none  [exchange(): return lax.all_to_all(values, axis, split_axis=0, concat_axis=0, tiled=True)]
    convert_element_type x2 -> x0, local copies, waits for them, and re-layouts: 8.08 us -> none  [body(): spec_weight.transpose(3, 1, 2, 4, 0).reshape(2, C, C, LINE).astype(F32)]
    reshape x1 -> x0, local copies, waits for them, and re-layouts: 4.46 us -> none  [body(): grad_spec = weight_grad.reshape(2, C, C, PAIRS, KY).transpose(4, 1, 2, 0, 3)]
    convert_element_type x1 -> x0, other arithmetic: 2.77 us -> none  [body(): spec_weight.transpose(3, 1, 2, 4, 0).reshape(2, C, C, LINE).astype(F32)]
    pallas_call x9 -> x6, Pallas kernels: 12.4 us -> 14.9 us  [the longest x1 5.02 us: body(): call(cells_kernel, (line_message, shaped((8, 128), F32), shaped(cells, BF...]
  transfers between devices with their start and end apart: 4 -> 0, of which waited for: 3 -> 0; matrix products, arithmetic and copies ran while one was open for 13% -> 0% of each run, Pallas kernels for 1% -> 0%
where the time goes in v1:
time: 156 us
  blocking collectives  134 us (86%)
  Pallas kernels  18.5 us (12%)
  local copies, waits for them, and re-layouts  2.18 us (1%)
    all_to_all x8, blocking collectives, exchange(): return lax.all_to_all(values, axis, split_axis=0, concat_axis=0, tiled=True)  134 us
    pallas_call x1, Pallas kernels, body(): call(cells_kernel, (line_message, shaped((8, 128), F32), shaped(cells, BF...  5.02 us
    pallas_call x1, Pallas kernels, body(): call(last_kernel, (shaped((C, C), F32), shaped((1, C), F32), shaped(cells...  3.62 us

profile of v1, /device:TPU:1, one launch (start us, length us, event | category | flops | bytes accessed | tf_op | source)
XLA Modules:
  0.0 155.9 jit_solution(10905979401738544115)
XLA Ops:
  0.6 0.0 copy-start
  0.6 0.0 copy-start.1
  0.7 1.2 copy-done.1
  1.9 0.9 copy-done.5
  2.8 1.2 spectrum.1
  4.0 22.9 %all_to_all.40.lines = bf16[16,240,128]{2,1,0:T(8,128)(2,1)S(1)} all-to-all(bf16[16,240,128]{2,1,0:T(8,128)(2,1)S(1)} %spectrum.1), channel_id=1, replica_groups=mesh['gx'=16,'gy'=16] {'gx'}, dimensions={0} | all-to-all | bytes 1966080 | tf_op jit(solution)/shard_map/all_to_all | solution.py:483
  26.9 0.0 copy-done.4
  27.0 0.0 copy-start.10
  27.0 0.0 copy-start.11
  27.0 1.5 x_analysis.1
  28.5 18.6 %all_to_all.41.lines = bf16[16,24,128]{2,1,0:T(8,128)(2,1)S(1)} all-to-all(bf16[16,24,128]{2,1,0:T(8,128)(2,1)S(1)} %x_analysis.1), channel_id=1, replica_groups=mesh['gx'=16,'gy'=16] {'gy'}, dimensions={0} | all-to-all | bytes 196608 | tf_op jit(solution)/shard_map/all_to_all | solution.py:483
  47.1 0.0 copy-done
  47.1 0.0 copy-done.8
  47.1 1.8 %product.1 = (bf16[16,24,128]{2,1,0:T(8,128)(2,1)S(1)}, f32[3,144,24]{2,1,0:T(8,128)S(1)}) custom-call(bf16[16,24,128]{2,1,0:T(8,128)(2,1)S(1)} %all_to_all.41.lines, bf16[7200,24]{1,0:T(8,128)(2,1)S(1)} %bitcast.20, bf16[240,128]{1,0:T(8,128)(2,1)S(1)} %copy-done.8), custom_call_target="tpu_custom_call" | custom-call | flops 100000000 | bytes 4000000 | tf_op jit(solution)/shard_map/product/pallas_call | solution.py:501
  48.8 10.9 %all_to_all.42.modes = bf16[16,24,128]{2,1,0:T(8,128)(2,1)S(1)} all-to-all(bf16[16,24,128]{2,1,0:T(8,128)(2,1)S(1)} %get-tuple-element.17), channel_id=1, replica_groups=mesh['gx'=16,'gy'=16] {'gy'}, dimensions={0} | all-to-all | bytes 196608 | tf_op jit(solution)/shard_map/all_to_all | solution.py:483
  59.7 0.0 copy-done.3
  59.7 1.0 x_synthesis.1
  60.7 18.8 %all_to_all.43.lines = bf16[16,240,128]{2,1,0:T(8,128)(2,1)S(1)} all-to-all(bf16[16,240,128]{2,1,0:T(8,128)(2,1)S(1)} %x_synthesis.1), channel_id=1, replica_groups=mesh['gx'=16,'gy'=16] {'gx'}, dimensions={0} | all-to-all | bytes 1966080 | tf_op jit(solution)/shard_map/all_to_all | solution.py:483
  79.5 0.0 copy-done.2
  79.5 0.0 copy-done.7
  79.5 0.0 copy-done.9
  79.5 0.0 copy-done.10
  79.5 5.0 %cells.1 = (bf16[16,240,128]{2,1,0:T(8,128)(2,1)S(1)}, f32[8,128]{1,0:T(8,128)S(1)}, bf16[16,160,128]{2,1,0:T(8,128)(2,1)S(1)}, bf16[16,160,128]{2,1,0:T(8,128)(2,1)}) custom-call(bf16[16,240,128]{2,1,0:T(8,128)(2,1)S(1)} %all_to_all.43.lines, bf16[32,24,128]{2,1,0:T(8,128)(2,1)S(1)} %copy-done.9, bf16[16,160,128]{2,1,0:T(8,128)(2,1)S(1)} %bitcast.23, ...), custom_call_target="tpu_custom_call" | custom-call | flops 100000000 | bytes 4000000 | tf_op jit(solution)/shard_map/cells/pallas_call | solution.py:507
  84.5 18.2 %all_to_all.44.lines = bf16[16,240,128]{2,1,0:T(8,128)(2,1)S(1)} all-to-all(bf16[16,240,128]{2,1,0:T(8,128)(2,1)S(1)} %get-tuple-element.19), channel_id=1, replica_groups=mesh['gx'=16,'gy'=16] {'gx'}, dimensions={0} | all-to-all | bytes 1966080 | tf_op jit(solution)/shard_map/all_to_all | solution.py:483
  102.7 1.5 x_analysis_back.1
  104.2 13.1 %all_to_all.45.lines = bf16[16,24,128]{2,1,0:T(8,128)(2,1)S(1)} all-to-all(bf16[16,24,128]{2,1,0:T(8,128)(2,1)S(1)} %x_analysis_back.1), channel_id=1, replica_groups=mesh['gx'=16,'gy'=16] {'gy'}, dimensions={0} | all-to-all | bytes 196608 | tf_op jit(solution)/shard_map/all_to_all | solution.py:483
  117.2 2.1 %back.1 = (bf16[16,32,128]{2,1,0:T(8,128)(2,1)S(1)}, f32[3,144,24]{2,1,0:T(8,128)S(1)}) custom-call(bf16[16,24,128]{2,1,0:T(8,128)(2,1)S(1)} %all_to_all.45.lines, bf16[7200,24]{1,0:T(8,128)(2,1)S(1)} %bitcast.21, f32[8,128]{1,0:T(8,128)S(1)} %get-tuple-element.20.sums, bf16[240,128]{1,0:T(8,128)(2,1)S(1)} %copy-done.8), custom_call_target="tpu_custom_call" | custom-call | flops 100000000 | bytes 4000000 | tf_op jit(solution)/shard_map/back/pallas_call | solution.py:518
  119.3 11.7 %all_to_all.46.modes = bf16[16,32,128]{2,1,0:T(8,128)(2,1)S(1)} all-to-all(bf16[16,32,128]{2,1,0:T(8,128)(2,1)S(1)} %get-tuple-element.21), channel_id=1, replica_groups=mesh['gx'=16,'gy'=16] {'gy'}, dimensions={0} | all-to-all | bytes 262144 | tf_op jit(solution)/shard_map/all_to_all | solution.py:483
  131.0 1.0 x_synthesis_back.1
  132.0 20.0 %all_to_all.47.lines = bf16[16,256,128]{2,1,0:T(8,128)(2,1)S(1)} all-to-all(bf16[16,256,128]{2,1,0:T(8,128)(2,1)S(1)} %x_synthesis_back.1), channel_id=1, replica_groups=mesh['gx'=16,'gy'=16] {'gx'}, dimensions={0} | all-to-all | bytes 2097152 | tf_op jit(solution)/shard_map/all_to_all | solution.py:483
  152.1 0.0 copy-done.6
  152.1 3.6 %last.1 = (f32[20,20]{1,0:T(8,128)}, f32[1,20]{1,0:T(1,128)}, bf16[16,160,128]{2,1,0:T(8,128)(2,1)}, f32[7200,24]{1,0:T(8,128)}) custom-call(bf16[16,256,128]{2,1,0:T(8,128)(2,1)S(1)} %all_to_all.47.lines, bf16[32,24,128]{2,1,0:T(8,128)(2,1)S(1)} %copy-done.6, bf16[16,160,128]{2,1,0:T(8,128)(2,1)S(1)} %get-tuple-element.22.slope, ...), custom_call_target="tpu_custom_call" | custom-call | flops 100000000 | bytes 4000000 | tf_op jit(solution)/shard_map/last/pallas_call | solution.py:529
  (9 shorter events, 0.0 us)
Async XLA Ops:
  0.6 46.4 %copy-start = (bf16[24,20,20,2,9]{0,3,4,2,1:T(2,128)(2,1)S(1)}, bf16[24,20,20,2,9]{0,3,4,2,1:T(2,128)(2,1)}, u32[]{:S(2)}) copy-start(bf16[24,20,20,2,9]{0,3,4,2,1:T(2,128)(2,1)} %param.13) | copy-start | bytes 1036804
  0.6 1.2 copy-start.1
  1.9 0.9 copy-start.5
  2.8 24.2 %copy-start.4 = (bf16[48,2048]{1,0:T(8,128)(2,1)S(1)}, bf16[48,2048]{1,0:T(8,128)(2,1)}, u32[]{:S(2)}) copy-start(bf16[48,2048]{1,0:T(8,128)(2,1)} %constant.11.clone.table) | copy-start | bytes 589828
  2.8 44.3 %copy-start.8 = (bf16[240,128]{1,0:T(8,128)(2,1)S(1)}, bf16[240,128]{1,0:T(8,128)(2,1)}, u32[]{:S(2)}) copy-start(bf16[240,128]{1,0:T(8,128)(2,1)} %constant.12.clone.tables) | copy-start | bytes 184324
  2.8 56.9 %copy-start.3 = (bf16[48,2048]{1,0:T(8,128)(2,1)S(1)}, bf16[48,2048]{1,0:T(8,128)(2,1)}, u32[]{:S(2)}) copy-start(bf16[48,2048]{1,0:T(8,128)(2,1)} %constant.13.clone.table) | copy-start | bytes 589828
  27.0 52.5 %copy-start.2 = (bf16[16,8,20,128]{3,1,2,0:T(8,128)(2,1)S(1)}, bf16[16,8,20,128]{3,1,2,0:T(8,128)(2,1)}, u32[]{:S(2)}) copy-start(bf16[16,8,20,128]{3,1,2,0:T(8,128)(2,1)} %param.10) | copy-start | bytes 1966084
  27.0 52.5 %copy-start.7 = (bf16[16,8,20,128]{3,1,2,0:T(8,128)(2,1)S(1)}, bf16[16,8,20,128]{3,1,2,0:T(8,128)(2,1)}, u32[]{:S(2)}) copy-start(bf16[16,8,20,128]{3,1,2,0:T(8,128)(2,1)} %param.14) | copy-start | bytes 1966084
  27.0 52.5 %copy-start.9 = (bf16[32,24,128]{2,1,0:T(8,128)(2,1)S(1)}, bf16[32,24,128]{2,1,0:T(8,128)(2,1)}, u32[]{:S(2)}) copy-start(bf16[32,24,128]{2,1,0:T(8,128)(2,1)} %constant.14.clone.depth) | copy-start | bytes 589828
  27.0 52.5 %copy-start.10 = (bf16[20,20]{1,0:T(8,128)(2,1)S(1)}, bf16[20,20]{1,0:T(8,128)(2,1)}, u32[]{:S(2)}) copy-start(bf16[20,20]{1,0:T(8,128)(2,1)} %weight.3) | copy-start | bytes 2404
  27.0 52.5 %copy-start.11 = (f32[20]{0:T(128)S(1)}, f32[20]{0:T(128)}, u32[]{:S(2)}) copy-start(f32[20]{0:T(128)} %param.12) | copy-start | bytes 244
  102.7 49.4 %copy-start.6 = (bf16[32,24,128]{2,1,0:T(8,128)(2,1)S(1)}, bf16[32,24,128]{2,1,0:T(8,128)(2,1)}, u32[]{:S(2)}) copy-start(bf16[32,24,128]{2,1,0:T(8,128)(2,1)} %constant.10.clone.depth) | copy-start | bytes 589828

commit v2 on v1

--- a/solution.py
+++ b/solution.py
@@ -97,44 +97,19 @@
     )
 
 
-def call(kernel, out_shape, spaces=None, out_spaces=None, scratch=(), name=None, limit=24 * 2**20):
-    def spec(space):
-        return pl.BlockSpec(memory_space=space)
-
-    options = {}
-    if spaces is not None:
-        options["in_specs"] = [spec(space) for space in spaces]
-    if out_spaces is not None:
-        specs = [spec(space) for space in out_spaces]
-        options["out_specs"] = specs if isinstance(out_shape, (tuple, list)) else specs[0]
+def call(kernel, out_shape, scratch=(), name=None):
     return pl.pallas_call(
         kernel,
         out_shape=out_shape,
         scratch_shapes=scratch,
-        compiler_params=pltpu.CompilerParams(vmem_limit_bytes=limit),
+        compiler_params=pltpu.CompilerParams(vmem_limit_bytes=24 * 2**20),
         cost_estimate=pl.CostEstimate(flops=10**8, bytes_accessed=4 * 10**6, transcendentals=0),
         name=name,
-        **options,
     )
-
-
-VMEM = pltpu.VMEM
-HBM = pltpu.HBM
-DMA = pltpu.SemaphoreType.DMA
 
 
 def shaped(shape, dtype):
     return jax.ShapeDtypeStruct(shape, dtype)
-
-
-def start_copies(pairs, semaphores, base=0):
-    copies = [
-        pltpu.make_async_copy(source, target, semaphores.at[base + k])
-        for k, (source, target) in enumerate(pairs)
-    ]
-    for copy in copies:
-        copy.start()
-    return copies
 
 
 def rows_of(group, count):
@@ -200,12 +175,26 @@
     return jnp.stack([wide[:, x * ZT : x * ZT + ZT] for x in range(CX)], axis=0)
 
 
+def put_spectra(matrix, columns, first, out):
+    spectra = dot(matrix, jnp.concatenate(columns, axis=0), 1, 1).astype(BF)
+    for k in range(len(columns)):
+        spectrum = spectra[:, k * 128 : k * 128 + 128].reshape(N, 48, 128)
+        out[:, rows_of(first + k, 48), :] = spectrum
+
+
+BATCHES = ((0, 1), (2, 3), (4,))
+
+
 def spectrum_kernel(field, depth, out):
     matrix = depth_matrix(depth[...])
-    for group in range(GROUPS):
-        columns = to_columns(field[:, rows_of(group, 32), :]).astype(BF)
-        spectrum = dot(matrix, columns, 1, 1)
-        out[:, rows_of(group, 48), :] = spectrum.astype(BF).reshape(N, 48, 128)
+    for batch in BATCHES:
+        columns = [to_columns(field[:, rows_of(g, 32), :]).astype(BF) for g in batch]
+        put_spectra(matrix, columns, batch[0], out)
+
+
+def from_spectra(lines, matrix):
+    rows = [lines[:, rows_of(g, 48), :].reshape(N * 48, 128) for g in range(GROUPS)]
+    return dot(jnp.concatenate(rows, axis=1), matrix, 0, 0)
 
 
 def split_dot(left, right):
@@ -217,8 +206,10 @@
 def x_analysis_kernel(lines, table, out):
     plain, turned = lane_maps()
     rows = jnp.concatenate([lines[a] for a in range(N)], axis=1)
-    coef = split_dot(dot(x_matrix(table[:KX]), rows, 1, 1), plain)
-    coef = coef + split_dot(dot(x_matrix(table[KX:]), rows, 1, 1), turned)
+    matrix = jnp.concatenate([x_matrix(table[:KX]), x_matrix(table[KX:])], axis=0)
+    both = dot(matrix, rows, 1, 1)
+    half = KX * CY
+    coef = split_dot(both[:half], plain) + split_dot(both[half:], turned)
     units = [coef[:, k * 128 : k * 128 + 128].reshape(KX, CY, 128) for k in range(2)]
     out[...] = jnp.stack(units, axis=1).reshape(N, 24, 128).astype(BF)
 
@@ -387,72 +378,40 @@
 
 
 def cells_kernel(
-    lines,
-    depth,
-    field,
-    cotangent,
-    weight,
-    bias,
-    out,
-    sums,
-    slope_out,
-    field_to,
-    field_out,
-    semaphores,
+    lines, depth, field, cotangent, weight, bias, out, sums, slope_out, field_out
 ):
     matrix = depth_matrix(depth[...])
     mixing = spread_map(weight[...], 1)
     shift = dot(spread_matrix(), bias[...], 0, 1, lax.Precision.HIGHEST)
     fields = flat_cells(field)
-    ones = jnp.ones((8, CX * ZT), BF)
-    stores, cross, total = [], [], []
-    for group in range(GROUPS):
-        rows = lines[:, group * 48 : group * 48 + 48, :].reshape(N * 48, 128)
-        span = rows_of(group, 32)
-        pointwise = dot(mixing[span], fields) + shift[span]
-        pre = dot(rows, matrix, 0, 0) + wide_to_columns(pointwise)
-        phi = 0.5 * (1.0 + lax.erf(pre * 0.7071067811865476))
-        field_out[group] = to_cells(pre * phi).astype(BF)
-        slope = phi + pre * jnp.exp(-0.5 * pre * pre) * 0.3989422804014327
-        slope = slope * to_columns(cotangent[:, span, :])
-        pair = (field_out.at[group], field_to.at[:, span, :])
-        stores += start_copies([pair], semaphores, group)
-        slopes = to_cells(slope).astype(BF)
-        slope_out[:, span, :] = slopes
-        spectrum = dot(matrix, slope.astype(BF), 1, 1)
-        out[:, group * 48 : group * 48 + 48, :] = spectrum.astype(BF).reshape(N, 48, 128)
-        slopes = flat_cells(slopes)
-        cross.append(dot(fields, slopes, 1, 1))
-        total.append(dot(ones, slopes, 1, 1))
-    cross = jnp.concatenate(cross, axis=1)
-    total = jnp.concatenate(total, axis=1)
+    spectral = from_spectra(lines, matrix)
+    pointwise = dot(mixing, fields) + shift
+    slopes = []
+    for batch in BATCHES:
+        columns = []
+        for group in batch:
+            span = rows_of(group, 32)
+            pre = spectral[rows_of(group, 128)] + wide_to_columns(pointwise[span])
+            phi = 0.5 * (1.0 + lax.erf(pre * 0.7071067811865476))
+            field_out[:, span, :] = to_cells(pre * phi).astype(BF)
+            slope = phi + pre * jnp.exp(-0.5 * pre * pre) * 0.3989422804014327
+            slope = slope * to_columns(cotangent[:, span, :])
+            columns.append(slope.astype(BF))
+            slope = to_cells(slope).astype(BF)
+            slope_out[:, span, :] = slope
+            slopes.append(flat_cells(slope))
+        put_spectra(matrix, columns, batch[0], out)
+    slopes = jnp.concatenate(slopes, axis=0)
+    cross = dot(fields, slopes, 1, 1)
+    total = dot(jnp.ones((8, CX * ZT), BF), slopes, 1, 1)
     sums[...] = pack_sums(pack_lines(cross, total))
-    for store in stores:
-        store.wait()
 
 
 def last_kernel(
-    lines,
-    depth,
-    slope,
-    weight,
-    coef,
-    dual,
-    point_out,
-    bias_out,
-    field_to,
-    weight_to,
-    field_out,
-    weight_out,
-    semaphores,
+    lines, depth, slope, weight, coef, dual, point_out, bias_out, field_out, weight_out
 ):
-    stores = []
-    step = WEIGHTS // GROUPS
-    for group in range(GROUPS):
-        for k in range(4):
-            weight_gradient(coef, dual, group * 4 + k, weight_out)
-        pair = (weight_out.at[rows_of(group, step)], weight_to.at[rows_of(group, step)])
-        stores += start_copies([pair], semaphores, group)
+    for channel in range(C):
+        weight_gradient(coef, dual, channel, weight_out)
     tails = jnp.sum(lines[:, ROWS:, :].astype(F32), axis=0)
     sums = (tails[:4] + tails[4:8]) * (NX * NY * ZT) ** -0.5
     for r in range(4):
@@ -465,18 +424,12 @@
                     point_out[index : index + 1, :] = row[:, :C]
                 else:
                     bias_out[...] = row[:, :C]
-    mixing = spread_map(weight[...], 0)
-    slopes = flat_cells(slope)
-    matrix = depth_matrix(depth[...])
+    pointwise = dot(spread_map(weight[...], 0), flat_cells(slope))
+    spectral = from_spectra(lines, depth_matrix(depth[...]))
     for group in range(GROUPS):
-        rows = lines[:, group * 48 : group * 48 + 48, :].reshape(N * 48, 128)
         span = rows_of(group, 32)
-        pointwise = wide_to_cells(dot(mixing[span], slopes))
-        field_out[group] = (to_cells(dot(rows, matrix, 0, 0)) + pointwise).astype(BF)
-        pair = (field_out.at[group], field_to.at[:, span, :])
-        stores += start_copies([pair], semaphores, GROUPS + group)
-    for store in stores:
-        store.wait()
+        total = to_cells(spectral[rows_of(group, 128)]) + wide_to_cells(pointwise[span])
+        field_out[:, span, :] = total.astype(BF)
 
 
 def exchange(values, axis):
@@ -488,8 +441,7 @@
     line_message = shaped((N, ROWS, 128), BF)
     mode_message = shaped((N, 24, 128), BF)
     mode_lines = shaped((3, 144, KY), F32)
-    group_cells = VMEM((GROUPS, CX, 4 * CY, ZT), BF)
-    wide_weights = VMEM((WEIGHTS, KY), F32)
+    wide_weights = pltpu.VMEM((WEIGHTS, KY), F32)
     field = field_in.transpose(0, 2, 1, 3).reshape(cells)
     cotangent = out_cotangent.transpose(0, 2, 1, 3).reshape(cells)
     weights = spec_weight.transpose(1, 2, 4, 3, 0).reshape(WEIGHTS, KY)
@@ -507,10 +459,7 @@
     message, sums, slope, output_field = call(
         cells_kernel,
         (line_message, shaped((8, 128), F32), shaped(cells, BF), shaped(cells, BF)),
-        [VMEM] * 6,
-        [VMEM, VMEM, VMEM, HBM],
-        [group_cells, DMA((GROUPS,))],
-        "cells",
+        name="cells",
     )(message, DEPTH_MID, field, cotangent, point_weight, point_bias.reshape(1, C))
     message = exchange(message, "gx")
     message = call(x_analysis_kernel, mode_message, name="x_analysis_back")(message, X_MID)
@@ -534,10 +483,7 @@
             shaped(cells, BF),
             shaped((WEIGHTS, KY), F32),
         ),
-        [VMEM] * 6,
-        [VMEM, VMEM, HBM, HBM],
-        [group_cells, wide_weights, DMA((2 * GROUPS,))],
-        "last",
+        name="last",
     )(message, DEPTH_IN, slope, point_weight, coef, dual)
     grad_spec = weight_grad.reshape(C, C, PAIRS, 2, KY).transpose(4, 0, 1, 3, 2)
 

time: 156 us -> 152 us (0.974)
  Pallas kernels: 18.5 us -> 15 us
    pallas_call x1, Pallas kernels: 5.02 us -> 2.98 us  [body(): call(cells_kernel, (line_message, shaped((8, 128), F32), shaped(cells, BF...]
where the time goes in v2:
time: 152 us
  blocking collectives  134 us (88%)
  Pallas kernels  15 us (10%)
  local copies, waits for them, and re-layouts  2.18 us (1%)
    all_to_all x8, blocking collectives, exchange(): return lax.all_to_all(values, axis, split_axis=0, concat_axis=0, tiled=True)  134 us
    pallas_call x1, Pallas kernels, body(): call(last_kernel, (shaped((C, C), F32), shaped((1, C), F32), shaped(cells...  3.45 us

profile of v2, /device:TPU:1, one launch (start us, length us, event | category | flops | bytes accessed | tf_op | source)
XLA Modules:
  0.0 152.0 jit_solution(8487948723374835478)
XLA Ops:
  0.6 0.0 copy-start
  0.6 0.0 copy-start.1
  0.7 1.2 copy-done.1
  1.9 0.9 copy-done.5
  2.8 0.8 spectrum.1
  3.6 23.0 %all_to_all.40.lines = bf16[16,240,128]{2,1,0:T(8,128)(2,1)S(1)} all-to-all(bf16[16,240,128]{2,1,0:T(8,128)(2,1)S(1)} %spectrum.1), channel_id=1, replica_groups=mesh['gx'=16,'gy'=16] {'gx'}, dimensions={0} | all-to-all | bytes 1966080 | tf_op jit(solution)/shard_map/all_to_all | solution.py:436
  26.6 0.0 copy-done.4
  26.6 0.0 copy-start.10
  26.6 0.0 copy-start.11
  26.6 1.0 x_analysis.1
  27.6 18.6 %all_to_all.41.lines = bf16[16,24,128]{2,1,0:T(8,128)(2,1)S(1)} all-to-all(bf16[16,24,128]{2,1,0:T(8,128)(2,1)S(1)} %x_analysis.1), channel_id=1, replica_groups=mesh['gx'=16,'gy'=16] {'gy'}, dimensions={0} | all-to-all | bytes 196608 | tf_op jit(solution)/shard_map/all_to_all | solution.py:436
  46.2 0.0 copy-done
  46.2 0.0 copy-done.8
  46.2 1.8 %product.1 = (bf16[16,24,128]{2,1,0:T(8,128)(2,1)S(1)}, f32[3,144,24]{2,1,0:T(8,128)S(1)}) custom-call(bf16[16,24,128]{2,1,0:T(8,128)(2,1)S(1)} %all_to_all.41.lines, bf16[7200,24]{1,0:T(8,128)(2,1)S(1)} %bitcast.20, bf16[240,128]{1,0:T(8,128)(2,1)S(1)} %copy-done.8), custom_call_target="tpu_custom_call" | custom-call | flops 100000000 | bytes 4000000 | tf_op jit(solution)/shard_map/product/pallas_call | solution.py:453
  48.0 10.9 %all_to_all.42.modes = bf16[16,24,128]{2,1,0:T(8,128)(2,1)S(1)} all-to-all(bf16[16,24,128]{2,1,0:T(8,128)(2,1)S(1)} %get-tuple-element.17), channel_id=1, replica_groups=mesh['gx'=16,'gy'=16] {'gy'}, dimensions={0} | all-to-all | bytes 196608 | tf_op jit(solution)/shard_map/all_to_all | solution.py:436
  58.9 0.0 copy-done.3
  58.9 1.0 x_synthesis.1
  59.9 18.8 %all_to_all.43.lines = bf16[16,240,128]{2,1,0:T(8,128)(2,1)S(1)} all-to-all(bf16[16,240,128]{2,1,0:T(8,128)(2,1)S(1)} %x_synthesis.1), channel_id=1, replica_groups=mesh['gx'=16,'gy'=16] {'gx'}, dimensions={0} | all-to-all | bytes 1966080 | tf_op jit(solution)/shard_map/all_to_all | solution.py:436
  78.6 0.0 copy-done.2
  78.6 0.0 copy-done.7
  78.6 0.0 copy-done.10
  78.6 0.0 copy-done.11
  78.6 3.0 %cells.1 = (bf16[16,240,128]{2,1,0:T(8,128)(2,1)S(1)}, f32[8,128]{1,0:T(8,128)S(1)}, bf16[16,160,128]{2,1,0:T(8,128)(2,1)S(1)}, bf16[16,160,128]{2,1,0:T(8,128)(2,1)}) custom-call(bf16[16,240,128]{2,1,0:T(8,128)(2,1)S(1)} %all_to_all.43.lines, bf16[32,24,128]{2,1,0:T(8,128)(2,1)S(1)} %copy-done.9, bf16[16,160,128]{2,1,0:T(8,128)(2,1)S(1)} %bitcast.23, ...), custom_call_target="tpu_custom_call" | custom-call | flops 100000000 | bytes 4000000 | tf_op jit(solution)/shard_map/cells/pallas_call | solution.py:459
  81.6 18.2 %all_to_all.44.lines = bf16[16,240,128]{2,1,0:T(8,128)(2,1)S(1)} all-to-all(bf16[16,240,128]{2,1,0:T(8,128)(2,1)S(1)} %get-tuple-element.19), channel_id=1, replica_groups=mesh['gx'=16,'gy'=16] {'gx'}, dimensions={0} | all-to-all | bytes 1966080 | tf_op jit(solution)/shard_map/all_to_all | solution.py:436
  99.8 1.0 x_analysis_back.1
  100.8 13.1 %all_to_all.45.lines = bf16[16,24,128]{2,1,0:T(8,128)(2,1)S(1)} all-to-all(bf16[16,24,128]{2,1,0:T(8,128)(2,1)S(1)} %x_analysis_back.1), channel_id=1, replica_groups=mesh['gx'=16,'gy'=16] {'gy'}, dimensions={0} | all-to-all | bytes 196608 | tf_op jit(solution)/shard_map/all_to_all | solution.py:436
  113.9 2.1 %back.1 = (bf16[16,32,128]{2,1,0:T(8,128)(2,1)S(1)}, f32[3,144,24]{2,1,0:T(8,128)S(1)}) custom-call(bf16[16,24,128]{2,1,0:T(8,128)(2,1)S(1)} %all_to_all.45.lines, bf16[7200,24]{1,0:T(8,128)(2,1)S(1)} %bitcast.21, f32[8,128]{1,0:T(8,128)S(1)} %get-tuple-element.20.sums, bf16[240,128]{1,0:T(8,128)(2,1)S(1)} %copy-done.8), custom_call_target="tpu_custom_call" | custom-call | flops 100000000 | bytes 4000000 | tf_op jit(solution)/shard_map/back/pallas_call | solution.py:467
  115.9 11.6 %all_to_all.46.modes = bf16[16,32,128]{2,1,0:T(8,128)(2,1)S(1)} all-to-all(bf16[16,32,128]{2,1,0:T(8,128)(2,1)S(1)} %get-tuple-element.21), channel_id=1, replica_groups=mesh['gx'=16,'gy'=16] {'gy'}, dimensions={0} | all-to-all | bytes 262144 | tf_op jit(solution)/shard_map/all_to_all | solution.py:436
  127.5 1.0 x_synthesis_back.1
  128.5 20.0 %all_to_all.47.lines = bf16[16,256,128]{2,1,0:T(8,128)(2,1)S(1)} all-to-all(bf16[16,256,128]{2,1,0:T(8,128)(2,1)S(1)} %x_synthesis_back.1), channel_id=1, replica_groups=mesh['gx'=16,'gy'=16] {'gx'}, dimensions={0} | all-to-all | bytes 2097152 | tf_op jit(solution)/shard_map/all_to_all | solution.py:436
  148.5 0.0 copy-done.6
  148.5 3.5 %last.1 = (f32[20,20]{1,0:T(8,128)}, f32[1,20]{1,0:T(1,128)}, bf16[16,160,128]{2,1,0:T(8,128)(2,1)}, f32[7200,24]{1,0:T(8,128)}) custom-call(bf16[16,256,128]{2,1,0:T(8,128)(2,1)S(1)} %all_to_all.47.lines, bf16[32,24,128]{2,1,0:T(8,128)(2,1)S(1)} %copy-done.6, bf16[16,160,128]{2,1,0:T(8,128)(2,1)S(1)} %get-tuple-element.22.slope, ...), custom_call_target="tpu_custom_call" | custom-call | flops 100000000 | bytes 4000000 | tf_op jit(solution)/shard_map/last/pallas_call | solution.py:478
  (9 shorter events, 0.0 us)
Async XLA Ops:
  0.6 45.6 %copy-start = (bf16[24,20,20,2,9]{0,3,4,2,1:T(2,128)(2,1)S(1)}, bf16[24,20,20,2,9]{0,3,4,2,1:T(2,128)(2,1)}, u32[]{:S(2)}) copy-start(bf16[24,20,20,2,9]{0,3,4,2,1:T(2,128)(2,1)} %param.13) | copy-start | bytes 1036804
  0.6 1.2 copy-start.1
  1.9 0.9 copy-start.5
  2.8 23.8 %copy-start.4 = (bf16[48,2048]{1,0:T(8,128)(2,1)S(1)}, bf16[48,2048]{1,0:T(8,128)(2,1)}, u32[]{:S(2)}) copy-start(bf16[48,2048]{1,0:T(8,128)(2,1)} %constant.11.clone.table) | copy-start | bytes 589828
  2.8 43.4 %copy-start.8 = (bf16[240,128]{1,0:T(8,128)(2,1)S(1)}, bf16[240,128]{1,0:T(8,128)(2,1)}, u32[]{:S(2)}) copy-start(bf16[240,128]{1,0:T(8,128)(2,1)} %constant.12.clone.tables) | copy-start | bytes 184324
  2.8 56.1 %copy-start.3 = (bf16[48,2048]{1,0:T(8,128)(2,1)S(1)}, bf16[48,2048]{1,0:T(8,128)(2,1)}, u32[]{:S(2)}) copy-start(bf16[48,2048]{1,0:T(8,128)(2,1)} %constant.13.clone.table) | copy-start | bytes 589828
  26.6 52.0 %copy-start.2 = (bf16[16,8,20,128]{3,1,2,0:T(8,128)(2,1)S(1)}, bf16[16,8,20,128]{3,1,2,0:T(8,128)(2,1)}, u32[]{:S(2)}) copy-start(bf16[16,8,20,128]{3,1,2,0:T(8,128)(2,1)} %param.10) | copy-start | bytes 1966084
  26.6 52.0 %copy-start.7 = (bf16[16,8,20,128]{3,1,2,0:T(8,128)(2,1)S(1)}, bf16[16,8,20,128]{3,1,2,0:T(8,128)(2,1)}, u32[]{:S(2)}) copy-start(bf16[16,8,20,128]{3,1,2,0:T(8,128)(2,1)} %param.14) | copy-start | bytes 1966084
  26.6 52.0 %copy-start.9 = (bf16[32,24,128]{2,1,0:T(8,128)(2,1)S(1)}, bf16[32,24,128]{2,1,0:T(8,128)(2,1)}, u32[]{:S(2)}) copy-start(bf16[32,24,128]{2,1,0:T(8,128)(2,1)} %constant.14.clone.depth) | copy-start | bytes 589828
  26.6 52.0 %copy-start.10 = (bf16[20,20]{1,0:T(8,128)(2,1)S(1)}, bf16[20,20]{1,0:T(8,128)(2,1)}, u32[]{:S(2)}) copy-start(bf16[20,20]{1,0:T(8,128)(2,1)} %weight.3) | copy-start | bytes 2404
  26.6 52.0 %copy-start.11 = (f32[20]{0:T(128)S(1)}, f32[20]{0:T(128)}, u32[]{:S(2)}) copy-start(f32[20]{0:T(128)} %param.12) | copy-start | bytes 244
  99.8 48.7 %copy-start.6 = (bf16[32,24,128]{2,1,0:T(8,128)(2,1)S(1)}, bf16[32,24,128]{2,1,0:T(8,128)(2,1)}, u32[]{:S(2)}) copy-start(bf16[32,24,128]{2,1,0:T(8,128)(2,1)} %constant.10.clone.depth) | copy-start | bytes 589828

commit v3 on v2

--- a/solution.py
+++ b/solution.py
@@ -27,6 +27,7 @@
 GROUPS = C // 4
 PAIRS = 9
 WEIGHTS = C * C * PAIRS * 2
+FIRST = 0
 
 BF = jnp.bfloat16
 F32 = jnp.float32
@@ -97,14 +98,20 @@
     )
 
 
-def call(kernel, out_shape, scratch=(), name=None):
+def call(kernel, out_shape, scratch=(), name=None, spaces=None, out_spaces=None, aliases=None):
+    options = {}
+    if spaces is not None:
+        options["in_specs"] = [pl.BlockSpec(memory_space=space) for space in spaces]
+        options["out_specs"] = [pl.BlockSpec(memory_space=space) for space in out_spaces]
     return pl.pallas_call(
         kernel,
         out_shape=out_shape,
         scratch_shapes=scratch,
         compiler_params=pltpu.CompilerParams(vmem_limit_bytes=24 * 2**20),
         cost_estimate=pl.CostEstimate(flops=10**8, bytes_accessed=4 * 10**6, transcendentals=0),
+        input_output_aliases=aliases or {},
         name=name,
+        **options,
     )
 
 
@@ -234,7 +241,26 @@
         out[a] = lines[:, a * 128 : a * 128 + 128]
 
 
-def x_synthesis_sums_kernel(modes, table, out):
+def when_core(core):
+    return pl.when(lax.axis_index("gy") % 2 == core)
+
+
+def start_weight_gradient(core, coef, dual, made, target, semaphore):
+    @when_core(core)
+    def _():
+        for channel in range(C):
+            weight_gradient(coef, dual, channel, made)
+        pltpu.make_async_copy(made, target, semaphore).start()
+
+
+def end_weight_gradient(core, made, target, semaphore):
+    @when_core(core)
+    def _():
+        pltpu.make_async_copy(made, target, semaphore).wait()
+
+
+def x_synthesis_sums_kernel(modes, table, coef, dual, out, weight_to, made, semaphore):
+    start_weight_gradient(FIRST, coef, dual, made, weight_to, semaphore)
     wide = modes[...].astype(F32)
     first, second = x_modes(wide[:, :24])
     lines = x_lines(first, second, table[...])
@@ -244,6 +270,7 @@
     for a in range(N):
         out[a, :ROWS] = lines[:, a * 128 : a * 128 + 128]
         out[a, ROWS:] = tail
+    end_weight_gradient(FIRST, made, weight_to, semaphore)
 
 
 def pack_sums(values):
@@ -408,10 +435,21 @@
 
 
 def last_kernel(
-    lines, depth, slope, weight, coef, dual, point_out, bias_out, field_out, weight_out
+    lines,
+    depth,
+    slope,
+    weight,
+    coef,
+    dual,
+    _,
+    point_out,
+    bias_out,
+    field_out,
+    weight_to,
+    made,
+    semaphore,
 ):
-    for channel in range(C):
-        weight_gradient(coef, dual, channel, weight_out)
+    start_weight_gradient(1 - FIRST, coef, dual, made, weight_to, semaphore)
     tails = jnp.sum(lines[:, ROWS:, :].astype(F32), axis=0)
     sums = (tails[:4] + tails[4:8]) * (NX * NY * ZT) ** -0.5
     for r in range(4):
@@ -430,6 +468,7 @@
         span = rows_of(group, 32)
         total = to_cells(spectral[rows_of(group, 128)]) + wide_to_cells(pointwise[span])
         field_out[:, span, :] = total.astype(BF)
+    end_weight_gradient(1 - FIRST, made, weight_to, semaphore)
 
 
 def exchange(values, axis):
@@ -471,20 +510,26 @@
         name="back",
     )(message, weights, sums, Y_ALL)
     message = exchange(message, "gy")
-    message = call(
-        x_synthesis_sums_kernel, shaped((N, 256, 128), BF), name="x_synthesis_back"
-    )(message, X_IN)
+    made = [wide_weights, pltpu.SemaphoreType.DMA(())]
+    weight_shape = shaped((WEIGHTS, KY), F32)
+    message, weight_grad = call(
+        x_synthesis_sums_kernel,
+        (shaped((N, 256, 128), BF), weight_shape),
+        made,
+        "x_synthesis_back",
+        [pltpu.VMEM] * 4,
+        [pltpu.VMEM, pl.ANY],
+    )(message, X_IN, coef, dual)
     message = exchange(message, "gx")
     grad_point, grad_bias, grad_in, weight_grad = call(
         last_kernel,
-        (
-            shaped((C, C), F32),
-            shaped((1, C), F32),
-            shaped(cells, BF),
-            shaped((WEIGHTS, KY), F32),
-        ),
-        name="last",
-    )(message, DEPTH_IN, slope, point_weight, coef, dual)
+        (shaped((C, C), F32), shaped((1, C), F32), shaped(cells, BF), weight_shape),
+        made,
+        "last",
+        [pltpu.VMEM] * 6 + [pl.ANY],
+        [pltpu.VMEM] * 3 + [pl.ANY],
+        {6: 3},
+    )(message, DEPTH_IN, slope, point_weight, coef, dual, weight_grad)
     grad_spec = weight_grad.reshape(C, C, PAIRS, 2, KY).transpose(4, 0, 1, 3, 2)
 
     def natural(values):

time: 152 us -> 151 us (level)
  no operation moved by 1% of the time
where the time goes in v3:
time: 151 us; the launch traced here: 150 us
  blocking collectives  133 us (88%)
  Pallas kernels  14.7 us (10%)
  local copies, waits for them, and re-layouts  2.18 us (1%)
    all_to_all x8, blocking collectives, exchange(): return lax.all_to_all(values, axis, split_axis=0, concat_axis=0, tiled=True)  133 us
    pallas_call x1, Pallas kernels, body(): call(last_kernel, (shaped((C, C), F32), shaped((1, C), F32), shaped(cells...  3.18 us

profile of v3, /device:TPU:1, one launch (start us, length us, event | category | flops | bytes accessed | tf_op | source)
XLA Modules:
  0.0 150.2 jit_solution(3871663031390539866)
XLA Ops:
  0.6 0.0 copy-start
  0.6 0.0 copy-start.1
  0.7 1.2 copy-done.1
  1.9 0.9 copy-done.3
  2.8 0.8 spectrum.1
  3.6 23.0 %all_to_all.40.lines = bf16[16,240,128]{2,1,0:T(8,128)(2,1)S(1)} all-to-all(bf16[16,240,128]{2,1,0:T(8,128)(2,1)S(1)} %spectrum.1), channel_id=1, replica_groups=mesh['gx'=16,'gy'=16] {'gx'}, dimensions={0} | all-to-all | bytes 1966080 | tf_op jit(solution)/shard_map/all_to_all | solution.py:475
  26.6 0.0 copy-done.6
  26.6 0.0 copy-start.10
  26.6 0.0 copy-start.11
  26.6 1.0 x_analysis.1
  27.6 18.6 %all_to_all.41.lines = bf16[16,24,128]{2,1,0:T(8,128)(2,1)S(1)} all-to-all(bf16[16,24,128]{2,1,0:T(8,128)(2,1)S(1)} %x_analysis.1), channel_id=1, replica_groups=mesh['gx'=16,'gy'=16] {'gy'}, dimensions={0} | all-to-all | bytes 196608 | tf_op jit(solution)/shard_map/all_to_all | solution.py:475
  46.2 0.0 copy-done
  46.2 0.0 copy-done.8
  46.2 1.8 %product.1 = (bf16[16,24,128]{2,1,0:T(8,128)(2,1)S(1)}, f32[3,144,24]{2,1,0:T(8,128)S(1)}) custom-call(bf16[16,24,128]{2,1,0:T(8,128)(2,1)S(1)} %all_to_all.41.lines, bf16[7200,24]{1,0:T(8,128)(2,1)S(1)} %bitcast.20, bf16[240,128]{1,0:T(8,128)(2,1)S(1)} %copy-done.8), custom_call_target="tpu_custom_call" | custom-call | flops 100000000 | bytes 4000000 | tf_op jit(solution)/shard_map/product/pallas_call | solution.py:492
  48.0 10.9 %all_to_all.42.modes = bf16[16,24,128]{2,1,0:T(8,128)(2,1)S(1)} all-to-all(bf16[16,24,128]{2,1,0:T(8,128)(2,1)S(1)} %get-tuple-element.19), channel_id=1, replica_groups=mesh['gx'=16,'gy'=16] {'gy'}, dimensions={0} | all-to-all | bytes 196608 | tf_op jit(solution)/shard_map/all_to_all | solution.py:475
  58.9 0.0 copy-done.5
  58.9 1.0 x_synthesis.1
  59.9 18.8 %all_to_all.43.lines = bf16[16,240,128]{2,1,0:T(8,128)(2,1)S(1)} all-to-all(bf16[16,240,128]{2,1,0:T(8,128)(2,1)S(1)} %x_synthesis.1), channel_id=1, replica_groups=mesh['gx'=16,'gy'=16] {'gx'}, dimensions={0} | all-to-all | bytes 1966080 | tf_op jit(solution)/shard_map/all_to_all | solution.py:475
  78.7 0.0 copy-done.2
  78.7 0.0 copy-done.7
  78.7 0.0 copy-done.9
  78.7 0.0 copy-done.10
  78.7 0.0 copy-done.11
  78.7 3.0 %cells.1 = (bf16[16,240,128]{2,1,0:T(8,128)(2,1)S(1)}, f32[8,128]{1,0:T(8,128)S(1)}, bf16[16,160,128]{2,1,0:T(8,128)(2,1)S(1)}, bf16[16,160,128]{2,1,0:T(8,128)(2,1)}) custom-call(bf16[16,240,128]{2,1,0:T(8,128)(2,1)S(1)} %all_to_all.43.lines, bf16[32,24,128]{2,1,0:T(8,128)(2,1)S(1)} %copy-done.9, bf16[16,160,128]{2,1,0:T(8,128)(2,1)S(1)} %bitcast.23, ...), custom_call_target="tpu_custom_call" | custom-call | flops 100000000 | bytes 4000000 | tf_op jit(solution)/shard_map/cells/pallas_call | solution.py:498
  81.7 18.2 %all_to_all.44.lines = bf16[16,240,128]{2,1,0:T(8,128)(2,1)S(1)} all-to-all(bf16[16,240,128]{2,1,0:T(8,128)(2,1)S(1)} %get-tuple-element.21), channel_id=1, replica_groups=mesh['gx'=16,'gy'=16] {'gx'}, dimensions={0} | all-to-all | bytes 1966080 | tf_op jit(solution)/shard_map/all_to_all | solution.py:475
  99.8 1.0 x_analysis_back.1
  100.8 13.1 %all_to_all.45.lines = bf16[16,24,128]{2,1,0:T(8,128)(2,1)S(1)} all-to-all(bf16[16,24,128]{2,1,0:T(8,128)(2,1)S(1)} %x_analysis_back.1), channel_id=1, replica_groups=mesh['gx'=16,'gy'=16] {'gy'}, dimensions={0} | all-to-all | bytes 196608 | tf_op jit(solution)/shard_map/all_to_all | solution.py:475
  113.9 2.0 %back.1 = (bf16[16,32,128]{2,1,0:T(8,128)(2,1)S(1)}, f32[3,144,24]{2,1,0:T(8,128)S(1)}) custom-call(bf16[16,24,128]{2,1,0:T(8,128)(2,1)S(1)} %all_to_all.45.lines, bf16[7200,24]{1,0:T(8,128)(2,1)S(1)} %bitcast.21, f32[8,128]{1,0:T(8,128)S(1)} %get-tuple-element.22.sums, bf16[240,128]{1,0:T(8,128)(2,1)S(1)} %copy-done.8), custom_call_target="tpu_custom_call" | custom-call | flops 100000000 | bytes 4000000 | tf_op jit(solution)/shard_map/back/pallas_call | solution.py:506
  115.9 11.6 %all_to_all.46.modes = bf16[16,32,128]{2,1,0:T(8,128)(2,1)S(1)} all-to-all(bf16[16,32,128]{2,1,0:T(8,128)(2,1)S(1)} %get-tuple-element.23), channel_id=1, replica_groups=mesh['gx'=16,'gy'=16] {'gy'}, dimensions={0} | all-to-all | bytes 262144 | tf_op jit(solution)/shard_map/all_to_all | solution.py:475
  127.5 1.0 x_synthesis_back.1
  128.5 18.5 %all_to_all.47.lines = bf16[16,256,128]{2,1,0:T(8,128)(2,1)S(1)} all-to-all(bf16[16,256,128]{2,1,0:T(8,128)(2,1)S(1)} %get-tuple-element.26), channel_id=1, replica_groups=mesh['gx'=16,'gy'=16] {'gx'}, dimensions={0} | all-to-all | bytes 2097152 | tf_op jit(solution)/shard_map/all_to_all | solution.py:475
  147.0 3.2 %last.1 = (f32[20,20]{1,0:T(8,128)}, f32[1,20]{1,0:T(1,128)}, bf16[16,160,128]{2,1,0:T(8,128)(2,1)}, f32[7200,24]{1,0:T(8,128)}) custom-call(bf16[16,256,128]{2,1,0:T(8,128)(2,1)S(1)} %all_to_all.47.lines, bf16[32,24,128]{2,1,0:T(8,128)(2,1)S(1)} %copy-done.4, bf16[16,160,128]{2,1,0:T(8,128)(2,1)S(1)} %get-tuple-element.27.slope, ...), custom_call_target="tpu_custom_call", output_to_operand_aliasing={{3}: (6, {})} | custom-call | flops 100000000 | bytes 4000000 | tf_op jit(solution)/shard_map/last/pallas_call | solution.py:524
  (9 shorter events, 0.0 us)
Async XLA Ops:
  0.6 45.6 %copy-start = (bf16[24,20,20,2,9]{0,3,4,2,1:T(2,128)(2,1)S(1)}, bf16[24,20,20,2,9]{0,3,4,2,1:T(2,128)(2,1)}, u32[]{:S(2)}) copy-start(bf16[24,20,20,2,9]{0,3,4,2,1:T(2,128)(2,1)} %param.13) | copy-start | bytes 1036804
  0.6 1.2 copy-start.1
  1.9 0.9 copy-start.3
  2.8 23.8 %copy-start.6 = (bf16[48,2048]{1,0:T(8,128)(2,1)S(1)}, bf16[48,2048]{1,0:T(8,128)(2,1)}, u32[]{:S(2)}) copy-start(bf16[48,2048]{1,0:T(8,128)(2,1)} %constant.11.clone.table) | copy-start | bytes 589828
  2.8 43.4 %copy-start.8 = (bf16[240,128]{1,0:T(8,128)(2,1)S(1)}, bf16[240,128]{1,0:T(8,128)(2,1)}, u32[]{:S(2)}) copy-start(bf16[240,128]{1,0:T(8,128)(2,1)} %constant.12.clone.tables) | copy-start | bytes 184324
  2.8 56.1 %copy-start.5 = (bf16[48,2048]{1,0:T(8,128)(2,1)S(1)}, bf16[48,2048]{1,0:T(8,128)(2,1)}, u32[]{:S(2)}) copy-start(bf16[48,2048]{1,0:T(8,128)(2,1)} %constant.13.clone.table) | copy-start | bytes 589828
  26.6 52.1 %copy-start.2 = (bf16[16,8,20,128]{3,1,2,0:T(8,128)(2,1)S(1)}, bf16[16,8,20,128]{3,1,2,0:T(8,128)(2,1)}, u32[]{:S(2)}) copy-start(bf16[16,8,20,128]{3,1,2,0:T(8,128)(2,1)} %param.10) | copy-start | bytes 1966084
  26.6 52.1 %copy-start.7 = (bf16[16,8,20,128]{3,1,2,0:T(8,128)(2,1)S(1)}, bf16[16,8,20,128]{3,1,2,0:T(8,128)(2,1)}, u32[]{:S(2)}) copy-start(bf16[16,8,20,128]{3,1,2,0:T(8,128)(2,1)} %param.14) | copy-start | bytes 1966084
  26.6 52.1 %copy-start.9 = (bf16[32,24,128]{2,1,0:T(8,128)(2,1)S(1)}, bf16[32,24,128]{2,1,0:T(8,128)(2,1)}, u32[]{:S(2)}) copy-start(bf16[32,24,128]{2,1,0:T(8,128)(2,1)} %constant.14.clone.depth) | copy-start | bytes 589828
  26.6 52.1 %copy-start.10 = (bf16[20,20]{1,0:T(8,128)(2,1)S(1)}, bf16[20,20]{1,0:T(8,128)(2,1)}, u32[]{:S(2)}) copy-start(bf16[20,20]{1,0:T(8,128)(2,1)} %weight.3) | copy-start | bytes 2404
  26.6 52.1 %copy-start.11 = (f32[20]{0:T(128)S(1)}, f32[20]{0:T(128)}, u32[]{:S(2)}) copy-start(f32[20]{0:T(128)} %param.12) | copy-start | bytes 244
  99.8 47.2 %copy-start.4 = (bf16[32,24,128]{2,1,0:T(8,128)(2,1)S(1)}, bf16[32,24,128]{2,1,0:T(8,128)(2,1)}, u32[]{:S(2)}) copy-start(bf16[32,24,128]{2,1,0:T(8,128)(2,1)} %constant.10.clone.depth) | copy-start | bytes 589828

commit v4 on v3

--- a/solution.py
+++ b/solution.py
@@ -141,7 +141,7 @@
 def x_matrix(rows):
     size = rows.shape[1]
     same = ones_where(iota((1, CY, size), 1) == iota((1, CY, size), 2) % CY)
-    wide = rows.astype(F32).reshape(KX, 1, size) * same
+    wide = rows.reshape(KX, 1, size) * same
     return wide.reshape(KX * CY, size).astype(BF)
 
 
@@ -213,6 +213,7 @@
 def x_analysis_kernel(lines, table, out):
     plain, turned = lane_maps()
     rows = jnp.concatenate([lines[a] for a in range(N)], axis=1)
+    table = table[...].astype(F32)
     matrix = jnp.concatenate([x_matrix(table[:KX]), x_matrix(table[KX:])], axis=0)
     both = dot(matrix, rows, 1, 1)
     half = KX * CY
@@ -230,6 +231,7 @@
 
 
 def x_lines(first, second, table):
+    table = table.astype(F32)
     lines = dot(first, x_matrix(table[:KX])) + dot(second, x_matrix(table[KX:]))
     return lines.astype(BF)
 

time: 151 us -> 151 us (level)
  no operation moved by 1% of the time
where the time goes in v4:
time: 151 us; the launch traced here: 150 us
  blocking collectives  133 us (88%)
  Pallas kernels  14.7 us (10%)
  local copies, waits for them, and re-layouts  2.18 us (1%)
    all_to_all x8, blocking collectives, exchange(): return lax.all_to_all(values, axis, split_axis=0, concat_axis=0, tiled=True)  133 us
    pallas_call x1, Pallas kernels, body(): call(last_kernel, (shaped((C, C), F32), shaped((1, C), F32), shaped(cells...  3.18 us

profile of v4, /device:TPU:1, one launch (start us, length us, event | category | flops | bytes accessed | tf_op | source)
XLA Modules:
  0.0 150.1 jit_solution(17713476833050510008)
XLA Ops:
  0.6 0.0 copy-start
  0.6 0.0 copy-start.1
  0.7 1.2 copy-done.1
  1.9 0.9 copy-done.3
  2.8 0.8 spectrum.1
  3.6 23.0 %all_to_all.40.lines = bf16[16,240,128]{2,1,0:T(8,128)(2,1)S(1)} all-to-all(bf16[16,240,128]{2,1,0:T(8,128)(2,1)S(1)} %spectrum.1), channel_id=1, replica_groups=mesh['gx'=16,'gy'=16] {'gx'}, dimensions={0} | all-to-all | bytes 1966080 | tf_op jit(solution)/shard_map/all_to_all | solution.py:477
  26.6 0.0 copy-done.6
  26.6 0.0 copy-start.10
  26.6 0.0 copy-start.11
  26.6 1.0 x_analysis.1
  27.6 18.6 %all_to_all.41.lines = bf16[16,24,128]{2,1,0:T(8,128)(2,1)S(1)} all-to-all(bf16[16,24,128]{2,1,0:T(8,128)(2,1)S(1)} %x_analysis.1), channel_id=1, replica_groups=mesh['gx'=16,'gy'=16] {'gy'}, dimensions={0} | all-to-all | bytes 196608 | tf_op jit(solution)/shard_map/all_to_all | solution.py:477
  46.2 0.0 copy-done
  46.2 0.0 copy-done.8
  46.2 1.8 %product.1 = (bf16[16,24,128]{2,1,0:T(8,128)(2,1)S(1)}, f32[3,144,24]{2,1,0:T(8,128)S(1)}) custom-call(bf16[16,24,128]{2,1,0:T(8,128)(2,1)S(1)} %all_to_all.41.lines, bf16[7200,24]{1,0:T(8,128)(2,1)S(1)} %bitcast.20, bf16[240,128]{1,0:T(8,128)(2,1)S(1)} %copy-done.8), custom_call_target="tpu_custom_call" | custom-call | flops 100000000 | bytes 4000000 | tf_op jit(solution)/shard_map/product/pallas_call | solution.py:494
  48.0 10.9 %all_to_all.42.modes = bf16[16,24,128]{2,1,0:T(8,128)(2,1)S(1)} all-to-all(bf16[16,24,128]{2,1,0:T(8,128)(2,1)S(1)} %get-tuple-element.19), channel_id=1, replica_groups=mesh['gx'=16,'gy'=16] {'gy'}, dimensions={0} | all-to-all | bytes 196608 | tf_op jit(solution)/shard_map/all_to_all | solution.py:477
  58.9 0.0 copy-done.5
  58.9 0.9 x_synthesis.1
  59.9 18.8 %all_to_all.43.lines = bf16[16,240,128]{2,1,0:T(8,128)(2,1)S(1)} all-to-all(bf16[16,240,128]{2,1,0:T(8,128)(2,1)S(1)} %x_synthesis.1), channel_id=1, replica_groups=mesh['gx'=16,'gy'=16] {'gx'}, dimensions={0} | all-to-all | bytes 1966080 | tf_op jit(solution)/shard_map/all_to_all | solution.py:477
  78.6 0.0 copy-done.2
  78.6 0.0 copy-done.7
  78.6 0.0 copy-done.9
  78.6 0.0 copy-done.10
  78.7 0.0 copy-done.11
  78.7 3.0 %cells.1 = (bf16[16,240,128]{2,1,0:T(8,128)(2,1)S(1)}, f32[8,128]{1,0:T(8,128)S(1)}, bf16[16,160,128]{2,1,0:T(8,128)(2,1)S(1)}, bf16[16,160,128]{2,1,0:T(8,128)(2,1)}) custom-call(bf16[16,240,128]{2,1,0:T(8,128)(2,1)S(1)} %all_to_all.43.lines, bf16[32,24,128]{2,1,0:T(8,128)(2,1)S(1)} %copy-done.9, bf16[16,160,128]{2,1,0:T(8,128)(2,1)S(1)} %bitcast.23, ...), custom_call_target="tpu_custom_call" | custom-call | flops 100000000 | bytes 4000000 | tf_op jit(solution)/shard_map/cells/pallas_call | solution.py:500
  81.6 18.2 %all_to_all.44.lines = bf16[16,240,128]{2,1,0:T(8,128)(2,1)S(1)} all-to-all(bf16[16,240,128]{2,1,0:T(8,128)(2,1)S(1)} %get-tuple-element.21), channel_id=1, replica_groups=mesh['gx'=16,'gy'=16] {'gx'}, dimensions={0} | all-to-all | bytes 1966080 | tf_op jit(solution)/shard_map/all_to_all | solution.py:477
  99.8 1.0 x_analysis_back.1
  100.8 13.1 %all_to_all.45.lines = bf16[16,24,128]{2,1,0:T(8,128)(2,1)S(1)} all-to-all(bf16[16,24,128]{2,1,0:T(8,128)(2,1)S(1)} %x_analysis_back.1), channel_id=1, replica_groups=mesh['gx'=16,'gy'=16] {'gy'}, dimensions={0} | all-to-all | bytes 196608 | tf_op jit(solution)/shard_map/all_to_all | solution.py:477
  113.9 2.0 %back.1 = (bf16[16,32,128]{2,1,0:T(8,128)(2,1)S(1)}, f32[3,144,24]{2,1,0:T(8,128)S(1)}) custom-call(bf16[16,24,128]{2,1,0:T(8,128)(2,1)S(1)} %all_to_all.45.lines, bf16[7200,24]{1,0:T(8,128)(2,1)S(1)} %bitcast.21, f32[8,128]{1,0:T(8,128)S(1)} %get-tuple-element.22.sums, bf16[240,128]{1,0:T(8,128)(2,1)S(1)} %copy-done.8), custom_call_target="tpu_custom_call" | custom-call | flops 100000000 | bytes 4000000 | tf_op jit(solution)/shard_map/back/pallas_call | solution.py:508
  115.9 11.6 %all_to_all.46.modes = bf16[16,32,128]{2,1,0:T(8,128)(2,1)S(1)} all-to-all(bf16[16,32,128]{2,1,0:T(8,128)(2,1)S(1)} %get-tuple-element.23), channel_id=1, replica_groups=mesh['gx'=16,'gy'=16] {'gy'}, dimensions={0} | all-to-all | bytes 262144 | tf_op jit(solution)/shard_map/all_to_all | solution.py:477
  127.5 1.0 x_synthesis_back.1
  128.4 18.5 %all_to_all.47.lines = bf16[16,256,128]{2,1,0:T(8,128)(2,1)S(1)} all-to-all(bf16[16,256,128]{2,1,0:T(8,128)(2,1)S(1)} %get-tuple-element.26), channel_id=1, replica_groups=mesh['gx'=16,'gy'=16] {'gx'}, dimensions={0} | all-to-all | bytes 2097152 | tf_op jit(solution)/shard_map/all_to_all | solution.py:477
  146.9 3.2 %last.1 = (f32[20,20]{1,0:T(8,128)}, f32[1,20]{1,0:T(1,128)}, bf16[16,160,128]{2,1,0:T(8,128)(2,1)}, f32[7200,24]{1,0:T(8,128)}) custom-call(bf16[16,256,128]{2,1,0:T(8,128)(2,1)S(1)} %all_to_all.47.lines, bf16[32,24,128]{2,1,0:T(8,128)(2,1)S(1)} %copy-done.4, bf16[16,160,128]{2,1,0:T(8,128)(2,1)S(1)} %get-tuple-element.27.slope, ...), custom_call_target="tpu_custom_call", output_to_operand_aliasing={{3}: (6, {})} | custom-call | flops 100000000 | bytes 4000000 | tf_op jit(solution)/shard_map/last/pallas_call | solution.py:526
  (9 shorter events, 0.0 us)
Async XLA Ops:
  0.6 45.6 %copy-start = (bf16[24,20,20,2,9]{0,3,4,2,1:T(2,128)(2,1)S(1)}, bf16[24,20,20,2,9]{0,3,4,2,1:T(2,128)(2,1)}, u32[]{:S(2)}) copy-start(bf16[24,20,20,2,9]{0,3,4,2,1:T(2,128)(2,1)} %param.13) | copy-start | bytes 1036804
  0.6 1.2 copy-start.1
  1.9 0.9 copy-start.3
  2.8 23.8 %copy-start.6 = (bf16[48,2048]{1,0:T(8,128)(2,1)S(1)}, bf16[48,2048]{1,0:T(8,128)(2,1)}, u32[]{:S(2)}) copy-start(bf16[48,2048]{1,0:T(8,128)(2,1)} %constant.11.clone.table) | copy-start | bytes 589828
  2.8 43.4 %copy-start.8 = (bf16[240,128]{1,0:T(8,128)(2,1)S(1)}, bf16[240,128]{1,0:T(8,128)(2,1)}, u32[]{:S(2)}) copy-start(bf16[240,128]{1,0:T(8,128)(2,1)} %constant.12.clone.tables) | copy-start | bytes 184324
  2.8 56.1 %copy-start.5 = (bf16[48,2048]{1,0:T(8,128)(2,1)S(1)}, bf16[48,2048]{1,0:T(8,128)(2,1)}, u32[]{:S(2)}) copy-start(bf16[48,2048]{1,0:T(8,128)(2,1)} %constant.13.clone.table) | copy-start | bytes 589828
  26.6 52.0 %copy-start.2 = (bf16[16,8,20,128]{3,1,2,0:T(8,128)(2,1)S(1)}, bf16[16,8,20,128]{3,1,2,0:T(8,128)(2,1)}, u32[]{:S(2)}) copy-start(bf16[16,8,20,128]{3,1,2,0:T(8,128)(2,1)} %param.10) | copy-start | bytes 1966084
  26.6 52.0 %copy-start.7 = (bf16[16,8,20,128]{3,1,2,0:T(8,128)(2,1)S(1)}, bf16[16,8,20,128]{3,1,2,0:T(8,128)(2,1)}, u32[]{:S(2)}) copy-start(bf16[16,8,20,128]{3,1,2,0:T(8,128)(2,1)} %param.14) | copy-start | bytes 1966084
  26.6 52.0 %copy-start.9 = (bf16[32,24,128]{2,1,0:T(8,128)(2,1)S(1)}, bf16[32,24,128]{2,1,0:T(8,128)(2,1)}, u32[]{:S(2)}) copy-start(bf16[32,24,128]{2,1,0:T(8,128)(2,1)} %constant.14.clone.depth) | copy-start | bytes 589828
  26.6 52.0 %copy-start.10 = (bf16[20,20]{1,0:T(8,128)(2,1)S(1)}, bf16[20,20]{1,0:T(8,128)(2,1)}, u32[]{:S(2)}) copy-start(bf16[20,20]{1,0:T(8,128)(2,1)} %weight.3) | copy-start | bytes 2404
  26.6 52.0 %copy-start.11 = (f32[20]{0:T(128)S(1)}, f32[20]{0:T(128)}, u32[]{:S(2)}) copy-start(f32[20]{0:T(128)} %param.12) | copy-start | bytes 244
  99.8 47.2 %copy-start.4 = (bf16[32,24,128]{2,1,0:T(8,128)(2,1)S(1)}, bf16[32,24,128]{2,1,0:T(8,128)(2,1)}, u32[]{:S(2)}) copy-start(bf16[32,24,128]{2,1,0:T(8,128)(2,1)} %constant.10.clone.depth) | copy-start | bytes 589828

commit v5 on v4

--- a/solution.py
+++ b/solution.py
@@ -314,49 +314,95 @@
     return modes[unit, pl.ds(kind * 24 + channel, 1), :]
 
 
-def load_weights(weights, wide):
-    step = WEIGHTS // 10
-    for k in range(10):
-        wide[k * step : k * step + step, :] = weights[k * step : k * step + step, :].astype(F32)
-
-
-def mix_channels(weights, modes, out_step, in_step, sign):
+FIVE = 5
+STEP = C // FIVE
+
+
+def beside(pieces):
+    empty = jnp.zeros((pieces[0].shape[0], 128 - FIVE * KY), F32)
+    return jnp.concatenate(list(pieces) + [empty], axis=1)
+
+
+def piece_of(values, q):
+    return (pltpu.roll(values, 128 - q * KY, 1) if q > 0 else values)[:, :KY]
+
+
+def pack_weights(weights, packed):
+    size = WEIGHTS // C
+    for half in range(2):
+        wide = weights[half * (WEIGHTS // 2) : (half + 1) * (WEIGHTS // 2), :].astype(F32)
+        for group in range(STEP // 2):
+            base = group * FIVE * size
+            rows = [wide[base + q * size : base + q * size + size] for q in range(FIVE)]
+            start = (half * (STEP // 2) + group) * size
+            packed[start : start + size, :] = beside(rows)
+
+
+def mix_forward(packed, modes, lanes):
+    size = WEIGHTS // C
+    empty = jnp.zeros((4, KY), F32)
     units = []
     for unit in range(3):
-        reals, imags = [], []
+        for kind in range(6):
+            starts = [kind * 24 + q for q in range(FIVE)]
+            rows = [modes[unit, pl.ds(start, STEP, stride=FIVE), :] for start in starts]
+            lanes[unit, kind * 8 : kind * 8 + STEP, :] = beside(rows)
+        parts = [[], []]
         for mode in range(3):
-            pair = unit * 3 + mode
-            real = jnp.zeros((C, KY), F32)
-            imag = jnp.zeros((C, KY), F32)
+            real = jnp.zeros((C, 128), F32)
+            imag = jnp.zeros((C, 128), F32)
+            for group in range(STEP):
+                start = group * size + 2 * (unit * 3 + mode)
+                weight_re = packed[pl.ds(start, C, stride=2 * PAIRS), :]
+                weight_im = packed[pl.ds(start + 1, C, stride=2 * PAIRS), :]
+                re = lanes[unit, pl.ds(mode * 8 + group, 1), :]
+                im = lanes[unit, pl.ds((3 + mode) * 8 + group, 1), :]
+                real = real + (weight_re * re - weight_im * im)
+                imag = imag + (weight_re * im + weight_im * re)
+            for part, total in enumerate((real, imag)):
+                pieces = [piece_of(total, q) for q in range(FIVE)]
+                parts[part] += [sum(pieces[1:], pieces[0]), empty]
+        units.append(jnp.concatenate(parts[0] + parts[1], axis=0))
+    return units
+
+
+def mix_back(packed, modes, lanes, result):
+    size = WEIGHTS // C
+    result[...] = jnp.zeros(result.shape, F32)
+    units = []
+    for unit in range(3):
+        lanes[unit] = beside([modes[unit]] * FIVE)
+        for mode in range(3):
+            real = jnp.zeros((STEP, 128), F32)
+            imag = jnp.zeros((STEP, 128), F32)
             for k in range(C):
-                start = k * in_step + 2 * pair
-                weight_re = weights[pl.ds(start, C, stride=out_step), :]
-                weight_im = weights[pl.ds(start + 1, C, stride=out_step), :]
-                re = line_of(modes, unit, mode, k)
-                im = line_of(modes, unit, 3 + mode, k)
-                real = real + (weight_re * re - sign * (weight_im * im))
-                imag = imag + (weight_re * im + sign * (weight_im * re))
-            reals.append(real)
-            imags.append(imag)
-        empty = jnp.zeros((4, KY), F32)
-        parts = [jnp.concatenate([part, empty], axis=0) for part in reals + imags]
-        units.append(jnp.concatenate(parts, axis=0))
+                start = k * 2 * PAIRS + 2 * (unit * 3 + mode)
+                weight_re = packed[pl.ds(start, STEP, stride=size), :]
+                weight_im = packed[pl.ds(start + 1, STEP, stride=size), :]
+                re = lanes[unit, pl.ds(mode * 24 + k, 1), :]
+                im = lanes[unit, pl.ds((3 + mode) * 24 + k, 1), :]
+                real = real + (weight_re * re + weight_im * im)
+                imag = imag + (weight_re * im - weight_im * re)
+            for part, total in enumerate((real, imag)):
+                for q in range(FIVE):
+                    rows = pl.ds((part * 3 + mode) * 24 + q, STEP, stride=FIVE)
+                    result[unit, rows, :] = piece_of(total, q)
+        units.append(result[unit])
     return units
 
 
-def product_kernel(lines, weights, tables, out, coef, wide):
-    load_weights(weights, wide)
+def product_kernel(lines, weights, tables, out, coef, packed, lanes):
+    pack_weights(weights, packed)
     for u, unit in enumerate(y_analysis(lines[...], tables[Y_IN], tables[PICKS])):
         coef[u] = unit
-    product = mix_channels(wide, coef, 2 * PAIRS, 2 * PAIRS * C, 1.0)
+    product = mix_forward(packed, coef, lanes)
     out[...] = y_synthesis(product, tables[Y_MID], tables[PICKS]).astype(BF)
 
 
-def back_kernel(lines, weights, sums, tables, out, dual, wide):
-    load_weights(weights, wide)
+def back_kernel(lines, packed, sums, tables, out, dual, lanes, result):
     for u, unit in enumerate(y_analysis(lines[...], tables[Y_MID], tables[PICKS])):
         dual[u] = unit
-    modes = mix_channels(wide, dual, 2 * PAIRS * C, 2 * PAIRS, -1.0)
+    modes = mix_back(packed, dual, lanes, result)
     modes = y_synthesis(modes, tables[Y_IN], tables[PICKS])
     tail = jnp.broadcast_to(sums[...].reshape(1, 8, 128), (N, 8, 128))
     out[...] = jnp.concatenate([modes, tail], axis=1).astype(BF)
@@ -491,8 +537,11 @@
     message = exchange(message, "gx")
     message = call(x_analysis_kernel, mode_message, name="x_analysis")(message, X_IN)
     message = exchange(message, "gy")
-    message, coef = call(
-        product_kernel, (mode_message, mode_lines), scratch=[wide_weights], name="product"
+    message, coef, packed = call(
+        product_kernel,
+        (mode_message, mode_lines, shaped((WEIGHTS // FIVE, 128), F32)),
+        [pltpu.VMEM((3, 48, 128), F32)],
+        "product",
     )(message, weights, Y_ALL)
     message = exchange(message, "gy")
     message = call(x_synthesis_kernel, line_message, name="x_synthesis")(message, X_MID)
@@ -508,9 +557,9 @@
     message, dual = call(
         back_kernel,
         (shaped((N, 32, 128), BF), mode_lines),
-        scratch=[wide_weights],
-        name="back",
-    )(message, weights, sums, Y_ALL)
+        [pltpu.VMEM((3, 144, 128), F32), pltpu.VMEM((3, 144, KY), F32)],
+        "back",
+    )(message, packed, sums, Y_ALL)
     message = exchange(message, "gy")
     made = [wide_weights, pltpu.SemaphoreType.DMA(())]
     weight_shape = shaped((WEIGHTS, KY), F32)

time: 151 us -> 149 us (0.987)
  no operation moved by 1% of the time
where the time goes in v5:
time: 149 us
  blocking collectives  133 us (89%)
  Pallas kernels  13.4 us (9%)
  local copies, waits for them, and re-layouts  2.05 us (1%)
    all_to_all x8, blocking collectives, exchange(): return lax.all_to_all(values, axis, split_axis=0, concat_axis=0, tiled=True)  133 us
    pallas_call x1, Pallas kernels, body(): call(last_kernel, (shaped((C, C), F32), shaped((1, C), F32), shaped(cells...  3.18 us

profile of v5, /device:TPU:1, one launch (start us, length us, event | category | flops | bytes accessed | tf_op | source)
XLA Modules:
  0.0 148.9 jit_solution(1550125497267201724)
XLA Ops:
  0.6 0.0 copy-start
  0.6 1.1 copy-done
  1.7 0.9 copy-done.3
  2.7 0.8 spectrum.1
  3.5 23.0 %all_to_all.40.lines = bf16[16,240,128]{2,1,0:T(8,128)(2,1)S(1)} all-to-all(bf16[16,240,128]{2,1,0:T(8,128)(2,1)S(1)} %spectrum.1), channel_id=1, replica_groups=mesh['gx'=16,'gy'=16] {'gx'}, dimensions={0} | all-to-all | bytes 1966080 | tf_op jit(solution)/shard_map/all_to_all | solution.py:523
  26.4 0.0 copy-done.6
  26.5 0.0 copy-start.10
  26.5 0.0 copy-start.11
  26.5 1.0 x_analysis.1
  27.5 18.6 %all_to_all.41.lines = bf16[16,24,128]{2,1,0:T(8,128)(2,1)S(1)} all-to-all(bf16[16,24,128]{2,1,0:T(8,128)(2,1)S(1)} %x_analysis.1), channel_id=1, replica_groups=mesh['gx'=16,'gy'=16] {'gy'}, dimensions={0} | all-to-all | bytes 196608 | tf_op jit(solution)/shard_map/all_to_all | solution.py:523
  46.1 0.0 copy-done.2
  46.1 0.0 copy-done.8
  46.1 1.3 product.1
  47.4 10.9 %all_to_all.42.modes = bf16[16,24,128]{2,1,0:T(8,128)(2,1)S(1)} all-to-all(bf16[16,24,128]{2,1,0:T(8,128)(2,1)S(1)} %get-tuple-element.20), channel_id=1, replica_groups=mesh['gx'=16,'gy'=16] {'gy'}, dimensions={0} | all-to-all | bytes 196608 | tf_op jit(solution)/shard_map/all_to_all | solution.py:523
  58.3 0.0 copy-done.5
  58.3 0.9 x_synthesis.1
  59.3 18.8 %all_to_all.43.lines = bf16[16,240,128]{2,1,0:T(8,128)(2,1)S(1)} all-to-all(bf16[16,240,128]{2,1,0:T(8,128)(2,1)S(1)} %x_synthesis.1), channel_id=1, replica_groups=mesh['gx'=16,'gy'=16] {'gx'}, dimensions={0} | all-to-all | bytes 1966080 | tf_op jit(solution)/shard_map/all_to_all | solution.py:523
  78.0 0.0 copy-done.1
  78.0 0.0 copy-done.7
  78.0 0.0 copy-done.9
  78.1 0.0 copy-done.10
  78.1 0.0 copy-done.11
  78.1 3.0 %cells.1 = (bf16[16,240,128]{2,1,0:T(8,128)(2,1)S(1)}, f32[8,128]{1,0:T(8,128)S(1)}, bf16[16,160,128]{2,1,0:T(8,128)(2,1)S(1)}, bf16[16,160,128]{2,1,0:T(8,128)(2,1)}) custom-call(bf16[16,240,128]{2,1,0:T(8,128)(2,1)S(1)} %all_to_all.43.lines, bf16[32,24,128]{2,1,0:T(8,128)(2,1)S(1)} %copy-done.9, bf16[16,160,128]{2,1,0:T(8,128)(2,1)S(1)} %bitcast.21, ...), custom_call_target="tpu_custom_call" | custom-call | flops 100000000 | bytes 4000000 | tf_op jit(solution)/shard_map/cells/pallas_call | solution.py:549
  81.0 18.3 %all_to_all.44.lines = bf16[16,240,128]{2,1,0:T(8,128)(2,1)S(1)} all-to-all(bf16[16,240,128]{2,1,0:T(8,128)(2,1)S(1)} %get-tuple-element.22), channel_id=1, replica_groups=mesh['gx'=16,'gy'=16] {'gx'}, dimensions={0} | all-to-all | bytes 1966080 | tf_op jit(solution)/shard_map/all_to_all | solution.py:523
  99.3 1.0 x_analysis_back.1
  100.3 13.1 %all_to_all.45.lines = bf16[16,24,128]{2,1,0:T(8,128)(2,1)S(1)} all-to-all(bf16[16,24,128]{2,1,0:T(8,128)(2,1)S(1)} %x_analysis_back.1), channel_id=1, replica_groups=mesh['gx'=16,'gy'=16] {'gy'}, dimensions={0} | all-to-all | bytes 196608 | tf_op jit(solution)/shard_map/all_to_all | solution.py:523
  113.4 1.3 back.1
  114.7 11.6 %all_to_all.46.modes = bf16[16,32,128]{2,1,0:T(8,128)(2,1)S(1)} all-to-all(bf16[16,32,128]{2,1,0:T(8,128)(2,1)S(1)} %get-tuple-element.25), channel_id=1, replica_groups=mesh['gx'=16,'gy'=16] {'gy'}, dimensions={0} | all-to-all | bytes 262144 | tf_op jit(solution)/shard_map/all_to_all | solution.py:523
  126.2 1.0 x_synthesis_back.1
  127.2 18.5 %all_to_all.47.lines = bf16[16,256,128]{2,1,0:T(8,128)(2,1)S(1)} all-to-all(bf16[16,256,128]{2,1,0:T(8,128)(2,1)S(1)} %get-tuple-element.28), channel_id=1, replica_groups=mesh['gx'=16,'gy'=16] {'gx'}, dimensions={0} | all-to-all | bytes 2097152 | tf_op jit(solution)/shard_map/all_to_all | solution.py:523
  145.7 0.0 copy-done.4
  145.7 3.2 %last.1 = (f32[20,20]{1,0:T(8,128)}, f32[1,20]{1,0:T(1,128)}, bf16[16,160,128]{2,1,0:T(8,128)(2,1)}, f32[7200,24]{1,0:T(8,128)}) custom-call(bf16[16,256,128]{2,1,0:T(8,128)(2,1)S(1)} %all_to_all.47.lines, bf16[32,24,128]{2,1,0:T(8,128)(2,1)S(1)} %copy-done.4, bf16[16,160,128]{2,1,0:T(8,128)(2,1)S(1)} %get-tuple-element.29.slope, ...), custom_call_target="tpu_custom_call", output_to_operand_aliasing={{3}: (6, {})} | custom-call | flops 100000000 | bytes 4000000 | tf_op jit(solution)/shard_map/last/pallas_call | solution.py:575
  (9 shorter events, 0.0 us)
Async XLA Ops:
  0.6 1.1 copy-start
  1.7 0.9 copy-start.3
  2.6 23.8 %copy-start.6 = (bf16[48,2048]{1,0:T(8,128)(2,1)S(1)}, bf16[48,2048]{1,0:T(8,128)(2,1)}, u32[]{:S(2)}) copy-start(bf16[48,2048]{1,0:T(8,128)(2,1)} %constant.11.clone.table) | copy-start | bytes 589828
  2.7 43.4 %copy-start.2 = (bf16[24,20,20,2,9]{0,3,4,2,1:T(2,128)(2,1)S(1)}, bf16[24,20,20,2,9]{0,3,4,2,1:T(2,128)(2,1)}, u32[]{:S(2)}) copy-start(bf16[24,20,20,2,9]{0,3,4,2,1:T(2,128)(2,1)} %param.13) | copy-start | bytes 1036804
  2.7 43.4 %copy-start.8 = (bf16[240,128]{1,0:T(8,128)(2,1)S(1)}, bf16[240,128]{1,0:T(8,128)(2,1)}, u32[]{:S(2)}) copy-start(bf16[240,128]{1,0:T(8,128)(2,1)} %constant.12.clone.tables) | copy-start | bytes 184324
  2.7 55.7 %copy-start.5 = (bf16[48,2048]{1,0:T(8,128)(2,1)S(1)}, bf16[48,2048]{1,0:T(8,128)(2,1)}, u32[]{:S(2)}) copy-start(bf16[48,2048]{1,0:T(8,128)(2,1)} %constant.13.clone.table) | copy-start | bytes 589828
  26.5 51.6 %copy-start.1 = (bf16[16,8,20,128]{3,1,2,0:T(8,128)(2,1)S(1)}, bf16[16,8,20,128]{3,1,2,0:T(8,128)(2,1)}, u32[]{:S(2)}) copy-start(bf16[16,8,20,128]{3,1,2,0:T(8,128)(2,1)} %param.10) | copy-start | bytes 1966084
  26.5 51.6 %copy-start.7 = (bf16[16,8,20,128]{3,1,2,0:T(8,128)(2,1)S(1)}, bf16[16,8,20,128]{3,1,2,0:T(8,128)(2,1)}, u32[]{:S(2)}) copy-start(bf16[16,8,20,128]{3,1,2,0:T(8,128)(2,1)} %param.14) | copy-start | bytes 1966084
  26.5 51.6 %copy-start.9 = (bf16[32,24,128]{2,1,0:T(8,128)(2,1)S(1)}, bf16[32,24,128]{2,1,0:T(8,128)(2,1)}, u32[]{:S(2)}) copy-start(bf16[32,24,128]{2,1,0:T(8,128)(2,1)} %constant.14.clone.depth) | copy-start | bytes 589828
  26.5 51.6 %copy-start.10 = (bf16[20,20]{1,0:T(8,128)(2,1)S(1)}, bf16[20,20]{1,0:T(8,128)(2,1)}, u32[]{:S(2)}) copy-start(bf16[20,20]{1,0:T(8,128)(2,1)} %weight.3) | copy-start | bytes 2404
  26.5 51.6 %copy-start.11 = (f32[20]{0:T(128)S(1)}, f32[20]{0:T(128)}, u32[]{:S(2)}) copy-start(f32[20]{0:T(128)} %param.12) | copy-start | bytes 244
  81.0 64.7 %copy-start.4 = (bf16[32,24,128]{2,1,0:T(8,128)(2,1)S(1)}, bf16[32,24,128]{2,1,0:T(8,128)(2,1)}, u32[]{:S(2)}) copy-start(bf16[32,24,128]{2,1,0:T(8,128)(2,1)} %constant.10.clone.depth) | copy-start | bytes 589828

commit v6 on v5

--- a/solution.py
+++ b/solution.py
@@ -192,8 +192,31 @@
 BATCHES = ((0, 1), (2, 3), (4,))
 
 
-def spectrum_kernel(field, depth, out):
-    matrix = depth_matrix(depth[...])
+def depth_rows_here(scale):
+    row, lane = iota((24, 1), 0), iota((1, ZT), 1)
+    mode = row % 3
+    quarter = jnp.where(row % 6 < 3, 0.0, 8.0)
+    z, t = (lane // T_SIZE).astype(F32), (lane % T_SIZE).astype(F32)
+    blocks = []
+    for block in range(2 * N):
+        jz, jt = divmod(3 * block, KT)
+        carry = mode + jt >= KT
+        jt = jnp.where(carry, mode + jt - KT, mode + jt)
+        jz = jnp.where(carry, jz + 1, jz)
+        fz = jnp.where(jz < KZ // 2, jz, jz + Z - KZ).astype(F32)
+        turns = fz * z + (jt * (Z // KT)).astype(F32) * t + quarter
+        turns = turns - 32.0 * jnp.floor(turns * (1.0 / 32.0))
+        angle = (jnp.abs(turns * 0.0625 - 1.0) - 0.5) * math.pi
+        square = angle * angle
+        wave = 1.0 + square * (-1.0 / 110.0)
+        for factor in (72.0, 42.0, 20.0, 6.0):
+            wave = 1.0 - square * (1.0 / factor) * wave
+        blocks.append(angle * wave * scale)
+    return jnp.stack(blocks, axis=0)
+
+
+def spectrum_kernel(field, out):
+    matrix = depth_matrix(depth_rows_here(ZT**-0.5))
     for batch in BATCHES:
         columns = [to_columns(field[:, rows_of(g, 32), :]).astype(BF) for g in batch]
         put_spectra(matrix, columns, batch[0], out)
@@ -533,7 +556,7 @@
     cotangent = out_cotangent.transpose(0, 2, 1, 3).reshape(cells)
     weights = spec_weight.transpose(1, 2, 4, 3, 0).reshape(WEIGHTS, KY)
 
-    message = call(spectrum_kernel, line_message, name="spectrum")(field, DEPTH_IN)
+    message = call(spectrum_kernel, line_message, name="spectrum")(field)
     message = exchange(message, "gx")
     message = call(x_analysis_kernel, mode_message, name="x_analysis")(message, X_IN)
     message = exchange(message, "gy")

time: 149 us -> 149 us (level)
  no operation moved by 1% of the time
where the time goes in v6:
time: 149 us; the launch traced here: 148 us
  blocking collectives  133 us (89%)
  Pallas kernels  13.8 us (9%)
    all_to_all x8, blocking collectives, exchange(): return lax.all_to_all(values, axis, split_axis=0, concat_axis=0, tiled=True)  133 us
    pallas_call x1, Pallas kernels, body(): call(last_kernel, (shaped((C, C), F32), shaped((1, C), F32), shaped(cells...  3.18 us

profile of v6, /device:TPU:1, one launch (start us, length us, event | category | flops | bytes accessed | tf_op | source)
XLA Modules:
  0.0 148.4 jit_solution(12675514767970263717)
XLA Ops:
  0.6 0.0 copy-start
  0.6 1.1 copy-done
  1.7 0.0 copy-start.4
  1.7 1.2 spectrum.1
  2.9 23.0 %all_to_all.40.lines = bf16[16,240,128]{2,1,0:T(8,128)(2,1)S(1)} all-to-all(bf16[16,240,128]{2,1,0:T(8,128)(2,1)S(1)} %spectrum.1), channel_id=1, replica_groups=mesh['gx'=16,'gy'=16] {'gx'}, dimensions={0} | all-to-all | bytes 1966080 | tf_op jit(solution)/shard_map/all_to_all | solution.py:546
  25.9 0.0 copy-done.4
  25.9 0.0 copy-start.9
  25.9 0.0 copy-start.10
  25.9 1.0 x_analysis.1
  27.0 18.6 %all_to_all.41.lines = bf16[16,24,128]{2,1,0:T(8,128)(2,1)S(1)} all-to-all(bf16[16,24,128]{2,1,0:T(8,128)(2,1)S(1)} %x_analysis.1), channel_id=1, replica_groups=mesh['gx'=16,'gy'=16] {'gy'}, dimensions={0} | all-to-all | bytes 196608 | tf_op jit(solution)/shard_map/all_to_all | solution.py:546
  45.5 0.0 copy-done.2
  45.5 0.0 copy-done.6
  45.5 1.3 product.1
  46.9 10.9 %all_to_all.42.modes = bf16[16,24,128]{2,1,0:T(8,128)(2,1)S(1)} all-to-all(bf16[16,24,128]{2,1,0:T(8,128)(2,1)S(1)} %get-tuple-element.20), channel_id=1, replica_groups=mesh['gx'=16,'gy'=16] {'gy'}, dimensions={0} | all-to-all | bytes 196608 | tf_op jit(solution)/shard_map/all_to_all | solution.py:546
  57.8 0.0 copy-done.3
  57.8 0.9 x_synthesis.1
  58.7 18.8 %all_to_all.43.lines = bf16[16,240,128]{2,1,0:T(8,128)(2,1)S(1)} all-to-all(bf16[16,240,128]{2,1,0:T(8,128)(2,1)S(1)} %x_synthesis.1), channel_id=1, replica_groups=mesh['gx'=16,'gy'=16] {'gx'}, dimensions={0} | all-to-all | bytes 1966080 | tf_op jit(solution)/shard_map/all_to_all | solution.py:546
  77.5 0.0 copy-done.1
  77.5 0.0 copy-done.5
  77.5 0.0 copy-done.8
  77.5 0.0 copy-done.9
  77.5 0.0 copy-done.10
  77.5 3.0 %cells.1 = (bf16[16,240,128]{2,1,0:T(8,128)(2,1)S(1)}, f32[8,128]{1,0:T(8,128)S(1)}, bf16[16,160,128]{2,1,0:T(8,128)(2,1)S(1)}, bf16[16,160,128]{2,1,0:T(8,128)(2,1)}) custom-call(bf16[16,240,128]{2,1,0:T(8,128)(2,1)S(1)} %all_to_all.43.lines, bf16[32,24,128]{2,1,0:T(8,128)(2,1)S(1)} %copy-done.8, bf16[16,160,128]{2,1,0:T(8,128)(2,1)S(1)} %bitcast.21, ...), custom_call_target="tpu_custom_call" | custom-call | flops 100000000 | bytes 4000000 | tf_op jit(solution)/shard_map/cells/pallas_call | solution.py:572
  80.5 18.3 %all_to_all.44.lines = bf16[16,240,128]{2,1,0:T(8,128)(2,1)S(1)} all-to-all(bf16[16,240,128]{2,1,0:T(8,128)(2,1)S(1)} %get-tuple-element.22), channel_id=1, replica_groups=mesh['gx'=16,'gy'=16] {'gx'}, dimensions={0} | all-to-all | bytes 1966080 | tf_op jit(solution)/shard_map/all_to_all | solution.py:546
  98.8 1.0 x_analysis_back.1
  99.8 13.1 %all_to_all.45.lines = bf16[16,24,128]{2,1,0:T(8,128)(2,1)S(1)} all-to-all(bf16[16,24,128]{2,1,0:T(8,128)(2,1)S(1)} %x_analysis_back.1), channel_id=1, replica_groups=mesh['gx'=16,'gy'=16] {'gy'}, dimensions={0} | all-to-all | bytes 196608 | tf_op jit(solution)/shard_map/all_to_all | solution.py:546
  112.9 1.3 back.1
  114.1 11.6 %all_to_all.46.modes = bf16[16,32,128]{2,1,0:T(8,128)(2,1)S(1)} all-to-all(bf16[16,32,128]{2,1,0:T(8,128)(2,1)S(1)} %get-tuple-element.25), channel_id=1, replica_groups=mesh['gx'=16,'gy'=16] {'gy'}, dimensions={0} | all-to-all | bytes 262144 | tf_op jit(solution)/shard_map/all_to_all | solution.py:546
  125.7 1.0 x_synthesis_back.1
  126.7 18.5 %all_to_all.47.lines = bf16[16,256,128]{2,1,0:T(8,128)(2,1)S(1)} all-to-all(bf16[16,256,128]{2,1,0:T(8,128)(2,1)S(1)} %get-tuple-element.28), channel_id=1, replica_groups=mesh['gx'=16,'gy'=16] {'gx'}, dimensions={0} | all-to-all | bytes 2097152 | tf_op jit(solution)/shard_map/all_to_all | solution.py:546
  145.2 0.0 copy-done.7
  145.2 3.2 %last.1 = (f32[20,20]{1,0:T(8,128)}, f32[1,20]{1,0:T(1,128)}, bf16[16,160,128]{2,1,0:T(8,128)(2,1)}, f32[7200,24]{1,0:T(8,128)}) custom-call(bf16[16,256,128]{2,1,0:T(8,128)(2,1)S(1)} %all_to_all.47.lines, bf16[32,24,128]{2,1,0:T(8,128)(2,1)S(1)} %copy-done.7, bf16[16,160,128]{2,1,0:T(8,128)(2,1)S(1)} %get-tuple-element.29.slope, ...), custom_call_target="tpu_custom_call", output_to_operand_aliasing={{3}: (6, {})} | custom-call | flops 100000000 | bytes 4000000 | tf_op jit(solution)/shard_map/last/pallas_call | solution.py:598
  (7 shorter events, 0.0 us)
Async XLA Ops:
  0.6 1.1 copy-start
  1.7 24.2 %copy-start.4 = (bf16[48,2048]{1,0:T(8,128)(2,1)S(1)}, bf16[48,2048]{1,0:T(8,128)(2,1)}, u32[]{:S(2)}) copy-start(bf16[48,2048]{1,0:T(8,128)(2,1)} %constant.10.clone.table) | copy-start | bytes 589828
  1.7 43.8 %copy-start.2 = (bf16[24,20,20,2,9]{0,3,4,2,1:T(2,128)(2,1)S(1)}, bf16[24,20,20,2,9]{0,3,4,2,1:T(2,128)(2,1)}, u32[]{:S(2)}) copy-start(bf16[24,20,20,2,9]{0,3,4,2,1:T(2,128)(2,1)} %param.13) | copy-start | bytes 1036804
  1.7 43.8 %copy-start.6 = (bf16[240,128]{1,0:T(8,128)(2,1)S(1)}, bf16[240,128]{1,0:T(8,128)(2,1)}, u32[]{:S(2)}) copy-start(bf16[240,128]{1,0:T(8,128)(2,1)} %constant.11.clone.tables) | copy-start | bytes 184324
  1.7 56.1 %copy-start.3 = (bf16[48,2048]{1,0:T(8,128)(2,1)S(1)}, bf16[48,2048]{1,0:T(8,128)(2,1)}, u32[]{:S(2)}) copy-start(bf16[48,2048]{1,0:T(8,128)(2,1)} %constant.12.clone.table) | copy-start | bytes 589828
  25.9 51.6 %copy-start.1 = (bf16[16,8,20,128]{3,1,2,0:T(8,128)(2,1)S(1)}, bf16[16,8,20,128]{3,1,2,0:T(8,128)(2,1)}, u32[]{:S(2)}) copy-start(bf16[16,8,20,128]{3,1,2,0:T(8,128)(2,1)} %param.10) | copy-start | bytes 1966084
  25.9 51.6 %copy-start.5 = (bf16[16,8,20,128]{3,1,2,0:T(8,128)(2,1)S(1)}, bf16[16,8,20,128]{3,1,2,0:T(8,128)(2,1)}, u32[]{:S(2)}) copy-start(bf16[16,8,20,128]{3,1,2,0:T(8,128)(2,1)} %param.14) | copy-start | bytes 1966084
  25.9 51.6 %copy-start.8 = (bf16[32,24,128]{2,1,0:T(8,128)(2,1)S(1)}, bf16[32,24,128]{2,1,0:T(8,128)(2,1)}, u32[]{:S(2)}) copy-start(bf16[32,24,128]{2,1,0:T(8,128)(2,1)} %constant.13.clone.depth) | copy-start | bytes 589828
  25.9 51.6 %copy-start.9 = (bf16[20,20]{1,0:T(8,128)(2,1)S(1)}, bf16[20,20]{1,0:T(8,128)(2,1)}, u32[]{:S(2)}) copy-start(bf16[20,20]{1,0:T(8,128)(2,1)} %weight.3) | copy-start | bytes 2404
  25.9 51.6 %copy-start.10 = (f32[20]{0:T(128)S(1)}, f32[20]{0:T(128)}, u32[]{:S(2)}) copy-start(f32[20]{0:T(128)} %param.12) | copy-start | bytes 244
  80.5 64.7 %copy-start.7 = (bf16[32,24,128]{2,1,0:T(8,128)(2,1)S(1)}, bf16[32,24,128]{2,1,0:T(8,128)(2,1)}, u32[]{:S(2)}) copy-start(bf16[32,24,128]{2,1,0:T(8,128)(2,1)} %constant.14.clone.depth) | copy-start | bytes 589828

commit v7 on v6

--- a/solution.py
+++ b/solution.py
@@ -24,7 +24,7 @@
 CX = NX // N
 CY = NY // N
 ROWS = 12 * C
-GROUPS = C // 4
+GROUPS = C // 2
 PAIRS = 9
 WEIGHTS = C * C * PAIRS * 2
 FIRST = 0
@@ -60,8 +60,8 @@
 
 def depth_rows(scale):
     table = depth_table(scale).reshape(2, N, 2, 3, ZT).transpose(1, 2, 0, 3, 4)
-    table = np.broadcast_to(table[:, :, None], (N, 2, 4, 2, 3, ZT))
-    return np.ascontiguousarray(table).reshape(2 * N, 24, ZT)
+    table = np.broadcast_to(table[:, :, None], (N, 2, 2, 2, 3, ZT))
+    return np.ascontiguousarray(table).reshape(N, 24, ZT)
 
 
 def x_rows(scale):
@@ -133,8 +133,8 @@
 
 def depth_matrix(rows):
     wide = rows.astype(F32)
-    channel = iota((1, 24, 1), 1) // 6
-    parts = [(wide * ones_where(channel == k)).reshape(N * 48, ZT) for k in range(4)]
+    channel = iota((1, 24, 1), 1) // 6 % 2
+    parts = [(wide * ones_where(channel == k)).reshape(N * 24, ZT) for k in range(2)]
     return jnp.concatenate(parts, axis=1).astype(BF)
 
 
@@ -147,8 +147,8 @@
 
 def lane_maps():
     row, lane = iota((ROWS, 1), 0), iota((1, 256), 1)
-    inner = row % 24
-    start = (row // 24) % 2 * 128 + row // 48 * 24
+    inner = row % 12
+    start = (row // 12) % 2 * 128 + row // 24 * 12
     real = inner % 6 < 3
     plain = ones_where(lane == start + inner)
     other = jnp.where(real, inner + 3, inner - 3)
@@ -161,13 +161,13 @@
 
 
 def to_columns(values):
-    wide = values.astype(F32).reshape(CX, 4, CY, ZT)
-    return jnp.concatenate([wide[:, k].reshape(CX * CY, ZT) for k in range(4)], axis=1)
+    wide = values.astype(F32).reshape(CX, 2, CY, ZT)
+    return jnp.concatenate([wide[:, k].reshape(CX * CY, ZT) for k in range(2)], axis=1)
 
 
 def to_cells(columns):
-    parts = [columns[:, k * ZT : (k + 1) * ZT].reshape(CX, CY, ZT) for k in range(4)]
-    return jnp.stack(parts, axis=1).reshape(CX, 4 * CY, ZT)
+    parts = [columns[:, k * ZT : (k + 1) * ZT].reshape(CX, CY, ZT) for k in range(2)]
+    return jnp.stack(parts, axis=1).reshape(CX, 2 * CY, ZT)
 
 
 def wide_to_columns(wide):
@@ -175,34 +175,33 @@
         rows = wide[k * CY : k * CY + CY]
         return jnp.concatenate([rows[:, x * ZT : x * ZT + ZT] for x in range(CX)], axis=0)
 
-    return jnp.concatenate([channel(k) for k in range(4)], axis=1)
+    return jnp.concatenate([channel(k) for k in range(2)], axis=1)
 
 
 def wide_to_cells(wide):
     return jnp.stack([wide[:, x * ZT : x * ZT + ZT] for x in range(CX)], axis=0)
 
 
-def put_spectra(matrix, columns, first, out):
-    spectra = dot(matrix, jnp.concatenate(columns, axis=0), 1, 1).astype(BF)
-    for k in range(len(columns)):
-        spectrum = spectra[:, k * 128 : k * 128 + 128].reshape(N, 48, 128)
-        out[:, rows_of(first + k, 48), :] = spectrum
-
-
-BATCHES = ((0, 1), (2, 3), (4,))
+def put_spectra(matrix, columns, batch, out):
+    spectra = dot(matrix, jnp.concatenate(columns, axis=0), 1, 1)
+    parts = [spectra[:, k * 128 : k * 128 + 128].reshape(N, 24, 128) for k in range(2)]
+    out[:, rows_of(batch, 48), :] = jnp.concatenate(parts, axis=1).astype(BF)
+
+
+BATCHES = GROUPS // 2
 
 
 def depth_rows_here(scale):
     row, lane = iota((24, 1), 0), iota((1, ZT), 1)
-    mode = row % 3
+    mode = row // 12 * 3 + row % 3
     quarter = jnp.where(row % 6 < 3, 0.0, 8.0)
     z, t = (lane // T_SIZE).astype(F32), (lane % T_SIZE).astype(F32)
     blocks = []
-    for block in range(2 * N):
-        jz, jt = divmod(3 * block, KT)
-        carry = mode + jt >= KT
-        jt = jnp.where(carry, mode + jt - KT, mode + jt)
-        jz = jnp.where(carry, jz + 1, jz)
+    for block in range(N):
+        jz, jt = divmod(6 * block, KT)
+        jt = mode + jt
+        jz = jz + jt // KT
+        jt = jt % KT
         fz = jnp.where(jz < KZ // 2, jz, jz + Z - KZ).astype(F32)
         turns = fz * z + (jt * (Z // KT)).astype(F32) * t + quarter
         turns = turns - 32.0 * jnp.floor(turns * (1.0 / 32.0))
@@ -217,14 +216,18 @@
 
 def spectrum_kernel(field, out):
     matrix = depth_matrix(depth_rows_here(ZT**-0.5))
-    for batch in BATCHES:
-        columns = [to_columns(field[:, rows_of(g, 32), :]).astype(BF) for g in batch]
-        put_spectra(matrix, columns, batch[0], out)
+    for batch in range(BATCHES):
+        groups = (2 * batch, 2 * batch + 1)
+        columns = [to_columns(field[:, rows_of(g, 16), :]).astype(BF) for g in groups]
+        put_spectra(matrix, columns, batch, out)
 
 
 def from_spectra(lines, matrix):
-    rows = [lines[:, rows_of(g, 48), :].reshape(N * 48, 128) for g in range(GROUPS)]
-    return dot(jnp.concatenate(rows, axis=1), matrix, 0, 0)
+    rows = []
+    for batch in range(BATCHES):
+        wide = lines[:, rows_of(batch, 48), :].astype(F32).reshape(N, 2, 24, 128)
+        rows += [wide[:, k].reshape(N * 24, 128) for k in range(2)]
+    return dot(jnp.concatenate(rows, axis=1).astype(BF), matrix, 0, 0)
 
 
 def split_dot(left, right):
@@ -485,10 +488,10 @@
     spectral = from_spectra(lines, matrix)
     pointwise = dot(mixing, fields) + shift
     slopes = []
-    for batch in BATCHES:
+    for batch in range(BATCHES):
         columns = []
-        for group in batch:
-            span = rows_of(group, 32)
+        for group in (2 * batch, 2 * batch + 1):
+            span = rows_of(group, 16)
             pre = spectral[rows_of(group, 128)] + wide_to_columns(pointwise[span])
             phi = 0.5 * (1.0 + lax.erf(pre * 0.7071067811865476))
             field_out[:, span, :] = to_cells(pre * phi).astype(BF)
@@ -498,7 +501,7 @@
             slope = to_cells(slope).astype(BF)
             slope_out[:, span, :] = slope
             slopes.append(flat_cells(slope))
-        put_spectra(matrix, columns, batch[0], out)
+        put_spectra(matrix, columns, batch, out)
     slopes = jnp.concatenate(slopes, axis=0)
     cross = dot(fields, slopes, 1, 1)
     total = dot(jnp.ones((8, CX * ZT), BF), slopes, 1, 1)
@@ -536,7 +539,7 @@
     pointwise = dot(spread_map(weight[...], 0), flat_cells(slope))
     spectral = from_spectra(lines, depth_matrix(depth[...]))
     for group in range(GROUPS):
-        span = rows_of(group, 32)
+        span = rows_of(group, 16)
         total = to_cells(spectral[rows_of(group, 128)]) + wide_to_cells(pointwise[span])
         field_out[:, span, :] = total.astype(BF)
     end_weight_gradient(1 - FIRST, made, weight_to, semaphore)

time: 149 us -> 148 us (level)
  no operation moved by 1% of the time
where the time goes in v7:
time: 148 us; the launch traced here: 147 us
  blocking collectives  133 us (90%)
  Pallas kernels  12.8 us (9%)
    all_to_all x8, blocking collectives, exchange(): return lax.all_to_all(values, axis, split_axis=0, concat_axis=0, tiled=True)  133 us
    pallas_call x1, Pallas kernels, body(): call(last_kernel, (shaped((C, C), F32), shaped((1, C), F32), shaped(cells...  3.17 us

profile of v7, /device:TPU:1, one launch (start us, length us, event | category | flops | bytes accessed | tf_op | source)
XLA Modules:
  0.0 147.5 jit_solution(1513895577067397316)
XLA Ops:
  0.6 0.0 copy-start
  0.6 1.1 copy-done
  1.7 0.0 copy-start.2
  1.7 0.6 spectrum.1
  2.3 23.1 %all_to_all.40.lines = bf16[16,240,128]{2,1,0:T(8,128)(2,1)S(1)} all-to-all(bf16[16,240,128]{2,1,0:T(8,128)(2,1)S(1)} %spectrum.1), channel_id=1, replica_groups=mesh['gx'=16,'gy'=16] {'gx'}, dimensions={0} | all-to-all | bytes 1966080 | tf_op jit(solution)/shard_map/all_to_all | solution.py:549
  25.4 0.0 copy-done.4
  25.5 0.0 copy-start.9
  25.5 0.0 copy-start.10
  25.5 1.0 x_analysis.1
  26.5 18.6 %all_to_all.41.lines = bf16[16,24,128]{2,1,0:T(8,128)(2,1)S(1)} all-to-all(bf16[16,24,128]{2,1,0:T(8,128)(2,1)S(1)} %x_analysis.1), channel_id=1, replica_groups=mesh['gx'=16,'gy'=16] {'gy'}, dimensions={0} | all-to-all | bytes 196608 | tf_op jit(solution)/shard_map/all_to_all | solution.py:549
  45.1 0.0 copy-done.2
  45.1 0.0 copy-done.6
  45.1 1.3 product.1
  46.4 10.9 %all_to_all.42.modes = bf16[16,24,128]{2,1,0:T(8,128)(2,1)S(1)} all-to-all(bf16[16,24,128]{2,1,0:T(8,128)(2,1)S(1)} %get-tuple-element.20), channel_id=1, replica_groups=mesh['gx'=16,'gy'=16] {'gy'}, dimensions={0} | all-to-all | bytes 196608 | tf_op jit(solution)/shard_map/all_to_all | solution.py:549
  57.3 0.0 copy-done.3
  57.3 0.9 x_synthesis.1
  58.3 18.8 %all_to_all.43.lines = bf16[16,240,128]{2,1,0:T(8,128)(2,1)S(1)} all-to-all(bf16[16,240,128]{2,1,0:T(8,128)(2,1)S(1)} %x_synthesis.1), channel_id=1, replica_groups=mesh['gx'=16,'gy'=16] {'gx'}, dimensions={0} | all-to-all | bytes 1966080 | tf_op jit(solution)/shard_map/all_to_all | solution.py:549
  77.0 0.0 copy-done.1
  77.0 0.0 copy-done.5
  77.0 0.0 copy-done.7
  77.0 0.0 copy-done.9
  77.1 0.0 copy-done.10
  77.1 2.5 %cells.1 = (bf16[16,240,128]{2,1,0:T(8,128)(2,1)S(1)}, f32[8,128]{1,0:T(8,128)S(1)}, bf16[16,160,128]{2,1,0:T(8,128)(2,1)S(1)}, bf16[16,160,128]{2,1,0:T(8,128)(2,1)}) custom-call(bf16[16,240,128]{2,1,0:T(8,128)(2,1)S(1)} %all_to_all.43.lines, bf16[16,24,128]{2,1,0:T(8,128)(2,1)S(1)} %copy-done.7, bf16[16,160,128]{2,1,0:T(8,128)(2,1)S(1)} %bitcast.21, ...), custom_call_target="tpu_custom_call" | custom-call | flops 100000000 | bytes 4000000 | tf_op jit(solution)/shard_map/cells/pallas_call | solution.py:575
  79.6 18.3 %all_to_all.44.lines = bf16[16,240,128]{2,1,0:T(8,128)(2,1)S(1)} all-to-all(bf16[16,240,128]{2,1,0:T(8,128)(2,1)S(1)} %get-tuple-element.22), channel_id=1, replica_groups=mesh['gx'=16,'gy'=16] {'gx'}, dimensions={0} | all-to-all | bytes 1966080 | tf_op jit(solution)/shard_map/all_to_all | solution.py:549
  97.9 1.0 x_analysis_back.1
  98.9 13.1 %all_to_all.45.lines = bf16[16,24,128]{2,1,0:T(8,128)(2,1)S(1)} all-to-all(bf16[16,24,128]{2,1,0:T(8,128)(2,1)S(1)} %x_analysis_back.1), channel_id=1, replica_groups=mesh['gx'=16,'gy'=16] {'gy'}, dimensions={0} | all-to-all | bytes 196608 | tf_op jit(solution)/shard_map/all_to_all | solution.py:549
  112.0 1.3 back.1
  113.2 11.6 %all_to_all.46.modes = bf16[16,32,128]{2,1,0:T(8,128)(2,1)S(1)} all-to-all(bf16[16,32,128]{2,1,0:T(8,128)(2,1)S(1)} %get-tuple-element.25), channel_id=1, replica_groups=mesh['gx'=16,'gy'=16] {'gy'}, dimensions={0} | all-to-all | bytes 262144 | tf_op jit(solution)/shard_map/all_to_all | solution.py:549
  124.8 1.0 x_synthesis_back.1
  125.8 18.5 %all_to_all.47.lines = bf16[16,256,128]{2,1,0:T(8,128)(2,1)S(1)} all-to-all(bf16[16,256,128]{2,1,0:T(8,128)(2,1)S(1)} %get-tuple-element.28), channel_id=1, replica_groups=mesh['gx'=16,'gy'=16] {'gx'}, dimensions={0} | all-to-all | bytes 2097152 | tf_op jit(solution)/shard_map/all_to_all | solution.py:549
  144.3 0.0 copy-done.8
  144.3 3.2 %last.1 = (f32[20,20]{1,0:T(8,128)}, f32[1,20]{1,0:T(1,128)}, bf16[16,160,128]{2,1,0:T(8,128)(2,1)}, f32[7200,24]{1,0:T(8,128)}) custom-call(bf16[16,256,128]{2,1,0:T(8,128)(2,1)S(1)} %all_to_all.47.lines, bf16[16,24,128]{2,1,0:T(8,128)(2,1)S(1)} %copy-done.8, bf16[16,160,128]{2,1,0:T(8,128)(2,1)S(1)} %get-tuple-element.29.slope, ...), custom_call_target="tpu_custom_call", output_to_operand_aliasing={{3}: (6, {})} | custom-call | flops 100000000 | bytes 4000000 | tf_op jit(solution)/shard_map/last/pallas_call | solution.py:601
  (7 shorter events, 0.0 us)
Async XLA Ops:
  0.6 1.1 copy-start
  1.7 23.7 %copy-start.4 = (bf16[48,2048]{1,0:T(8,128)(2,1)S(1)}, bf16[48,2048]{1,0:T(8,128)(2,1)}, u32[]{:S(2)}) copy-start(bf16[48,2048]{1,0:T(8,128)(2,1)} %constant.10.clone.table) | copy-start | bytes 589828
  1.7 43.3 %copy-start.2 = (bf16[24,20,20,2,9]{0,3,4,2,1:T(2,128)(2,1)S(1)}, bf16[24,20,20,2,9]{0,3,4,2,1:T(2,128)(2,1)}, u32[]{:S(2)}) copy-start(bf16[24,20,20,2,9]{0,3,4,2,1:T(2,128)(2,1)} %param.13) | copy-start | bytes 1036804
  1.7 43.4 %copy-start.6 = (bf16[240,128]{1,0:T(8,128)(2,1)S(1)}, bf16[240,128]{1,0:T(8,128)(2,1)}, u32[]{:S(2)}) copy-start(bf16[240,128]{1,0:T(8,128)(2,1)} %constant.11.clone.tables) | copy-start | bytes 184324
  1.7 55.6 %copy-start.3 = (bf16[48,2048]{1,0:T(8,128)(2,1)S(1)}, bf16[48,2048]{1,0:T(8,128)(2,1)}, u32[]{:S(2)}) copy-start(bf16[48,2048]{1,0:T(8,128)(2,1)} %constant.12.clone.table) | copy-start | bytes 589828
  25.4 51.6 %copy-start.1 = (bf16[16,8,20,128]{3,1,2,0:T(8,128)(2,1)S(1)}, bf16[16,8,20,128]{3,1,2,0:T(8,128)(2,1)}, u32[]{:S(2)}) copy-start(bf16[16,8,20,128]{3,1,2,0:T(8,128)(2,1)} %param.10) | copy-start | bytes 1966084
  25.4 51.6 %copy-start.5 = (bf16[16,8,20,128]{3,1,2,0:T(8,128)(2,1)S(1)}, bf16[16,8,20,128]{3,1,2,0:T(8,128)(2,1)}, u32[]{:S(2)}) copy-start(bf16[16,8,20,128]{3,1,2,0:T(8,128)(2,1)} %param.14) | copy-start | bytes 1966084
  25.4 51.6 %copy-start.7 = (bf16[16,24,128]{2,1,0:T(8,128)(2,1)S(1)}, bf16[16,24,128]{2,1,0:T(8,128)(2,1)}, u32[]{:S(2)}) copy-start(bf16[16,24,128]{2,1,0:T(8,128)(2,1)} %constant.13.clone.depth) | copy-start | bytes 294916
  25.5 51.6 %copy-start.9 = (bf16[20,20]{1,0:T(8,128)(2,1)S(1)}, bf16[20,20]{1,0:T(8,128)(2,1)}, u32[]{:S(2)}) copy-start(bf16[20,20]{1,0:T(8,128)(2,1)} %weight.3) | copy-start | bytes 2404
  25.5 51.6 %copy-start.10 = (f32[20]{0:T(128)S(1)}, f32[20]{0:T(128)}, u32[]{:S(2)}) copy-start(f32[20]{0:T(128)} %param.12) | copy-start | bytes 244
  79.6 64.7 %copy-start.8 = (bf16[16,24,128]{2,1,0:T(8,128)(2,1)S(1)}, bf16[16,24,128]{2,1,0:T(8,128)(2,1)}, u32[]{:S(2)}) copy-start(bf16[16,24,128]{2,1,0:T(8,128)(2,1)} %constant.14.clone.depth) | copy-start | bytes 294916

commit v8 on v7

--- a/solution.py
+++ b/solution.py
@@ -271,6 +271,20 @@
 
 def when_core(core):
     return pl.when(lax.axis_index("gy") % 2 == core)
+
+
+def put_sums(core, field, slope, out):
+    @when_core(core)
+    def _():
+        fields, slopes = flat_cells(field), flat_cells(slope)
+        cross = dot(fields, slopes, 1, 1)
+        total = dot(jnp.ones((8, CX * ZT), BF), slopes, 1, 1)
+        out[...] = pack_sums(pack_lines(cross, total))
+
+
+def x_analysis_sums_kernel(lines, table, field, slope, out, sums):
+    x_analysis_kernel(lines, table, out)
+    put_sums(1, field, slope, sums)
 
 
 def start_weight_gradient(core, coef, dual, made, target, semaphore):
@@ -425,12 +439,13 @@
     out[...] = y_synthesis(product, tables[Y_MID], tables[PICKS]).astype(BF)
 
 
-def back_kernel(lines, packed, sums, tables, out, dual, lanes, result):
+def back_kernel(lines, packed, sums, late_sums, tables, out, dual, lanes, result):
     for u, unit in enumerate(y_analysis(lines[...], tables[Y_MID], tables[PICKS])):
         dual[u] = unit
     modes = mix_back(packed, dual, lanes, result)
     modes = y_synthesis(modes, tables[Y_IN], tables[PICKS])
-    tail = jnp.broadcast_to(sums[...].reshape(1, 8, 128), (N, 8, 128))
+    tail = jnp.where(lax.axis_index("gy") % 2 == 0, sums[...], late_sums[...])
+    tail = jnp.broadcast_to(tail.reshape(1, 8, 128), (N, 8, 128))
     out[...] = jnp.concatenate([modes, tail], axis=1).astype(BF)
 
 
@@ -487,7 +502,6 @@
     fields = flat_cells(field)
     spectral = from_spectra(lines, matrix)
     pointwise = dot(mixing, fields) + shift
-    slopes = []
     for batch in range(BATCHES):
         columns = []
         for group in (2 * batch, 2 * batch + 1):
@@ -498,14 +512,9 @@
             slope = phi + pre * jnp.exp(-0.5 * pre * pre) * 0.3989422804014327
             slope = slope * to_columns(cotangent[:, span, :])
             columns.append(slope.astype(BF))
-            slope = to_cells(slope).astype(BF)
-            slope_out[:, span, :] = slope
-            slopes.append(flat_cells(slope))
+            slope_out[:, span, :] = to_cells(slope).astype(BF)
         put_spectra(matrix, columns, batch, out)
-    slopes = jnp.concatenate(slopes, axis=0)
-    cross = dot(fields, slopes, 1, 1)
-    total = dot(jnp.ones((8, CX * ZT), BF), slopes, 1, 1)
-    sums[...] = pack_sums(pack_lines(cross, total))
+    put_sums(0, field, slope_out, sums)
 
 
 def last_kernel(
@@ -578,14 +587,16 @@
         name="cells",
     )(message, DEPTH_MID, field, cotangent, point_weight, point_bias.reshape(1, C))
     message = exchange(message, "gx")
-    message = call(x_analysis_kernel, mode_message, name="x_analysis_back")(message, X_MID)
+    message, late_sums = call(
+        x_analysis_sums_kernel, (mode_message, shaped((8, 128), F32)), name="x_analysis_back"
+    )(message, X_MID, field, slope)
     message = exchange(message, "gy")
     message, dual = call(
         back_kernel,
         (shaped((N, 32, 128), BF), mode_lines),
         [pltpu.VMEM((3, 144, 128), F32), pltpu.VMEM((3, 144, KY), F32)],
         "back",
-    )(message, packed, sums, Y_ALL)
+    )(message, packed, sums, late_sums, Y_ALL)
     message = exchange(message, "gy")
     made = [wide_weights, pltpu.SemaphoreType.DMA(())]
     weight_shape = shaped((WEIGHTS, KY), F32)

time: 148 us -> 148 us (level)
  no operation moved by 1% of the time
where the time goes in v8:
time: 148 us; the launch traced here: 147 us
  blocking collectives  132 us (89%)
  Pallas kernels  13.8 us (9%)
    all_to_all x8, blocking collectives, exchange(): return lax.all_to_all(values, axis, split_axis=0, concat_axis=0, tiled=True)  132 us
    pallas_call x1, Pallas kernels, body(): call(last_kernel, (shaped((C, C), F32), shaped((1, C), F32), shaped(cells...  3.18 us

profile of v8, /device:TPU:1, one launch (start us, length us, event | category | flops | bytes accessed | tf_op | source)
XLA Modules:
  0.0 147.5 jit_solution(8284123466383701009)
XLA Ops:
  0.6 0.0 copy-start
  0.6 1.1 copy-done
  1.7 0.0 copy-start.4
  1.7 0.6 spectrum.1
  2.3 23.1 %all_to_all.40.lines = bf16[16,240,128]{2,1,0:T(8,128)(2,1)S(1)} all-to-all(bf16[16,240,128]{2,1,0:T(8,128)(2,1)S(1)} %spectrum.1), channel_id=1, replica_groups=mesh['gx'=16,'gy'=16] {'gx'}, dimensions={0} | all-to-all | bytes 1966080 | tf_op jit(solution)/shard_map/all_to_all | solution.py:558
  25.4 0.0 copy-done.4
  25.5 0.0 copy-start.9
  25.5 0.0 copy-start.10
  25.5 1.0 x_analysis.1
  26.5 18.6 %all_to_all.41.lines = bf16[16,24,128]{2,1,0:T(8,128)(2,1)S(1)} all-to-all(bf16[16,24,128]{2,1,0:T(8,128)(2,1)S(1)} %x_analysis.1), channel_id=1, replica_groups=mesh['gx'=16,'gy'=16] {'gy'}, dimensions={0} | all-to-all | bytes 196608 | tf_op jit(solution)/shard_map/all_to_all | solution.py:558
  45.1 0.0 copy-done.2
  45.1 0.0 copy-done.6
  45.1 1.3 product.1
  46.4 10.9 %all_to_all.42.modes = bf16[16,24,128]{2,1,0:T(8,128)(2,1)S(1)} all-to-all(bf16[16,24,128]{2,1,0:T(8,128)(2,1)S(1)} %get-tuple-element.22), channel_id=1, replica_groups=mesh['gx'=16,'gy'=16] {'gy'}, dimensions={0} | all-to-all | bytes 196608 | tf_op jit(solution)/shard_map/all_to_all | solution.py:558
  57.3 0.0 copy-done.3
  57.3 0.9 x_synthesis.1
  58.3 18.8 %all_to_all.43.lines = bf16[16,240,128]{2,1,0:T(8,128)(2,1)S(1)} all-to-all(bf16[16,240,128]{2,1,0:T(8,128)(2,1)S(1)} %x_synthesis.1), channel_id=1, replica_groups=mesh['gx'=16,'gy'=16] {'gx'}, dimensions={0} | all-to-all | bytes 1966080 | tf_op jit(solution)/shard_map/all_to_all | solution.py:558
  77.0 0.0 copy-done.1
  77.0 0.0 copy-done.5
  77.0 0.0 copy-done.7
  77.0 0.0 copy-done.9
  77.1 0.0 copy-done.10
  77.1 2.5 %cells.1 = (bf16[16,240,128]{2,1,0:T(8,128)(2,1)S(1)}, f32[8,128]{1,0:T(8,128)S(1)}, bf16[16,160,128]{2,1,0:T(8,128)(2,1)S(1)}, bf16[16,160,128]{2,1,0:T(8,128)(2,1)}) custom-call(bf16[16,240,128]{2,1,0:T(8,128)(2,1)S(1)} %all_to_all.43.lines, bf16[16,24,128]{2,1,0:T(8,128)(2,1)S(1)} %copy-done.7, bf16[16,160,128]{2,1,0:T(8,128)(2,1)S(1)} %bitcast.21, ...), custom_call_target="tpu_custom_call" | custom-call | flops 100000000 | bytes 4000000 | tf_op jit(solution)/shard_map/cells/pallas_call | solution.py:584
  79.6 17.3 %all_to_all.44.lines = bf16[16,240,128]{2,1,0:T(8,128)(2,1)S(1)} all-to-all(bf16[16,240,128]{2,1,0:T(8,128)(2,1)S(1)} %get-tuple-element.24), channel_id=1, replica_groups=mesh['gx'=16,'gy'=16] {'gx'}, dimensions={0} | all-to-all | bytes 1966080 | tf_op jit(solution)/shard_map/all_to_all | solution.py:558
  96.8 2.0 %x_analysis_back.1 = (bf16[16,24,128]{2,1,0:T(8,128)(2,1)S(1)}, f32[8,128]{1,0:T(8,128)S(1)}) custom-call(bf16[16,240,128]{2,1,0:T(8,128)(2,1)S(1)} %all_to_all.44.lines, bf16[48,2048]{1,0:T(8,128)(2,1)S(1)} %copy-done.3, bf16[16,160,128]{2,1,0:T(8,128)(2,1)S(1)} %bitcast.22, bf16[16,160,128]{2,1,0:T(8,128)(2,1)S(1)} %get-tuple-element.25.slope), custom_call_target="tpu_custom_call" | custom-call | flops 100000000 | bytes 4000000 | tf_op jit(solution)/shard_map/x_analysis_back/pallas_call | solution.py:590
  98.8 13.1 %all_to_all.45.lines = bf16[16,24,128]{2,1,0:T(8,128)(2,1)S(1)} all-to-all(bf16[16,24,128]{2,1,0:T(8,128)(2,1)S(1)} %get-tuple-element.26), channel_id=1, replica_groups=mesh['gx'=16,'gy'=16] {'gy'}, dimensions={0} | all-to-all | bytes 196608 | tf_op jit(solution)/shard_map/all_to_all | solution.py:558
  111.9 1.2 back.1
  113.2 11.6 %all_to_all.46.modes = bf16[16,32,128]{2,1,0:T(8,128)(2,1)S(1)} all-to-all(bf16[16,32,128]{2,1,0:T(8,128)(2,1)S(1)} %get-tuple-element.30), channel_id=1, replica_groups=mesh['gx'=16,'gy'=16] {'gy'}, dimensions={0} | all-to-all | bytes 262144 | tf_op jit(solution)/shard_map/all_to_all | solution.py:558
  124.7 1.0 x_synthesis_back.1
  125.7 18.6 %all_to_all.47.lines = bf16[16,256,128]{2,1,0:T(8,128)(2,1)S(1)} all-to-all(bf16[16,256,128]{2,1,0:T(8,128)(2,1)S(1)} %get-tuple-element.33), channel_id=1, replica_groups=mesh['gx'=16,'gy'=16] {'gx'}, dimensions={0} | all-to-all | bytes 2097152 | tf_op jit(solution)/shard_map/all_to_all | solution.py:558
  144.3 0.0 copy-done.8
  144.3 3.2 %last.1 = (f32[20,20]{1,0:T(8,128)}, f32[1,20]{1,0:T(1,128)}, bf16[16,160,128]{2,1,0:T(8,128)(2,1)}, f32[7200,24]{1,0:T(8,128)}) custom-call(bf16[16,256,128]{2,1,0:T(8,128)(2,1)S(1)} %all_to_all.47.lines, bf16[16,24,128]{2,1,0:T(8,128)(2,1)S(1)} %copy-done.8, bf16[16,160,128]{2,1,0:T(8,128)(2,1)S(1)} %get-tuple-element.25.slope, ...), custom_call_target="tpu_custom_call", output_to_operand_aliasing={{3}: (6, {})} | custom-call | flops 100000000 | bytes 4000000 | tf_op jit(solution)/shard_map/last/pallas_call | solution.py:612
  (7 shorter events, 0.0 us)
Async XLA Ops:
  0.6 1.1 copy-start
  1.7 23.7 %copy-start.4 = (bf16[48,2048]{1,0:T(8,128)(2,1)S(1)}, bf16[48,2048]{1,0:T(8,128)(2,1)}, u32[]{:S(2)}) copy-start(bf16[48,2048]{1,0:T(8,128)(2,1)} %constant.10.clone.table) | copy-start | bytes 589828
  1.7 43.3 %copy-start.2 = (bf16[24,20,20,2,9]{0,3,4,2,1:T(2,128)(2,1)S(1)}, bf16[24,20,20,2,9]{0,3,4,2,1:T(2,128)(2,1)}, u32[]{:S(2)}) copy-start(bf16[24,20,20,2,9]{0,3,4,2,1:T(2,128)(2,1)} %param.13) | copy-start | bytes 1036804
  1.7 43.4 %copy-start.6 = (bf16[240,128]{1,0:T(8,128)(2,1)S(1)}, bf16[240,128]{1,0:T(8,128)(2,1)}, u32[]{:S(2)}) copy-start(bf16[240,128]{1,0:T(8,128)(2,1)} %constant.11.clone.tables) | copy-start | bytes 184324
  1.7 55.6 %copy-start.3 = (bf16[48,2048]{1,0:T(8,128)(2,1)S(1)}, bf16[48,2048]{1,0:T(8,128)(2,1)}, u32[]{:S(2)}) copy-start(bf16[48,2048]{1,0:T(8,128)(2,1)} %constant.12.clone.table) | copy-start | bytes 589828
  25.4 51.6 %copy-start.1 = (bf16[16,8,20,128]{3,1,2,0:T(8,128)(2,1)S(1)}, bf16[16,8,20,128]{3,1,2,0:T(8,128)(2,1)}, u32[]{:S(2)}) copy-start(bf16[16,8,20,128]{3,1,2,0:T(8,128)(2,1)} %param.10) | copy-start | bytes 1966084
  25.4 51.6 %copy-start.5 = (bf16[16,8,20,128]{3,1,2,0:T(8,128)(2,1)S(1)}, bf16[16,8,20,128]{3,1,2,0:T(8,128)(2,1)}, u32[]{:S(2)}) copy-start(bf16[16,8,20,128]{3,1,2,0:T(8,128)(2,1)} %param.14) | copy-start | bytes 1966084
  25.4 51.6 %copy-start.7 = (bf16[16,24,128]{2,1,0:T(8,128)(2,1)S(1)}, bf16[16,24,128]{2,1,0:T(8,128)(2,1)}, u32[]{:S(2)}) copy-start(bf16[16,24,128]{2,1,0:T(8,128)(2,1)} %constant.13.clone.depth) | copy-start | bytes 294916
  25.5 51.6 %copy-start.9 = (bf16[20,20]{1,0:T(8,128)(2,1)S(1)}, bf16[20,20]{1,0:T(8,128)(2,1)}, u32[]{:S(2)}) copy-start(bf16[20,20]{1,0:T(8,128)(2,1)} %weight.3) | copy-start | bytes 2404
  25.5 51.6 %copy-start.10 = (f32[20]{0:T(128)S(1)}, f32[20]{0:T(128)}, u32[]{:S(2)}) copy-start(f32[20]{0:T(128)} %param.12) | copy-start | bytes 244
  96.8 47.5 %copy-start.8 = (bf16[16,24,128]{2,1,0:T(8,128)(2,1)S(1)}, bf16[16,24,128]{2,1,0:T(8,128)(2,1)}, u32[]{:S(2)}) copy-start(bf16[16,24,128]{2,1,0:T(8,128)(2,1)} %constant.14.clone.depth) | copy-start | bytes 294916

commit v9 on v8

--- a/solution.py
+++ b/solution.py
@@ -282,9 +282,16 @@
         out[...] = pack_sums(pack_lines(cross, total))
 
 
-def x_analysis_sums_kernel(lines, table, field, slope, out, sums):
+def put_point_back(core, slope, weight, out):
+    @when_core(core)
+    def _():
+        out[...] = dot(spread_map(weight[...], 0), flat_cells(slope))
+
+
+def x_analysis_sums_kernel(lines, table, field, slope, weight, out, sums, point):
     x_analysis_kernel(lines, table, out)
     put_sums(1, field, slope, sums)
+    put_point_back(1, slope, weight, point)
 
 
 def start_weight_gradient(core, coef, dual, made, target, semaphore):
@@ -301,8 +308,11 @@
         pltpu.make_async_copy(made, target, semaphore).wait()
 
 
-def x_synthesis_sums_kernel(modes, table, coef, dual, out, weight_to, made, semaphore):
+def x_synthesis_sums_kernel(
+    modes, table, coef, dual, slope, weight, out, point, weight_to, made, semaphore
+):
     start_weight_gradient(FIRST, coef, dual, made, weight_to, semaphore)
+    put_point_back(0, slope, weight, point)
     wide = modes[...].astype(F32)
     first, second = x_modes(wide[:, :24])
     lines = x_lines(first, second, table[...])
@@ -520,8 +530,8 @@
 def last_kernel(
     lines,
     depth,
-    slope,
-    weight,
+    late_point,
+    point,
     coef,
     dual,
     _,
@@ -545,11 +555,12 @@
                     point_out[index : index + 1, :] = row[:, :C]
                 else:
                     bias_out[...] = row[:, :C]
-    pointwise = dot(spread_map(weight[...], 0), flat_cells(slope))
+    late = lax.axis_index("gy") % 2 == 0
     spectral = from_spectra(lines, depth_matrix(depth[...]))
     for group in range(GROUPS):
         span = rows_of(group, 16)
-        total = to_cells(spectral[rows_of(group, 128)]) + wide_to_cells(pointwise[span])
+        pointwise = jnp.where(late, late_point[span], point[span])
+        total = to_cells(spectral[rows_of(group, 128)]) + wide_to_cells(pointwise)
         field_out[:, span, :] = total.astype(BF)
     end_weight_gradient(1 - FIRST, made, weight_to, semaphore)
 
@@ -587,9 +598,12 @@
         name="cells",
     )(message, DEPTH_MID, field, cotangent, point_weight, point_bias.reshape(1, C))
     message = exchange(message, "gx")
-    message, late_sums = call(
-        x_analysis_sums_kernel, (mode_message, shaped((8, 128), F32)), name="x_analysis_back"
-    )(message, X_MID, field, slope)
+    point_shape = shaped((C * CY, CX * ZT), F32)
+    message, late_sums, point = call(
+        x_analysis_sums_kernel,
+        (mode_message, shaped((8, 128), F32), point_shape),
+        name="x_analysis_back",
+    )(message, X_MID, field, slope, point_weight)
     message = exchange(message, "gy")
     message, dual = call(
         back_kernel,
@@ -600,14 +614,14 @@
     message = exchange(message, "gy")
     made = [wide_weights, pltpu.SemaphoreType.DMA(())]
     weight_shape = shaped((WEIGHTS, KY), F32)
-    message, weight_grad = call(
+    message, late_point, weight_grad = call(
         x_synthesis_sums_kernel,
-        (shaped((N, 256, 128), BF), weight_shape),
+        (shaped((N, 256, 128), BF), point_shape, weight_shape),
         made,
         "x_synthesis_back",
-        [pltpu.VMEM] * 4,
-        [pltpu.VMEM, pl.ANY],
-    )(message, X_IN, coef, dual)
+        [pltpu.VMEM] * 6,
+        [pltpu.VMEM] * 2 + [pl.ANY],
+    )(message, X_IN, coef, dual, slope, point_weight)
     message = exchange(message, "gx")
     grad_point, grad_bias, grad_in, weight_grad = call(
         last_kernel,
@@ -617,7 +631,7 @@
         [pltpu.VMEM] * 6 + [pl.ANY],
         [pltpu.VMEM] * 3 + [pl.ANY],
         {6: 3},
-    )(message, DEPTH_IN, slope, point_weight, coef, dual, weight_grad)
+    )(message, DEPTH_IN, late_point, point, coef, dual, weight_grad)
     grad_spec = weight_grad.reshape(C, C, PAIRS, 2, KY).transpose(4, 0, 1, 3, 2)
 
     def natural(values):

time: 148 us -> 148 us (level)
  no operation moved by 1% of the time
where the time goes in v9:
time: 148 us; the launch traced here: 147 us
  blocking collectives  131 us (89%)
  Pallas kernels  14.2 us (10%)
    all_to_all x8, blocking collectives, exchange(): return lax.all_to_all(values, axis, split_axis=0, concat_axis=0, tiled=True)  131 us
    pallas_call x1, Pallas kernels, body(): call(last_kernel, (shaped((C, C), F32), shaped((1, C), F32), shaped(cells...  3.19 us

profile of v9, /device:TPU:1, one launch (start us, length us, event | category | flops | bytes accessed | tf_op | source)
XLA Modules:
  0.0 147.3 jit_solution(9921406485612117741)
XLA Ops:
  0.6 0.0 copy-start
  0.6 1.1 copy-done
  1.7 0.6 spectrum.1
  2.3 0.0 copy-start.2
  2.3 0.0 copy-start.6
  2.4 23.1 %all_to_all.40.lines = bf16[16,240,128]{2,1,0:T(8,128)(2,1)S(1)} all-to-all(bf16[16,240,128]{2,1,0:T(8,128)(2,1)S(1)} %spectrum.1), channel_id=1, replica_groups=mesh['gx'=16,'gy'=16] {'gx'}, dimensions={0} | all-to-all | bytes 1966080 | tf_op jit(solution)/shard_map/all_to_all | solution.py:569
  25.5 0.0 copy-done.4
  25.5 1.0 x_analysis.1
  26.5 18.6 %all_to_all.41.lines = bf16[16,24,128]{2,1,0:T(8,128)(2,1)S(1)} all-to-all(bf16[16,24,128]{2,1,0:T(8,128)(2,1)S(1)} %x_analysis.1), channel_id=1, replica_groups=mesh['gx'=16,'gy'=16] {'gy'}, dimensions={0} | all-to-all | bytes 196608 | tf_op jit(solution)/shard_map/all_to_all | solution.py:569
  45.1 0.0 copy-done.2
  45.1 0.0 copy-done.6
  45.1 1.4 product.1
  46.4 0.0 copy-start.1
  46.4 0.0 copy-start.5
  46.5 0.0 copy-start.8
  46.5 0.0 copy-start.9
  46.5 0.0 copy-start.10
  46.5 11.0 %all_to_all.42.modes = bf16[16,24,128]{2,1,0:T(8,128)(2,1)S(1)} all-to-all(bf16[16,24,128]{2,1,0:T(8,128)(2,1)S(1)} %get-tuple-element.24), channel_id=1, replica_groups=mesh['gx'=16,'gy'=16] {'gy'}, dimensions={0} | all-to-all | bytes 196608 | tf_op jit(solution)/shard_map/all_to_all | solution.py:569
  57.5 0.0 copy-done.3
  57.5 0.9 x_synthesis.1
  58.5 18.8 %all_to_all.43.lines = bf16[16,240,128]{2,1,0:T(8,128)(2,1)S(1)} all-to-all(bf16[16,240,128]{2,1,0:T(8,128)(2,1)S(1)} %x_synthesis.1), channel_id=1, replica_groups=mesh['gx'=16,'gy'=16] {'gx'}, dimensions={0} | all-to-all | bytes 1966080 | tf_op jit(solution)/shard_map/all_to_all | solution.py:569
  77.2 0.0 copy-done.5
  77.3 2.5 %cells.1 = (bf16[16,240,128]{2,1,0:T(8,128)(2,1)S(1)}, f32[8,128]{1,0:T(8,128)S(1)}, bf16[16,160,128]{2,1,0:T(8,128)(2,1)S(1)}, bf16[16,160,128]{2,1,0:T(8,128)(2,1)}) custom-call(bf16[16,240,128]{2,1,0:T(8,128)(2,1)S(1)} %all_to_all.43.lines, bf16[16,24,128]{2,1,0:T(8,128)(2,1)S(1)} %copy-done.8, bf16[16,160,128]{2,1,0:T(8,128)(2,1)S(1)} %bitcast.21, ...), custom_call_target="tpu_custom_call" | custom-call | flops 100000000 | bytes 4000000 | tf_op jit(solution)/shard_map/cells/pallas_call | solution.py:595
  79.7 17.3 %all_to_all.44.lines = bf16[16,240,128]{2,1,0:T(8,128)(2,1)S(1)} all-to-all(bf16[16,240,128]{2,1,0:T(8,128)(2,1)S(1)} %get-tuple-element.26), channel_id=1, replica_groups=mesh['gx'=16,'gy'=16] {'gx'}, dimensions={0} | all-to-all | bytes 1966080 | tf_op jit(solution)/shard_map/all_to_all | solution.py:569
  97.0 2.4 %x_analysis_back.1 = (bf16[16,24,128]{2,1,0:T(8,128)(2,1)S(1)}, f32[8,128]{1,0:T(8,128)S(1)}, f32[160,2048]{1,0:T(8,128)S(1)}) custom-call(bf16[16,240,128]{2,1,0:T(8,128)(2,1)S(1)} %all_to_all.44.lines, bf16[48,2048]{1,0:T(8,128)(2,1)S(1)} %copy-done.3, bf16[16,160,128]{2,1,0:T(8,128)(2,1)S(1)} %bitcast.22, ...), custom_call_target="tpu_custom_call" | custom-call | flops 100000000 | bytes 4000000 | tf_op jit(solution)/shard_map/x_analysis_back/pallas_call | solution.py:602
  99.4 12.7 %all_to_all.45.lines = bf16[16,24,128]{2,1,0:T(8,128)(2,1)S(1)} all-to-all(bf16[16,24,128]{2,1,0:T(8,128)(2,1)S(1)} %get-tuple-element.28), channel_id=1, replica_groups=mesh['gx'=16,'gy'=16] {'gy'}, dimensions={0} | all-to-all | bytes 196608 | tf_op jit(solution)/shard_map/all_to_all | solution.py:569
  112.1 1.3 back.1
  113.4 0.0 copy-start.7
  113.4 11.7 %all_to_all.46.modes = bf16[16,32,128]{2,1,0:T(8,128)(2,1)S(1)} all-to-all(bf16[16,32,128]{2,1,0:T(8,128)(2,1)S(1)} %get-tuple-element.32), channel_id=1, replica_groups=mesh['gx'=16,'gy'=16] {'gy'}, dimensions={0} | all-to-all | bytes 262144 | tf_op jit(solution)/shard_map/all_to_all | solution.py:569
  125.1 1.0 x_synthesis_back.1
  126.1 18.1 %all_to_all.47.lines = bf16[16,256,128]{2,1,0:T(8,128)(2,1)S(1)} all-to-all(bf16[16,256,128]{2,1,0:T(8,128)(2,1)S(1)} %get-tuple-element.35), channel_id=1, replica_groups=mesh['gx'=16,'gy'=16] {'gx'}, dimensions={0} | all-to-all | bytes 2097152 | tf_op jit(solution)/shard_map/all_to_all | solution.py:569
  144.1 3.2 %last.1 = (f32[20,20]{1,0:T(8,128)}, f32[1,20]{1,0:T(1,128)}, bf16[16,160,128]{2,1,0:T(8,128)(2,1)}, f32[7200,24]{1,0:T(8,128)}) custom-call(bf16[16,256,128]{2,1,0:T(8,128)(2,1)S(1)} %all_to_all.47.lines, bf16[16,24,128]{2,1,0:T(8,128)(2,1)S(1)} %copy-done.7, f32[160,2048]{1,0:T(8,128)S(1)} %get-tuple-element.36.late_point, ...), custom_call_target="tpu_custom_call", output_to_operand_aliasing={{3}: (6, {})} | custom-call | flops 100000000 | bytes 4000000 | tf_op jit(solution)/shard_map/last/pallas_call | solution.py:626
  (7 shorter events, 0.0 us)
Async XLA Ops:
  0.6 1.1 copy-start
  1.7 23.7 %copy-start.4 = (bf16[48,2048]{1,0:T(8,128)(2,1)S(1)}, bf16[48,2048]{1,0:T(8,128)(2,1)}, u32[]{:S(2)}) copy-start(bf16[48,2048]{1,0:T(8,128)(2,1)} %constant.10.clone.table) | copy-start | bytes 589828
  2.3 42.7 %copy-start.2 = (bf16[24,20,20,2,9]{0,3,4,2,1:T(2,128)(2,1)S(1)}, bf16[24,20,20,2,9]{0,3,4,2,1:T(2,128)(2,1)}, u32[]{:S(2)}) copy-start(bf16[24,20,20,2,9]{0,3,4,2,1:T(2,128)(2,1)} %param.13) | copy-start | bytes 1036804
  2.3 42.7 %copy-start.6 = (bf16[240,128]{1,0:T(8,128)(2,1)S(1)}, bf16[240,128]{1,0:T(8,128)(2,1)}, u32[]{:S(2)}) copy-start(bf16[240,128]{1,0:T(8,128)(2,1)} %constant.11.clone.tables) | copy-start | bytes 184324
  25.5 32.1 %copy-start.3 = (bf16[48,2048]{1,0:T(8,128)(2,1)S(1)}, bf16[48,2048]{1,0:T(8,128)(2,1)}, u32[]{:S(2)}) copy-start(bf16[48,2048]{1,0:T(8,128)(2,1)} %constant.12.clone.table) | copy-start | bytes 589828
  46.4 30.8 %copy-start.1 = (bf16[16,8,20,128]{3,1,2,0:T(8,128)(2,1)S(1)}, bf16[16,8,20,128]{3,1,2,0:T(8,128)(2,1)}, u32[]{:S(2)}) copy-start(bf16[16,8,20,128]{3,1,2,0:T(8,128)(2,1)} %param.10) | copy-start | bytes 1966084
  46.4 30.8 %copy-start.5 = (bf16[16,8,20,128]{3,1,2,0:T(8,128)(2,1)S(1)}, bf16[16,8,20,128]{3,1,2,0:T(8,128)(2,1)}, u32[]{:S(2)}) copy-start(bf16[16,8,20,128]{3,1,2,0:T(8,128)(2,1)} %param.14) | copy-start | bytes 1966084
  46.5 30.8 %copy-start.8 = (bf16[16,24,128]{2,1,0:T(8,128)(2,1)S(1)}, bf16[16,24,128]{2,1,0:T(8,128)(2,1)}, u32[]{:S(2)}) copy-start(bf16[16,24,128]{2,1,0:T(8,128)(2,1)} %constant.13.clone.depth) | copy-start | bytes 294916
  46.5 30.8 %copy-start.9 = (bf16[20,20]{1,0:T(8,128)(2,1)S(1)}, bf16[20,20]{1,0:T(8,128)(2,1)}, u32[]{:S(2)}) copy-start(bf16[20,20]{1,0:T(8,128)(2,1)} %weight.5) | copy-start | bytes 2404
  46.5 30.8 %copy-start.10 = (f32[20]{0:T(128)S(1)}, f32[20]{0:T(128)}, u32[]{:S(2)}) copy-start(f32[20]{0:T(128)} %param.12) | copy-start | bytes 244
  113.4 30.8 %copy-start.7 = (bf16[16,24,128]{2,1,0:T(8,128)(2,1)S(1)}, bf16[16,24,128]{2,1,0:T(8,128)(2,1)}, u32[]{:S(2)}) copy-start(bf16[16,24,128]{2,1,0:T(8,128)(2,1)} %constant.14.clone.depth) | copy-start | bytes 294916
